TPU v7x, 32 devices: a whole 2x2x4 slice. The times are simulated.
32 devices in a mesh: chan: 2 (over x), row: 16 (over z, y, core).
Axes of the slice: x: 2, y: 2, z: 4, core: 2. Of those that a mesh axis runs over, the one named last changes fastest.
Arguments:
- inputs: bfloat16 [1, 192, 448, 1024], P(None, 'row', None, 'chan'), may hold values from -6 to 6
- cotangent: bfloat16 [1, 192, 448, 1024], P(None, 'row', None, 'chan'), may hold values from -6 to 6
- ln_gain: float32 [1024], P('chan'), may hold values from 0.1 to 1.9
- ln_shift: float32 [1024], P('chan'), may hold values from -3 to 3
- first_weight: bfloat16 [2, 1024, 128], P(None, 'chan'), may hold values from -0.375 to 0.375
- first_bias: float32 [2, 1024], P(None, 'chan'), may hold values from -3 to 3
- second_weight: bfloat16 [2, 1024, 128], P(None, 'chan'), may hold values from -0.375 to 0.375
- second_bias: float32 [2, 1024], P(None, 'chan'), may hold values from -3 to 3
Outputs:
- input_grad: bfloat16 [1, 192, 448, 1024], P(None, 'row', None, 'chan')
- first_weight_grad: float32 [2, 1024, 128], P(None, 'chan')
- first_bias_grad: float32 [2, 1024], P(None, 'chan')
- second_weight_grad: float32 [2, 1024, 128], P(None, 'chan')
- second_bias_grad: float32 [2, 1024], P(None, 'chan')
- gain_grad: float32 [1024], P('chan')
- shift_grad: float32 [1024], P('chan')
All inputs are finite; a program needn't handle non-finite values.
Results may differ from a plain program's by a relative error of at most 0.03.
The roundings to bfloat16 on the way count: a program that leaves them out, or rounds other values in their place, can miss the bound.
Values sent between devices are 32-bit elements; how exact they have to be, the bound alone decides.
No kernel may reach another device: no remote copies, remote signals or barrier semaphores. Data moves between devices by JAX's collectives and lax.ppermute only.
A program may use at most 128 MiB of HBM per device.

v0:
```python
import math

import jax
import jax.numpy as jnp
from jax import lax
from jax.sharding import PartitionSpec as P

H = 192
K = 192
BS = 128


EPS = 1e-05
LAMBDA = 0.01
HIGHER = lax.Precision.HIGH
ROOT_TWO_PI = math.sqrt(2.0 / math.pi)


def gelu_parts(values):
    inner = ROOT_TWO_PI * (values + 0.044715 * values * values * values)
    tangent = jnp.tanh(inner)
    output = 0.5 * values * (1.0 + tangent)
    slope = 0.5 * (1.0 + tangent) + 0.5 * values * (1.0 - tangent * tangent) * ROOT_TWO_PI * (
        1.0 + 3.0 * 0.044715 * values * values
    )
    return (output, slope)


def shrink_slope(values):
    tangent = jnp.tanh(values / LAMBDA)
    return tangent * tangent


def lon_table(width, kept):
    column = jnp.arange(width, dtype=jnp.int32)[:, None]
    number = jnp.arange(kept, dtype=jnp.int32)[None, :]
    phase = (column * number % width).astype(jnp.float32) * (2.0 * math.pi / width)
    factor = 1.0 / math.sqrt(width)
    return jnp.stack([jnp.cos(phase) * factor, -jnp.sin(phase) * factor], axis=1)


def lat_table(length, sign):
    first = jnp.arange(length, dtype=jnp.int32)[:, None]
    second = jnp.arange(length, dtype=jnp.int32)[None, :]
    phase = (first * second % length).astype(jnp.float32) * (2.0 * math.pi / length)
    factor = 1.0 / math.sqrt(length)
    cosine = jnp.cos(phase) * factor
    sine = jnp.sin(phase) * factor * -sign
    return jnp.stack([jnp.stack([cosine, sine], 1), jnp.stack([-sine, cosine], 1)], 0)


def mult(left, right):
    return jnp.einsum("bgkni,nio->bgkno", left, right, preferred_element_type=jnp.float32)


def mult_t(left, right):
    return jnp.einsum("bgkno,nio->bgkni", left, right, preferred_element_type=jnp.float32)


def outer(left, right):
    return jnp.einsum("bgkni,bgkno->nio", left, right, preferred_element_type=jnp.float32)


def on_device(
    inputs, cotangent, ln_gain, ln_shift, first_weight, first_bias, second_weight, second_bias
):
    batch, rows, width, local = inputs.shape
    blocks = local // BS
    total_chan = local * lax.axis_size("chan")
    values = inputs.astype(jnp.float32)
    mean = lax.psum(jnp.sum(values, -1), "chan") / total_chan
    centred = values - mean[..., None]
    variance = lax.psum(jnp.sum(centred * centred, -1), "chan") / total_chan
    rstd = lax.rsqrt(variance + EPS)[..., None]
    normed = centred * rstd
    mixed_in = normed * ln_gain + ln_shift
    longitude = lon_table(width, K)
    table_high = longitude.astype(jnp.bfloat16)
    table_low = (longitude - table_high.astype(jnp.float32)).astype(jnp.bfloat16)
    kept = jnp.where(jnp.arange(K) == 0, 1.0, 2.0).astype(jnp.float32)
    forward_lat = lat_table(H, -1)
    inverse_lat = lat_table(H, 1)

    def to_spectrum(piece):
        return jnp.einsum("qgph,bhpkc->bqgkc", forward_lat, piece, precision=HIGHER)

    input_lon = jnp.einsum("bhwc,wpk->bhpkc", mixed_in, longitude, precision=HIGHER)
    high = jnp.einsum("bhwc,wpk->bhpkc", cotangent, table_high, preferred_element_type=jnp.float32)
    low = jnp.einsum("bhwc,wpk->bhpkc", cotangent, table_low, preferred_element_type=jnp.float32)
    cot_lon = (high + low) * kept[None, None, None, :, None]
    spectrum = to_spectrum(
        lax.all_to_all(input_lon, "row", split_axis=3, concat_axis=1, tiled=True)
    )
    cot_spec = to_spectrum(lax.all_to_all(cot_lon, "row", split_axis=3, concat_axis=1, tiled=True))
    kept_local = spectrum.shape[3]
    block_shape = (batch, 2, H, kept_local, blocks, BS)
    w_one = first_weight.reshape(2, blocks, BS, BS)
    w_two = second_weight.reshape(2, blocks, BS, BS)
    b_one = first_bias.reshape(2, blocks, BS)
    b_two = second_bias.reshape(2, blocks, BS)
    spec_blocks = spectrum.reshape(block_shape).astype(jnp.bfloat16)
    spec_re = spec_blocks[:, 0]
    spec_im = spec_blocks[:, 1]
    pre_one_re = mult(spec_re, w_one[0]) - mult(spec_im, w_one[1]) + b_one[0]
    pre_one_im = mult(spec_re, w_one[1]) + mult(spec_im, w_one[0]) + b_one[1]
    act_re, slope_re = gelu_parts(pre_one_re)
    act_im, slope_im = gelu_parts(pre_one_im)
    hid_re = act_re.astype(jnp.bfloat16)
    hid_im = act_im.astype(jnp.bfloat16)
    pre_two_re = mult(hid_re, w_two[0]) - mult(hid_im, w_two[1]) + b_two[0]
    pre_two_im = mult(hid_re, w_two[1]) + mult(hid_im, w_two[0]) + b_two[1]
    cot_blocks = cot_spec.reshape(block_shape)
    grad_two_re = (cot_blocks[:, 0] * shrink_slope(pre_two_re)).astype(jnp.bfloat16)
    grad_two_im = (cot_blocks[:, 1] * shrink_slope(pre_two_im)).astype(jnp.bfloat16)
    grad_hid_re = mult_t(grad_two_re, w_two[0]) + mult_t(grad_two_im, w_two[1])
    grad_hid_im = mult_t(grad_two_im, w_two[0]) - mult_t(grad_two_re, w_two[1])
    dw_two = jnp.stack(
        [
            outer(hid_re, grad_two_re) + outer(hid_im, grad_two_im),
            outer(hid_re, grad_two_im) - outer(hid_im, grad_two_re),
        ]
    )
    db_two = jnp.stack(
        [
            jnp.sum(grad_two_re.astype(jnp.float32), (0, 1, 2)),
            jnp.sum(grad_two_im.astype(jnp.float32), (0, 1, 2)),
        ]
    )
    grad_pre_re = (grad_hid_re * slope_re).astype(jnp.bfloat16)
    grad_pre_im = (grad_hid_im * slope_im).astype(jnp.bfloat16)
    dw_one = jnp.stack(
        [
            outer(spec_re, grad_pre_re) + outer(spec_im, grad_pre_im),
            outer(spec_re, grad_pre_im) - outer(spec_im, grad_pre_re),
        ]
    )
    db_one = jnp.stack(
        [
            jnp.sum(grad_pre_re.astype(jnp.float32), (0, 1, 2)),
            jnp.sum(grad_pre_im.astype(jnp.float32), (0, 1, 2)),
        ]
    )
    grad_spec_re = mult_t(grad_pre_re, w_one[0]) + mult_t(grad_pre_im, w_one[1])
    grad_spec_im = mult_t(grad_pre_im, w_one[0]) - mult_t(grad_pre_re, w_one[1])
    grad_spec = jnp.stack([grad_spec_re, grad_spec_im], 1).reshape(batch, 2, H, kept_local, local)
    grad_lat = jnp.einsum("phqg,bqgkc->bhpkc", inverse_lat, grad_spec, precision=HIGHER)
    grad_mixed = jnp.einsum(
        "bhpkc,wpk->bhwc",
        lax.all_to_all(grad_lat, "row", split_axis=1, concat_axis=3, tiled=True),
        longitude,
        precision=HIGHER,
    )
    grad_norm = grad_mixed * ln_gain
    sum_one, sum_two = lax.psum((jnp.sum(grad_norm, -1), jnp.sum(grad_norm * normed, -1)), "chan")
    cot_values = cotangent.astype(jnp.float32)
    input_grad = cot_values + rstd * (
        grad_norm - sum_one[..., None] / total_chan - normed * (sum_two[..., None] / total_chan)
    )
    gain_local = jnp.sum(grad_mixed * normed, (0, 1, 2))
    shift_local = jnp.sum(grad_mixed, (0, 1, 2))
    dw_one, db_one, dw_two, db_two, gain_total, shift_total = lax.psum(
        (dw_one, db_one, dw_two, db_two, gain_local, shift_local), "row"
    )
    spec_scale = 1.0 / math.sqrt(batch * H * K)
    ln_scale = 1.0 / math.sqrt(batch * H * width)
    return (
        input_grad.astype(jnp.bfloat16),
        (dw_one * spec_scale).reshape(2, local, BS),
        (db_one * spec_scale).reshape(2, local),
        (dw_two * spec_scale).reshape(2, local, BS),
        (db_two * spec_scale).reshape(2, local),
        gain_total * ln_scale,
        shift_total * ln_scale,
    )


def solution(mesh):
    placed = (
        P(None, "row", None, "chan"),
        P(None, "row", None, "chan"),
        P("chan"),
        P("chan"),
        P(None, "chan", None),
        P(None, "chan"),
        P(None, "chan", None),
        P(None, "chan"),
    )
    return jax.shard_map(
        on_device,
        mesh=mesh,
        in_specs=placed,
        out_specs=(
            P(None, "row", None, "chan"),
            P(None, "chan", None),
            P(None, "chan"),
            P(None, "chan", None),
            P(None, "chan"),
            P("chan"),
            P("chan"),
        ),
        check_vma=False,
    )
```

profile of v0, /device:TPU:0, one launch (start us, length us, event | category | flops | bytes accessed | tf_op | source)
XLA Modules:
  0.0 934.7 jit_solution(10081038176205882450)
XLA Ops:
  8.9 4.9 fusion.28
  16.5 15.0 %copy.58 = f32[1,12,2,192,512]{4,2,1,0,3:T(2,128)} copy(f32[1,12,2,192,512]{4,3,1,2,0:T(8,128)S(1)} %fusion.25) | data formatting | bytes 18874368 | tf_op jit(solution)/shard_map/mul | solution.py:90
  31.5 7.4 all-to-all-start
  42.5 8.3 psum.70
  50.9 4.6 fusion.16
  55.5 7.6 psum.71
  63.1 10.5 %fusion.68 = f32[1,12,2,192,512]{4,3,1,2,0:T(8,128)S(1)} fusion(bf16[1,12,448,512]{3,2,1,0:T(8,128)(2,1)} %param.8, f32[512]{0:T(512)S(1)} %copy-done.29, f32[512]{0:T(512)S(1)} %copy-done.27, f32[12,448]{1,0:T(8,128)S(1)} %rsqrt_bitcast_fusion, f32[12,448]{1,0:T(8,128)S(1)} %multiply_bitcast_fusion.2, f32[448,1,192]{0,2,1:T(8,128)S(1)} %get-tuple-element.47, ...), kind=kOutput, calls=%fused_computation.90 | convolution fusion | flops 6355722240 | bytes 15677440 | tf_op jit(solution)/shard_map/bhwc,wpk->bhpkc/dot_general | solution.py:87
  73.7 15.1 %copy.63 = f32[1,12,2,192,512]{4,2,1,0,3:T(2,128)} copy(f32[1,12,2,192,512]{4,3,1,2,0:T(8,128)S(1)} %fusion.68) | data formatting | bytes 18874368 | tf_op jit(solution)/shard_map/bhwc,wpk->bhpkc/transpose | solution.py:87
  88.8 119.2 %all-to-all-done = f32[1,12,2,192,512]{4,2,1,0,3:T(2,128)} async-done(((f32[1,12,2,192,512]{4,2,1,0,3:T(2,128)}), f32[1,12,2,192,512]{4,2,1,0,3:T(2,128)}, u32[]{:S(2)}, u32[]{:S(2)}) %all-to-all-start) | async-done | bytes 9437216 | tf_op jit(solution)/shard_map/all_to_all | solution.py:94
  208.0 40.8 %all-to-all-start.1 = ((f32[1,12,2,192,512]{4,2,1,0,3:T(2,128)}), f32[1,12,2,192,512]{4,2,1,0,3:T(2,128)}, u32[]{:S(2)}, u32[]{:S(2)}) async-start(f32[1,12,2,192,512]{4,2,1,0,3:T(2,128)} %copy.63), calls=%async_computation.1 | async-start | bytes 18874368 | tf_op jit(solution)/shard_map/all_to_all | solution.py:92
  252.1 5.9 copy.59
  260.3 14.3 %fusion.65 = f32[1,2,192,12,512]{4,2,1,3,0:T(8,128)} fusion(f32[192,2,12,512,1]{3,1,2,0,4:T(2,128)S(1)} %bitcast.485, f32[1,192,2,192]{3,1,2,0:T(8,128)S(1)} %get-tuple-element.28, f32[1,192,2,192]{3,1,2,0:T(8,128)S(1)} %get-tuple-element.29), kind=kOutput, calls=%fused_computation.89 | convolution fusion | flops 5435965440 | bytes 19464192 | tf_op jit(solution)/shard_map/qgph,bhpkc->bqgkc/dot_general | solution.py:85
  274.6 11.8 %reshape.382 = f32[1,2,192,12,4,128]{5,4,2,1,3,0:T(4,128)} reshape(f32[1,2,192,12,512]{4,2,1,3,0:T(8,128)} %fusion.65) | data formatting | bytes 18874368 | tf_op jit(solution)/shard_map/reshape | solution.py:112
  286.5 8.3 fusion.234
  294.8 122.9 %all-to-all-done.1 = f32[1,12,2,192,512]{4,2,1,0,3:T(2,128)} async-done(((f32[1,12,2,192,512]{4,2,1,0,3:T(2,128)}), f32[1,12,2,192,512]{4,2,1,0,3:T(2,128)}, u32[]{:S(2)}, u32[]{:S(2)}) %all-to-all-start.1) | async-done | bytes 9437216 | tf_op jit(solution)/shard_map/all_to_all | solution.py:92
  417.7 5.9 copy.64
  425.9 12.9 %fusion.50 = bf16[1,2,192,12,512]{4,2,1,3,0:T(8,128)(2,1)} fusion(f32[192,2,12,512,1]{3,1,2,0,4:T(2,128)S(1)} %bitcast.490, f32[1,192,2,192]{3,1,2,0:T(8,128)S(1)} %get-tuple-element.28, f32[1,192,2,192]{3,1,2,0:T(8,128)S(1)} %get-tuple-element.29), kind=kOutput, calls=%fused_computation.60 | convolution fusion | flops 5438324736 | bytes 14745600 | tf_op jit(solution)/shard_map/qgph,bhpkc->bqgkc/dot_general | solution.py:85
  438.8 7.7 convert_element_type.135
  446.5 4.0 fusion.235
  457.3 3.9 multiply_convert_fusion.1
  466.7 3.8 convert_reduce_fusion.3
  473.7 3.9 convert_reduce_fusion.4
  488.5 10.3 %fusion.71 = f32[1,192,2,12,512]{4,1,2,3,0:T(8,128)S(1)} fusion(f32[1,1,192,12,512]{4,2,1,3,0:T(8,128)S(1)} %copy.73, f32[1,1,192,12,512]{4,2,1,3,0:T(8,128)S(1)} %copy.72, f32[1,192,2,192]{3,1,2,0:T(8,128)S(1)} %copy-done.18, f32[1,192,2,192]{3,1,2,0:T(8,128)S(1)} %get-tuple-element.26), kind=kOutput, calls=%fused_computation.91 | convolution fusion | flops 5438324736 | bytes 19464192 | tf_op jit(solution)/shard_map/phqg,bqgkc->bhpkc/dot_general | solution.py:146
  498.8 15.0 %copy.74 = f32[1,192,2,12,512]{4,2,3,0,1:T(2,128)} copy(f32[1,192,2,12,512]{4,1,2,3,0:T(8,128)S(1)} %fusion.71) | data formatting | bytes 18874368 | tf_op jit(solution)/shard_map/phqg,bqgkc->bhpkc/transpose | solution.py:146
  513.8 40.7 %all-to-all-start.2 = ((f32[1,192,2,12,512]{4,2,3,0,1:T(2,128)}), f32[1,192,2,12,512]{4,2,3,0,1:T(2,128)}, u32[]{:S(2)}, u32[]{:S(2)}) async-start(f32[1,192,2,12,512]{4,2,3,0,1:T(2,128)} %copy.74), calls=%async_computation.2 | async-start | bytes 18874368 | tf_op jit(solution)/shard_map/all_to_all | solution.py:149
  566.5 250.7 %all-reduce.5.cloned.1.call-done = (f32[2,4,128,128]{3,2,1,0:T(8,128)}, f32[2,4,128,128]{3,2,1,0:T(8,128)}) async-done(((f32[2,4,128,128]{3,2,1,0:T(8,128)}, f32[2,4,128,128]{3,2,1,0:T(8,128)}), (f32[2,4,128,128]{3,2,1,0:T(8,128)}, f32[2,4,128,128]{3,2,1,0:T(8,128)})) %all-reduce.5.cloned.1.call-update) | async-done | bytes 1048592 | tf_op jit(solution)/shard_map/psum | solution.py:161
  821.1 6.8 copy.75
  827.9 14.5 %fusion.15 = (f32[512]{0:T(512)S(1)}, f32[12,448]{1,0:T(8,128)S(1)}, f32[12,448]{1,0:T(8,128)S(1)}, f32[448,12,512,1]{2,0,3,1:T(8,128)}) fusion(bf16[1,12,448,512]{3,2,1,0:T(8,128)(2,1)S(1)} %bitcast.487, f32[12,448]{1,0:T(8,128)S(1)} %copy-done.24, f32[12,448]{1,0:T(8,128)S(1)} %copy-done.20, f32[512]{0:T(512)S(1)} %copy-done.28, ...), kind=kOutput, calls=%fused_computation.16 | convolution fusion | flops 6366721024 | bytes 26730496 | tf_op jit(solution)/shard_map/bhpkc,wpk->bhwc/dot_general | solution.py:147
  842.4 9.0 all-reduce.2
  851.4 4.9 bitcast_reduce_fusion
  856.3 57.6 %all-reduce = (f32[2,4,128]{2,1,0:T(4,128)S(1)}, f32[2,4,128]{2,1,0:T(4,128)S(1)}, f32[512]{0:T(512)S(1)}, f32[512]{0:T(512)S(1)}) all-reduce(f32[2,4,128]{2,1,0:T(4,128)S(1)} %pad_maximum_fusion.10, f32[2,4,128]{2,1,0:T(4,128)S(1)} %pad_maximum_fusion.11, f32[512]{0:T(512)S(1)} %get-tuple-element.7, ...), channel_id=1, replica_groups=mesh['chan'=2,'row'=16] {'row'}, use_global_device_ids=true, to_apply=%region_11.12 | all-reduce | flops 3072 | bytes 24576 | tf_op jit(solution)/shard_map/psum | solution.py:161
  916.3 11.4 %fusion.14 = bf16[1,12,448,512]{3,2,1,0:T(8,128)(2,1)} fusion(bf16[1,12,448,512]{3,2,1,0:T(8,128)(2,1)} %param.8, bf16[1,12,448,512]{3,2,1,0:T(8,128)(2,1)} %param.9, f32[448,12,512,1]{2,0,3,1:T(8,128)} %get-tuple-element.38, f32[12,448]{1,0:T(8,128)S(1)} %multiply_bitcast_fusion, f32[12,448]{1,0:T(8,128)S(1)} %multiply_bitcast_fusion.1, ...), kind=kLoop, calls=%fused_computation.15 | loop fusion | flops 30277632 | bytes 27613184 | tf_op jit(solution)/shard_map/convert_element_type | solution.py:167
  (143 shorter events, 59.9 us)
Async XLA Ops:
  7.2 6.6 slice-start.2
  8.9 54.2 %copy-start.14 = (f32[448,1,192]{0,2,1:T(8,128)}, f32[448,1,192]{0,2,1:T(8,128)S(1)}, u32[]{:S(2)}) copy-start(f32[448,1,192]{0,2,1:T(8,128)S(1)} %get-tuple-element.47) | copy-start | bytes 1032196
  8.9 54.2 %copy-start.16 = (f32[448,1,192]{0,2,1:T(8,128)}, f32[448,1,192]{0,2,1:T(8,128)S(1)}, u32[]{:S(2)}) copy-start(f32[448,1,192]{0,2,1:T(8,128)S(1)} %get-tuple-element.48) | copy-start | bytes 1032196
  8.9 4.9 slice-start.3
  31.5 176.4 %all-to-all-start = ((f32[1,12,2,192,512]{4,2,1,0,3:T(2,128)}), f32[1,12,2,192,512]{4,2,1,0,3:T(2,128)}, u32[]{:S(2)}, u32[]{:S(2)}) async-start(f32[1,12,2,192,512]{4,2,1,0,3:T(2,128)} %copy.58), calls=%async_computation | async-start | bytes 18874368 | tf_op jit(solution)/shard_map/all_to_all | solution.py:94
  39.0 24.1 %copy-start.27 = (f32[512]{0:T(512)S(1)}, f32[512]{0:T(512)}, u32[]{:S(2)}) copy-start(f32[512]{0:T(512)} %param.10) | copy-start | bytes 6148
  39.0 24.1 %copy-start.29 = (f32[512]{0:T(512)S(1)}, f32[512]{0:T(512)}, u32[]{:S(2)}) copy-start(f32[512]{0:T(512)} %param.11) | copy-start | bytes 6148
  50.9 22.8 %copy-start.19 = (f32[12,448]{1,0:T(8,128)}, f32[12,448]{1,0:T(8,128)S(1)}, u32[]{:S(2)}) copy-start(f32[12,448]{1,0:T(8,128)S(1)} %multiply_bitcast_fusion.2) | copy-start | bytes 64516
  63.1 10.5 %copy-start.23 = (f32[12,448]{1,0:T(8,128)}, f32[12,448]{1,0:T(8,128)S(1)}, u32[]{:S(2)}) copy-start(f32[12,448]{1,0:T(8,128)S(1)} %rsqrt_bitcast_fusion) | copy-start | bytes 64516
  88.7 163.2 %copy-start.25 = (f32[2,512]{1,0:T(2,128)S(1)}, f32[2,512]{1,0:T(2,128)}, u32[]{:S(2)}) copy-start(f32[2,512]{1,0:T(2,128)} %param.13) | copy-start | bytes 12292
  88.7 163.2 %copy-start.26 = (f32[2,512]{1,0:T(2,128)S(1)}, f32[2,512]{1,0:T(2,128)}, u32[]{:S(2)}) copy-start(f32[2,512]{1,0:T(2,128)} %param.15) | copy-start | bytes 12292
  88.7 163.3 %copy-start.21 = (bf16[2,512,128]{2,1,0:T(8,128)(2,1)S(1)}, bf16[2,512,128]{2,1,0:T(8,128)(2,1)}, u32[]{:S(2)}) copy-start(bf16[2,512,128]{2,1,0:T(8,128)(2,1)} %param.12) | copy-start | bytes 786436
  88.7 163.3 %copy-start.22 = (bf16[2,512,128]{2,1,0:T(8,128)(2,1)S(1)}, bf16[2,512,128]{2,1,0:T(8,128)(2,1)}, u32[]{:S(2)}) copy-start(bf16[2,512,128]{2,1,0:T(8,128)(2,1)} %param.14) | copy-start | bytes 786436
  208.0 209.7 %all-to-all-start.1 = ((f32[1,12,2,192,512]{4,2,1,0,3:T(2,128)}), f32[1,12,2,192,512]{4,2,1,0,3:T(2,128)}, u32[]{:S(2)}, u32[]{:S(2)}) async-start(f32[1,12,2,192,512]{4,2,1,0,3:T(2,128)} %copy.63), calls=%async_computation.1 | async-start | bytes 18874368 | tf_op jit(solution)/shard_map/all_to_all | solution.py:92
  450.5 6.7 copy-start.12
  456.5 4.7 slice-start.6
  457.3 4.0 slice-start.7
  461.2 3.1 copy-start.6
  466.7 5.9 copy-start.10
  470.5 3.0 slice-start.8
  477.7 5.4 copy-start.8
  513.8 307.3 %all-to-all-start.2 = ((f32[1,192,2,12,512]{4,2,3,0,1:T(2,128)}), f32[1,192,2,12,512]{4,2,3,0,1:T(2,128)}, u32[]{:S(2)}, u32[]{:S(2)}) async-start(f32[1,192,2,12,512]{4,2,3,0,1:T(2,128)} %copy.74), calls=%async_computation.2 | async-start | bytes 18874368 | tf_op jit(solution)/shard_map/all_to_all | solution.py:149
  554.5 262.7 %all-reduce.5.cloned.1.call-start = ((), (), s32[]{:S(2)}) async-start(), calls=%async_computation.3 | async-start | bytes 2097152 | tf_op jit(solution)/shard_map/psum | solution.py:161
  554.8 3.4 copy-start.3
  554.8 3.8 copy-start.11
  564.8 263.1 %slice-start = ((s8[5505024]{0:T(1024)(128)(4,1)}), s8[1310720]{0:T(1024)(128)(4,1)S(1)}, s32[]{:S(2)}) async-start(s8[5505024]{0:T(1024)(128)(4,1)} %bitcast.486), calls=%async_computation.4 | async-start | bytes 2621440
  821.0 6.8 slice-start.1
  821.0 6.8 copy-start.15
  821.0 6.8 copy-start.17
  821.0 6.8 copy-start.20
  821.1 6.8 copy-start.24
  821.1 6.8 copy-start.28
  (12 other events, 23.1 us)
Sparse Core Ops, SparseCore 0:
  566.6 250.5 all-reduce.4
where the time goes:
time: 943 us; the launch traced here: 935 us
  waiting for transfers between devices  493 us (52%)
  local copies, waits for them, and re-layouts  115 us (12%)
  matrix products  104 us (11%)
  starting transfers between devices  89.1 us (9%)
  blocking collectives  82.5 us (9%)
  other arithmetic  35.9 us (4%)
  between operations  15.1 us (2%)
    psum x1, waiting for transfers between devices, on_device(): lax.psum((dw_one, db_one, dw_two, db_two, gain_local, shift_local), 'row')  251 us
    all_to_all x1, waiting for transfers between devices, on_device(): lax.all_to_all(input_lon, 'row', split_axis=3, concat_axis=1, tiled=True)  123 us
    all_to_all x1, waiting for transfers between devices, on_device(): lax.all_to_all(cot_lon, 'row', split_axis=3, concat_axis=1, tiled=True)  119 us
    psum x1, blocking collectives, on_device(): lax.psum((dw_one, db_one, dw_two, db_two, gain_local, shift_local), 'row')  57.6 us
    all_to_all x1, starting transfers between devices, on_device(): lax.all_to_all(input_lon, 'row', split_axis=3, concat_axis=1, tiled=True)  40.8 us
    all_to_all x1, starting transfers between devices, on_device(): lax.all_to_all(grad_lat, 'row', split_axis=1, concat_axis=3, tiled=True)  40.7 us
    dot_general x2, matrix products, to_spectrum(): return jnp.einsum('qgph,bhpkc->bqgkc', forward_lat, piece, precision=HIGHER)  27.2 us
  transfers between devices with their start and end apart: 4, of which 3 were waited for; matrix products, arithmetic and copies ran while one was open for 10% of the time, Pallas kernels for 0%

commit v1 on v0

v1 whole, which is shorter than its diff:
```python
import functools
import math

import jax
import jax.numpy as jnp
import numpy as np
from jax import lax
from jax.experimental import pallas as pl
from jax.experimental.pallas import tpu as pltpu
from jax.sharding import PartitionSpec as P

K = 192
BS = 128
EPS = 1e-05
LAMBDA = 0.01
ROOT_TWO_PI = math.sqrt(2.0 / math.pi)
BF16 = jnp.bfloat16
F32 = jnp.float32
VMEM_LIMIT = 48 * 1024 * 1024


def gelu_parts(values):
    inner = ROOT_TWO_PI * (values + 0.044715 * values * values * values)
    tangent = jnp.tanh(inner)
    output = 0.5 * values * (1.0 + tangent)
    slope = 0.5 * (1.0 + tangent) + 0.5 * values * (1.0 - tangent * tangent) * ROOT_TWO_PI * (
        1.0 + 3.0 * 0.044715 * values * values
    )
    return (output, slope)


def shrink_slope(values):
    tangent = jnp.tanh(values / LAMBDA)
    return tangent * tangent


def high_low(table):
    high = np.asarray(table, np.float32).astype(jnp.bfloat16)
    low = (np.asarray(table, np.float32) - high.astype(np.float32)).astype(jnp.bfloat16)
    return high, low


def lon_table(width, owners, padded):
    own = K // owners
    number = np.arange(K)[:, None]
    column = np.arange(width)[None, :]
    phase = (number * column % width) * (2.0 * math.pi / width)
    parts = np.stack([np.cos(phase), -np.sin(phase)]) / math.sqrt(width)
    parts = parts.reshape(2, owners, own, width).transpose(1, 0, 2, 3)
    table = np.zeros((owners, padded, width))
    table[:, : 2 * own] = parts.reshape(owners, 2 * own, width)
    return table.reshape(owners * padded, width)


def kept_scale(owners, padded):
    own = K // owners
    scale = np.full((2, K), 2.0)
    scale[:, 0] = 1.0
    out = np.ones((owners, padded))
    out[:, : 2 * own] = scale.reshape(2, owners, own).transpose(1, 0, 2).reshape(owners, 2 * own)
    return out.reshape(owners * padded, 1)


def lat_table(length):
    first = np.arange(length)
    phase = (first[:, None] * first[None, :] % length) * (2.0 * math.pi / length)
    cosine = np.cos(phase) / math.sqrt(length)
    sine = np.sin(phase) / math.sqrt(length)
    return np.block([[cosine, sine], [-sine, cosine]])


def dot(left, right):
    return jnp.dot(left, right, preferred_element_type=F32)


def dot_rows(left, right):
    return lax.dot_general(left, right, (((0,), (0,)), ((), ())), preferred_element_type=F32)


def dot_cols(left, right):
    return lax.dot_general(left, right, (((1,), (1,)), ((), ())), preferred_element_type=F32)


def split(values):
    high = values.astype(BF16)
    return high, (values - high.astype(F32)).astype(BF16)


def columns_of(stats):
    count = stats.shape[0]
    high, rest = split(stats)
    mid, low = split(stats - high.astype(F32))
    stacked = jnp.concatenate([high.astype(F32), mid.astype(F32), low.astype(F32)], 0)
    pad = -stacked.shape[0] % 16
    if pad:
        stacked = jnp.concatenate([stacked, jnp.zeros((pad, stacked.shape[1]), F32)], 0)
    rows = stacked.shape[0]
    row = lax.broadcasted_iota(jnp.int32, (rows, count * 128), 0)
    lane = lax.broadcasted_iota(jnp.int32, (rows, count * 128), 1)
    pick = (row % count == lane // 128) & (row < 3 * count)
    wide = dot_rows(stacked.astype(BF16), pick.astype(F32).astype(BF16))
    return [wide[:, i * 128 : (i + 1) * 128] for i in range(count)]


def cot_lon_kernel(high_ref, low_ref, cot_ref, out_ref):
    owners, blocks, _, padded, _ = out_ref.shape
    values = cot_ref[0, 0]
    result = dot(high_ref[...], values) + dot(low_ref[...], values)
    for b in range(blocks):
        out_ref[:, b, 0] = result[:, b * BS : (b + 1) * BS].reshape(owners, padded, BS)


def input_lon_kernel(high_ref, low_ref, in_ref, stat_ref, gain_ref, *out_refs):
    mean, rstd = columns_of(stat_ref[0])
    at = 0
    for out_ref in out_refs:
        owners, blocks, _, padded, _ = out_ref.shape
        pieces = []
        for b in range(at, at + blocks):
            lanes = slice(b * BS, (b + 1) * BS)
            values = in_ref[0, 0, :, lanes].astype(F32)
            pieces.append((values - mean) * rstd * gain_ref[:, lanes])
        at += blocks
        high, low = split(jnp.concatenate(pieces, 1))
        result = dot(high_ref[...], high) + dot(high_ref[...], low) + dot(low_ref[...], high)
        for b in range(blocks):
            out_ref[:, b, 0] = result[:, b * BS : (b + 1) * BS].reshape(owners, padded, BS)


def mixer_kernel(
    own,
    group,
    fwd_high_ref,
    fwd_low_ref,
    inv_high_ref,
    inv_low_ref,
    w_one_ref,
    w_one_t_ref,
    w_two_ref,
    w_two_t_ref,
    bias_ref,
    shift_ref,
    x_ref,
    c_ref,
    grad_ref,
    sums_ref,
    x_scr,
    c_scr,
    high_scr,
    low_scr,
    spec_scr,
    hid_scr,
    two_scr,
    pre_scr,
    gain_scr,
):
    sources, _, span, _ = x_ref.shape
    length = fwd_high_ref.shape[0] // 2
    padded = sources * span // length
    steps = own // group
    for s in range(sources):
        x_scr[s * span : (s + 1) * span] = x_ref[s, 0]
        c_scr[s * span : (s + 1) * span] = c_ref[s, 0]
    for k in range(own):
        step, place = divmod(k, group)
        for which, scr in enumerate((x_scr, c_scr)):
            lanes = slice((which * group + place) * BS, (which * group + place + 1) * BS)
            for part in range(2):
                values = scr[pl.ds(part * own + k, length, stride=padded), :]
                rows = slice(part * length, (part + 1) * length)
                high, low = split(values)
                high_scr[step, rows, lanes] = high
                low_scr[step, rows, lanes] = low
    gain_scr[...] = jnp.zeros_like(gain_scr)
    w_one = w_one_ref[0]
    w_two = w_two_ref[0]
    first = lax.broadcasted_iota(jnp.int32, (group * length, 1), 0) == 0

    def gather(full, which):
        rows = []
        for place in range(group):
            at = (which * group + place) * BS
            re = full[:length, at : at + BS]
            im = full[length:, at : at + BS]
            rows.append(jnp.concatenate([re, im], 1))
        return jnp.concatenate(rows, 0)

    def body(step, carry):
        high = high_scr[step]
        low = low_scr[step]
        full = dot(fwd_high_ref[...], high) + dot(fwd_high_ref[...], low)
        full = full + dot(fwd_low_ref[...], high)
        plain = gather(full, 0)
        cot = gather(full, 1)
        at = pl.ds(pl.multiple_of(step * (group * length), group * length), group * length)
        is_first = jnp.where(first & (step == 0), 1.0, 0.0)
        spec = (plain + is_first * shift_ref[0, 0:1]).astype(BF16)
        pre_one = dot(spec, w_one) + bias_ref[0, 0:1]
        act, slope = gelu_parts(pre_one)
        hid = act.astype(BF16)
        pre_two = dot(hid, w_two) + bias_ref[0, 1:2]
        grad_two = (cot * shrink_slope(pre_two)).astype(BF16)
        grad_pre = (dot(grad_two, w_two_t_ref[0]) * slope).astype(BF16)
        grad_spec = dot(grad_pre, w_one_t_ref[0])
        spec_scr[at] = spec
        hid_scr[at] = hid
        two_scr[at] = grad_two
        pre_scr[at] = grad_pre
        gain_scr[0:1] += jnp.sum(grad_spec * plain, 0, keepdims=True)
        gain_scr[1:2] += jnp.sum(grad_two.astype(F32), 0, keepdims=True)
        gain_scr[2:3] += jnp.sum(grad_pre.astype(F32), 0, keepdims=True)
        gain_scr[3:4] += jnp.sum(grad_spec * is_first, 0, keepdims=True)
        for place in range(group):
            piece = grad_spec[place * length : (place + 1) * length]
            stacked = jnp.concatenate([piece[:, :BS], piece[:, BS:]], 0)
            grad_high, grad_low = split(stacked)
            high_scr[step, :, place * BS : (place + 1) * BS] = grad_high
            low_scr[step, :, place * BS : (place + 1) * BS] = grad_low
        return carry

    lax.fori_loop(0, steps, body, 0)
    for step in range(steps):
        high = high_scr[step, :, : group * BS]
        low = low_scr[step, :, : group * BS]
        lon = dot(inv_high_ref[...], high) + dot(inv_high_ref[...], low)
        lon = lon + dot(inv_low_ref[...], high)
        for place in range(group):
            k = step * group + place
            for part in range(2):
                piece = lon[part * length : (part + 1) * length, place * BS : (place + 1) * BS]
                x_scr[pl.ds(part * own + k, length, stride=padded), :] = piece
    for k in range(2 * own, padded):
        x_scr[pl.ds(k, length, stride=padded), :] = jnp.zeros((length, BS), F32)
    for s in range(sources):
        grad_ref[s, 0] = x_scr[s * span : (s + 1) * span]
    for i, (left, right) in enumerate(((spec_scr, pre_scr), (hid_scr, two_scr))):
        square = dot_rows(left[...], right[...])
        sums_ref[0, 2 * i * BS : (2 * i + 1) * BS] = square[:BS, :BS] + square[BS:, BS:]
        sums_ref[0, (2 * i + 1) * BS : (2 * i + 2) * BS] = square[:BS, BS:] - square[BS:, :BS]
    total = gain_scr[...]
    sums_ref[0, 4 * BS : 4 * BS + 8] = jnp.concatenate(
        [
            total[2:3, :BS],
            total[2:3, BS:],
            total[1:2, :BS],
            total[1:2, BS:],
            total[0:1, :BS] + total[0:1, BS:],
            total[3:4, :BS] * shift_ref[0, 1:2, :BS],
            jnp.zeros((2, BS), F32),
        ],
        0,
    )


def lon_back_kernel(offset, carry_in, table_ref, grad_ref, in_ref, stat_ref, gain_ref, *refs):
    if carry_in:
        before_ref, out_ref, sums_ref = refs
    else:
        out_ref, sums_ref = refs
    sources, blocks, _, padded, _ = grad_ref.shape
    mean, rstd = columns_of(stat_ref[0])
    pieces = [grad_ref[:, b, 0].reshape(sources * padded, BS).astype(BF16) for b in range(blocks)]
    mixed = dot(table_ref[...], jnp.concatenate(pieces, 1))
    ones = jnp.ones((16, BS), BF16)
    grads = jnp.zeros((in_ref.shape[2], BS), F32)
    products = jnp.zeros((in_ref.shape[2], BS), F32)
    for b in range(blocks):
        lanes = slice((offset + b) * BS, (offset + b + 1) * BS)
        grad = mixed[:, b * BS : (b + 1) * BS] * gain_ref[:, lanes]
        values = in_ref[0, 0, :, b * BS : (b + 1) * BS].astype(F32)
        out_ref[0, :, b * BS : (b + 1) * BS] = grad
        grads = grads + grad
        products = products + grad * ((values - mean) * rstd)
    rows = []
    for values in (grads, products):
        high, low = split(values)
        rows.append((dot_cols(ones, high) + dot_cols(ones, low))[0:1])
    sums = jnp.concatenate(rows, 0)
    if carry_in:
        sums = sums + before_ref[0]
    sums_ref[0] = sums


def finish_kernel(chunks, channels, *refs):
    in_ref, cot_ref, stat_ref, sums_ref = refs[:4]
    grad_refs = refs[4 : 4 + len(chunks)]
    out_ref = refs[-1]
    stats = jnp.concatenate([stat_ref[0], sums_ref[0] / channels], 0)
    mean, rstd, one, two = columns_of(stats)
    at = 0
    for grad_ref, blocks in zip(grad_refs, chunks):
        for b in range(blocks):
            lanes = slice(at * BS, (at + 1) * BS)
            normed = (in_ref[0, 0, :, lanes].astype(F32) - mean) * rstd
            grad = grad_ref[0, :, b * BS : (b + 1) * BS]
            cot = cot_ref[0, 0, :, lanes].astype(F32)
            out_ref[0, 0, :, lanes] = (cot + rstd * (grad - one - normed * two)).astype(BF16)
            at += 1


def params():
    return pltpu.CompilerParams(vmem_limit_bytes=VMEM_LIMIT)


def whole(shape):
    return pl.BlockSpec(shape, lambda *_: (0,) * len(shape))


def cost(flops, moved, transcendentals=0):
    return pl.CostEstimate(
        flops=int(flops), bytes_accessed=int(moved), transcendentals=int(transcendentals)
    )


def on_device(
    inputs, cotangent, ln_gain, ln_shift, first_weight, first_bias, second_weight, second_bias
):
    batch, rows, width, local = inputs.shape
    blocks = local // BS
    owners = lax.axis_size("row")
    height = rows * owners
    own = K // owners
    padded = -(-2 * own // 8) * 8
    tall = owners * padded
    group = 2 if own % 2 == 0 else 1
    total_chan = local * lax.axis_size("chan")
    chunks = (blocks - 1, 1) if blocks > 1 else (1,)
    starts = [sum(chunks[:i]) for i in range(len(chunks))]
    gain = ln_gain.reshape(1, local)

    lon = lon_table(width, owners, padded)
    lon_high, lon_low = high_low(lon)
    cot_high, cot_low = high_low(lon * kept_scale(owners, padded))
    back = np.ascontiguousarray(lon.T).astype(np.float32).astype(jnp.bfloat16)
    fwd_high, fwd_low = high_low(lat_table(height))
    inv_high, inv_low = high_low(lat_table(height).T)

    def exchange(piece):
        return lax.all_to_all(piece, "row", split_axis=0, concat_axis=0, tiled=True)

    row_spec = pl.BlockSpec((1, 1, width, local), lambda h: (0, h, 0, 0))
    stat_spec = pl.BlockSpec((1, 2, width), lambda h: (h, 0, 0))

    def spectrum_spec(count):
        return pl.BlockSpec((owners, count, 1, padded, BS), lambda h: (0, 0, h, 0, 0))

    def spectrum_shape(count):
        return jax.ShapeDtypeStruct((owners, count, rows, padded, BS), F32)

    lon_flops = 2 * rows * tall * width * local
    cot_lon = pl.pallas_call(
        cot_lon_kernel,
        grid=(rows,),
        in_specs=[whole((tall, width)), whole((tall, width)), row_spec],
        out_specs=spectrum_spec(blocks),
        out_shape=spectrum_shape(blocks),
        compiler_params=params(),
        cost_estimate=cost(2 * lon_flops, rows * local * (2 * width + 4 * tall)),
        name="cot_lon",
    )(cot_high, cot_low, cotangent)
    cot_lon, inputs = lax.optimization_barrier((cot_lon, inputs))
    cot_spec = exchange(cot_lon)

    values = inputs.astype(F32)
    mean = lax.psum(jnp.sum(values, -1), "chan") / total_chan
    centred = values - mean[..., None]
    variance = lax.psum(jnp.sum(centred * centred, -1), "chan") / total_chan
    stats = jnp.stack([mean[0], lax.rsqrt(variance + EPS)[0]], 1)

    input_lon = pl.pallas_call(
        input_lon_kernel,
        grid=(rows,),
        in_specs=[
            whole((tall, width)),
            whole((tall, width)),
            row_spec,
            stat_spec,
            whole((1, local)),
        ],
        out_specs=[spectrum_spec(count) for count in chunks],
        out_shape=[spectrum_shape(count) for count in chunks],
        compiler_params=params(),
        cost_estimate=cost(3 * lon_flops, rows * local * (2 * width + 4 * tall)),
        name="input_lon",
    )(lon_high, lon_low, inputs, stats, gain)

    def square(weight):
        re, im = weight.reshape(2, blocks, BS, BS)
        return jnp.concatenate(
            [jnp.concatenate([re, im], 2), jnp.concatenate([-im, re], 2)], 1
        )

    w_one = square(first_weight)
    w_two = square(second_weight)
    w_one_t = w_one.swapaxes(1, 2)
    w_two_t = w_two.swapaxes(1, 2)
    bias = jnp.stack([first_bias, second_bias]).reshape(2, 2, blocks, BS)
    bias = bias.transpose(2, 0, 1, 3).reshape(blocks, 2, 2 * BS)
    is_origin = (lax.axis_index("row") == 0).astype(F32)
    shift = (ln_shift * (math.sqrt(height * width) * is_origin)).reshape(blocks, 1, BS)
    shift = jnp.concatenate([shift, jnp.zeros_like(shift)], 2)
    shift = jnp.concatenate([shift, jnp.full_like(shift, is_origin)], 1)

    span = rows * padded
    mat = pl.BlockSpec((1, 2 * BS, 2 * BS), lambda b: (b, 0, 0))

    def mix(index, x_spec):
        count = chunks[index]
        start = starts[index]

        def at(shape):
            return pl.BlockSpec(shape, lambda b: (b + start,) + (0,) * (len(shape) - 1))

        tokens = own * height
        flops = 2 * count * tokens * 2 * BS * (3 * 2 * height * 3 + 6 * 2 * BS)
        return pl.pallas_call(
            functools.partial(mixer_kernel, own, group),
            grid=(count,),
            in_specs=[whole((2 * height, 2 * height))] * 4
            + [at((1, 2 * BS, 2 * BS))] * 4
            + [
                at((1, 2, 2 * BS)),
                at((1, 2, 2 * BS)),
                pl.BlockSpec((owners, 1, span, BS), lambda b: (0, b, 0, 0)),
                pl.BlockSpec((owners, 1, span, BS), lambda b: (0, b + start, 0, 0)),
            ],
            out_specs=[
                pl.BlockSpec((owners, 1, span, BS), lambda b: (0, b, 0, 0)),
                pl.BlockSpec((1, 4 * BS + 8, BS), lambda b: (b, 0, 0)),
            ],
            out_shape=[
                jax.ShapeDtypeStruct((owners, count, span, BS), F32),
                jax.ShapeDtypeStruct((count, 4 * BS + 8, BS), F32),
            ],
            scratch_shapes=[
                pltpu.VMEM((owners * span, BS), F32),
                pltpu.VMEM((owners * span, BS), F32),
                pltpu.VMEM((own // group, 2 * height, 2 * group * BS), BF16),
                pltpu.VMEM((own // group, 2 * height, 2 * group * BS), BF16),
                pltpu.VMEM((tokens, 2 * BS), BF16),
                pltpu.VMEM((tokens, 2 * BS), BF16),
                pltpu.VMEM((tokens, 2 * BS), BF16),
                pltpu.VMEM((tokens, 2 * BS), BF16),
                pltpu.VMEM((8, 2 * BS), F32),
            ],
            compiler_params=params(),
            cost_estimate=cost(flops, 3 * count * owners * span * BS * 4, 4 * tokens * BS * count),
            name=f"mixer_{index}",
        )(
            fwd_high,
            fwd_low,
            inv_high,
            inv_low,
            w_one,
            w_one_t,
            w_two,
            w_two_t,
            bias,
            shift,
            x_spec.reshape(owners, count, span, BS),
            cot_spec.reshape(owners, blocks, span, BS),
        )

    mixed = [mix(i, exchange(piece)) for i, piece in enumerate(input_lon)]
    param_sums = lax.psum(jnp.concatenate([m[1] for m in mixed], 0), "row")

    grads = []
    sums = None
    for index, count in enumerate(chunks):
        start = starts[index]
        piece = exchange(mixed[index][0].reshape(owners, count, rows, padded, BS))
        in_spec = pl.BlockSpec(
            (1, 1, width, count * BS), lambda h, at=start // count: (0, h, 0, at)
        )
        carry_in = sums is not None
        grad, sums = pl.pallas_call(
            functools.partial(lon_back_kernel, start, carry_in),
            grid=(rows,),
            in_specs=[
                whole((width, tall)),
                spectrum_spec(count),
                in_spec,
                stat_spec,
                whole((1, local)),
            ]
            + [stat_spec] * carry_in,
            out_specs=[pl.BlockSpec((1, width, count * BS), lambda h: (h, 0, 0)), stat_spec],
            out_shape=[
                jax.ShapeDtypeStruct((rows, width, count * BS), F32),
                jax.ShapeDtypeStruct((rows, 2, width), F32),
            ],
            compiler_params=params(),
            cost_estimate=cost(
                2 * rows * tall * width * count * BS, rows * count * BS * (6 * width + 4 * tall)
            ),
            name=f"lon_back_{index}",
        )(back, piece, inputs, stats, gain, *([sums] * carry_in))
        grads.append(grad)

    input_grad = pl.pallas_call(
        functools.partial(finish_kernel, chunks, total_chan),
        grid=(rows,),
        in_specs=[row_spec, row_spec, stat_spec, stat_spec]
        + [pl.BlockSpec((1, width, count * BS), lambda h: (h, 0, 0)) for count in chunks],
        out_specs=row_spec,
        out_shape=jax.ShapeDtypeStruct(inputs.shape, BF16),
        compiler_params=params(),
        cost_estimate=cost(10 * rows * width * local, rows * width * local * 10),
        name="finish",
    )(inputs, cotangent, stats, lax.psum(sums, "chan"), *grads)

    spec_scale = 1.0 / math.sqrt(batch * height * K)
    dw = param_sums[:, : 4 * BS].reshape(blocks, 2, 2, BS, BS).transpose(1, 2, 0, 3, 4) * spec_scale
    db = param_sums[:, 4 * BS : 4 * BS + 4].reshape(blocks, 2, 2, BS).transpose(1, 2, 0, 3)
    db = db * spec_scale
    ln_scale = 1.0 / math.sqrt(batch * height * width)
    gain_grad = param_sums[:, 4 * BS + 4].reshape(local) / ln_gain * ln_scale
    return (
        input_grad,
        dw[0].reshape(2, local, BS),
        db[0].reshape(2, local),
        dw[1].reshape(2, local, BS),
        db[1].reshape(2, local),
        gain_grad,
        param_sums[:, 4 * BS + 5].reshape(local),
    )


def solution(mesh):
    placed = (
        P(None, "row", None, "chan"),
        P(None, "row", None, "chan"),
        P("chan"),
        P("chan"),
        P(None, "chan", None),
        P(None, "chan"),
        P(None, "chan", None),
        P(None, "chan"),
    )
    return jax.shard_map(
        on_device,
        mesh=mesh,
        in_specs=placed,
        out_specs=(
            P(None, "row", None, "chan"),
            P(None, "chan", None),
            P(None, "chan"),
            P(None, "chan", None),
            P(None, "chan"),
            P("chan"),
            P("chan"),
        ),
        check_vma=False,
    )
```

time: 943 us -> 854 us (0.906)
  blocking collectives: 82.5 us -> 396 us
  waiting for transfers between devices: 493 us -> 228 us
  Pallas kernels: 0 us -> 130 us
  matrix products: 104 us -> 0 us
  local copies, waits for them, and re-layouts: 115 us -> 25.4 us
  starting transfers between devices: 89.1 us -> 46.8 us
  other arithmetic: 35.9 us -> 11.4 us
    all_to_all x0 -> x2, blocking collectives: none -> 371 us  [exchange(): return lax.all_to_all(piece, 'row', split_axis=0, concat_axis=0, tiled=True)]
    all_to_all x3, waiting for transfers between devices: 242 us -> 103 us  [exchange(): return lax.all_to_all(piece, 'row', split_axis=0, concat_axis=0, tiled=True)]
    pallas_call x0 -> x7, Pallas kernels: none -> 130 us  [the longest x2 58.8 us: mix(): pl.pallas_call(functools.partial(mixer_kernel, own, group), grid=(count,)...]
    psum x1, waiting for transfers between devices: 251 us -> 124 us  [on_device(): param_sums = lax.psum(jnp.concatenate([m[1] for m in mixed], 0), 'row')]
    dot_general x31 -> x0, matrix products: 104 us -> none  [the longest x2 27.2 us: to_spectrum(): return jnp.einsum('qgph,bhpkc->bqgkc', forward_lat, piece, precision=HIGHER)]
    psum x2 -> x1, blocking collectives: 66.6 us -> 8.58 us  [on_device(): lax.psum(sums, 'chan')]
    all_to_all x3, starting transfers between devices: 88.9 us -> 46.7 us  [exchange(): return lax.all_to_all(piece, 'row', split_axis=0, concat_axis=0, tiled=True)]
    transpose x2 -> x0, local copies, waits for them, and re-layouts: 30.1 us -> none  [the longest x1 15.1 us: on_device(): jnp.einsum('bhwc,wpk->bhpkc', mixed_in, longitude, precision=HIGHER)]
  transfers between devices with their start and end apart: 4 -> 4, of which waited for: 3 -> 2; matrix products, arithmetic and copies ran while one was open for 10% -> 1% of each run, Pallas kernels for 0% -> 8%
where the time goes in v1:
time: 854 us; the launch traced here: 852 us
  blocking collectives  396 us (46%)
  waiting for transfers between devices  228 us (27%)
  Pallas kernels  130 us (15%)
  starting transfers between devices  46.8 us (5%)
  local copies, waits for them, and re-layouts  25.4 us (3%)
  between operations  14.5 us (2%)
  other arithmetic  11.4 us (1%)
    all_to_all x2, blocking collectives, exchange(): return lax.all_to_all(piece, 'row', split_axis=0, concat_axis=0, tiled=True)  371 us
    psum x1, waiting for transfers between devices, on_device(): param_sums = lax.psum(jnp.concatenate([m[1] for m in mixed], 0), 'row')  124 us
    all_to_all x3, waiting for transfers between devices, exchange(): return lax.all_to_all(piece, 'row', split_axis=0, concat_axis=0, tiled=True)  103 us
    pallas_call x2, Pallas kernels, mix(): pl.pallas_call(functools.partial(mixer_kernel, own, group), grid=(count,)...  58.8 us
    all_to_all x3, starting transfers between devices, exchange(): return lax.all_to_all(piece, 'row', split_axis=0, concat_axis=0, tiled=True)  46.7 us
    pallas_call x2, Pallas kernels, on_device(): pl.pallas_call(functools.partial(lon_back_kernel, start, carry_in), grid=...  24.4 us
    unnamed x73, local copies, waits for them, and re-layouts  20.6 us
    pallas_call x1, Pallas kernels, on_device(): pl.pallas_call(input_lon_kernel, grid=(rows,), in_specs=[whole((tall, wid...  19.8 us
  transfers between devices with their start and end apart: 4, of which 2 were waited for; matrix products, arithmetic and copies ran while one was open for 1% of the time, Pallas kernels for 8%

profile of v1, /device:TPU:0, one launch (start us, length us, event | category | flops | bytes accessed | tf_op | source)
XLA Modules:
  0.0 851.7 jit_solution(10691179946681241613)
XLA Ops:
  7.2 1.1 copy-done.14
  8.3 1.3 copy-done.15
  9.6 12.7 %cot_lon.1 = f32[16,4,12,24,128]{4,3,2,1,0:T(8,128)} custom-call(bf16[384,448]{1,0:T(8,128)(2,1)S(1)} %copy-done.15, bf16[384,448]{1,0:T(8,128)(2,1)S(1)} %copy-done.14, bf16[1,12,448,512]{3,2,1,0:T(8,128)(2,1)} %refs_1_.1), custom_call_target="tpu_custom_call" | custom-call | flops 4227858432 | bytes 14942208 | tf_op jit(solution)/shard_map/cot_lon/pallas_call | solution.py:351
  23.2 9.9 %psum.28 = f32[1,12,448]{2,0,1:T(1,128)S(1)} all-reduce(f32[1,12,448]{2,0,1:T(1,128)S(1)} %reduce_sum.23), channel_id=1, replica_groups=mesh['chan'=2,'row'=16] {'chan'}, use_global_device_ids=true, to_apply=%region_1.0 | all-reduce | flops 5376 | bytes 43008 | tf_op jit(solution)/shard_map/psum | solution.py:365
  33.1 4.6 fusion.1
  37.8 6.8 psum.29
  44.8 19.8 %input_lon.1 = (f32[16,3,12,24,128]{4,3,2,1,0:T(8,128)}, f32[16,1,12,24,128]{4,3,2,1,0:T(8,128)}) custom-call(bf16[384,448]{1,0:T(8,128)(2,1)S(1)} %copy-done.19, bf16[384,448]{1,0:T(8,128)(2,1)S(1)} %copy-done.18, bf16[1,12,448,512]{3,2,1,0:T(8,128)(2,1)} %refs_0_, f32[12,2,448]{2,1,0:T(2,128)S(1)} %pad_maximum_fusion.1.stat_ref.refs_2_, f32[1,512]{1,0:T(1,128)S(1)} %bitcast.41), custom_call_target="tpu_custom_call" | custom-call | flops 6341787648 | bytes 14942208 | tf_op jit(solution)/shard_map/input_lon/pallas_call | solution.py:370
  64.6 161.8 %all_to_all.25 = f32[16,3,12,24,128]{4,3,2,1,0:T(8,128)} all-to-all(f32[16,3,12,24,128]{4,3,2,1,0:T(8,128)} %get-tuple-element.23), channel_id=1, replica_groups=mesh['chan'=2,'row'=16] {'row'}, dimensions={0} | all-to-all | bytes 14155776 | tf_op jit(solution)/shard_map/all_to_all | solution.py:339
  226.4 209.2 %all_to_all.26 = f32[16,4,12,24,128]{4,3,2,1,0:T(8,128)} all-to-all(f32[16,4,12,24,128]{4,3,2,1,0:T(8,128)S(1)} %bitcast.45), channel_id=1, replica_groups=mesh['chan'=2,'row'=16] {'row'}, dimensions={0} | all-to-all | bytes 18874368 | tf_op jit(solution)/shard_map/all_to_all | solution.py:339
  435.6 6.0 all-to-all-start
  443.8 1.2 copy-done.10
  446.9 43.3 %mixer_0.1 = (f32[16,3,288,128]{3,2,1,0:T(8,128)}, f32[3,520,128]{2,1,0:T(8,128)S(1)}) custom-call(bf16[384,384]{1,0:T(8,128)(2,1)S(1)} %copy-done.26, bf16[384,384]{1,0:T(8,128)(2,1)S(1)} %copy-done.24, bf16[384,384]{1,0:T(8,128)(2,1)S(1)} %copy-done.22, bf16[384,384]{1,0:T(8,128)(2,1)S(1)} %copy-done.20, bf16[4,256,256]{2,1,0:T(8,128)(2,1)S(1)} %copy.44.w_one_ref, ...), custom_call_target="tpu_custom_call" | custom-call | flops 17666408448 | bytes 21233664 | tf_op jit(solution)/shard_map/mixer_0/pallas_call | solution.py:416
  490.2 9.5 %all-to-all-start.4 = ((f32[16,3,12,24,128]{4,3,2,1,0:T(8,128)}), f32[16,3,12,24,128]{4,3,2,1,0:T(8,128)}, u32[]{:S(2)}, u32[]{:S(2)}) async-start(f32[16,3,12,24,128]{4,3,2,1,0:T(8,128)} %bitcast.49), calls=%async_computation.4 | async-start | bytes 14155776 | tf_op jit(solution)/shard_map/all_to_all | solution.py:339
  499.8 1.0 copy-done.7
  500.8 1.0 copy-done.9
  501.9 1.0 copy-done.11
  502.9 1.0 copy-done.13
  506.8 15.5 %mixer_1.1 = (f32[16,1,288,128]{3,2,1,0:T(8,128)S(1)}, f32[1,520,128]{2,1,0:T(8,128)S(1)}) custom-call(bf16[384,384]{1,0:T(8,128)(2,1)S(1)} %copy-done.27, bf16[384,384]{1,0:T(8,128)(2,1)S(1)} %copy-done.25, bf16[384,384]{1,0:T(8,128)(2,1)S(1)} %copy-done.23, bf16[384,384]{1,0:T(8,128)(2,1)S(1)} %copy-done.21, bf16[4,256,256]{2,1,0:T(8,128)(2,1)S(1)} %copy-done.9, ...), custom_call_target="tpu_custom_call" | custom-call | flops 5888802816 | bytes 7077888 | tf_op jit(solution)/shard_map/mixer_1/pallas_call | solution.py:416
  522.3 1.4 copy-done.4
  524.4 103.2 %all-to-all-done.4.grad_ref = f32[16,3,12,24,128]{4,3,2,1,0:T(8,128)} async-done(((f32[16,3,12,24,128]{4,3,2,1,0:T(8,128)}), f32[16,3,12,24,128]{4,3,2,1,0:T(8,128)}, u32[]{:S(2)}, u32[]{:S(2)}) %all-to-all-start.4) | async-done | bytes 7077920 | tf_op jit(solution)/shard_map/all_to_all | solution.py:339
  627.7 31.2 %all-to-all-start.2 = ((f32[16,1,12,24,128]{4,3,2,1,0:T(8,128)}), f32[16,1,12,24,128]{4,3,2,1,0:T(8,128)S(1)}, u32[]{:S(2)}, u32[]{:S(2)}) async-start(f32[16,1,12,24,128]{4,3,2,1,0:T(8,128)} %bitcast.40), calls=%async_computation.2 | async-start | bytes 4718592 | tf_op jit(solution)/shard_map/all_to_all | solution.py:339
  659.0 2.1 pad_maximum_fusion
  661.1 124.3 %all-reduce.4.cloned.1.call-done = f32[4,520,128]{2,1,0:T(8,128)} async-done(((f32[4,520,128]{2,1,0:T(8,128)}), f32[4,520,128]{2,1,0:T(8,128)}) %all-reduce.4.cloned.1.call-update) | async-done | bytes 1064976 | tf_op jit(solution)/shard_map/psum | solution.py:465
  785.4 1.3 slice_multiply_fusion
  788.5 1.4 fusion.5
  791.8 2.6 copy-done.1
  794.3 13.5 %lon_back_0.1 = (f32[12,448,384]{2,1,0:T(8,128)}, f32[12,2,448]{2,1,0:T(2,128)S(1)}) custom-call(bf16[448,384]{1,0:T(8,128)(2,1)S(1)} %copy-done.5, f32[16,3,12,24,128]{4,3,2,1,0:T(8,128)} %all-to-all-done.4.grad_ref, bf16[1,12,448,512]{3,2,1,0:T(8,128)(2,1)S(1)} %copy-done.1, f32[12,2,448]{2,1,0:T(2,128)S(1)} %pad_maximum_fusion.1.stat_ref.refs_2_, ...), custom_call_target="tpu_custom_call" | custom-call | flops 1585446912 | bytes 19464192 | tf_op jit(solution)/shard_map/lon_back_0/pallas_call | solution.py:476
  807.8 10.9 %lon_back_1.1 = (f32[12,448,128]{2,1,0:T(8,128)S(1)}, f32[12,2,448]{2,1,0:T(2,128)S(1)}) custom-call(bf16[448,384]{1,0:T(8,128)(2,1)S(1)} %copy-done.5, f32[16,1,12,24,128]{4,3,2,1,0:T(8,128)S(1)} %all-to-all-done.2.grad_ref, bf16[1,12,448,512]{3,2,1,0:T(8,128)(2,1)} %refs_0_, f32[12,2,448]{2,1,0:T(2,128)S(1)} %pad_maximum_fusion.1.stat_ref.refs_2_, ...), custom_call_target="tpu_custom_call" | custom-call | flops 528482304 | bytes 6488064 | tf_op jit(solution)/shard_map/lon_back_1/pallas_call | solution.py:476
  818.7 1.6 copy-done.2
  820.2 8.6 %psum.30.refs_3_ = f32[12,2,448]{2,1,0:T(2,128)S(1)} all-reduce(f32[12,2,448]{2,1,0:T(2,128)S(1)} %get-tuple-element.26), channel_id=1, replica_groups=mesh['chan'=2,'row'=16] {'chan'}, use_global_device_ids=true, to_apply=%region_4.0 | all-reduce | flops 10752 | bytes 86016 | tf_op jit(solution)/shard_map/psum | solution.py:510
  828.8 1.8 copy-done.3
  830.6 14.3 %finish.1 = bf16[1,12,448,512]{3,2,1,0:T(8,128)(2,1)} custom-call(bf16[1,12,448,512]{3,2,1,0:T(8,128)(2,1)} %refs_0_, bf16[1,12,448,512]{3,2,1,0:T(8,128)(2,1)} %refs_1_.1, f32[12,2,448]{2,1,0:T(2,128)S(1)} %pad_maximum_fusion.1.stat_ref.refs_2_, f32[12,2,448]{2,1,0:T(2,128)S(1)} %psum.30.refs_3_, f32[12,448,384]{2,1,0:T(8,128)} %get-tuple-element.27.refs_4_, ...), custom_call_target="tpu_custom_call" | custom-call | flops 27525120 | bytes 27525120 | tf_op jit(solution)/shard_map/finish/pallas_call | solution.py:500
  (94 shorter events, 12.5 us)
Async XLA Ops:
  7.2 15.1 %copy-start = (bf16[1,12,448,512]{3,2,1,0:T(8,128)(2,1)S(1)}, bf16[1,12,448,512]{3,2,1,0:T(8,128)(2,1)}, u32[]{:S(2)}) copy-start(bf16[1,12,448,512]{3,2,1,0:T(8,128)(2,1)} %refs_0_) | copy-start | bytes 16515076
  7.2 1.1 copy-start.14
  8.3 1.3 copy-start.15
  22.3 22.4 %copy-start.17 = (f32[512]{0:T(512)S(1)}, f32[512]{0:T(512)}, u32[]{:S(2)}) copy-start(f32[512]{0:T(512)} %param.19) | copy-start | bytes 6148
  22.3 22.4 %copy-start.18 = (bf16[384,448]{1,0:T(8,128)(2,1)S(1)}, bf16[384,448]{1,0:T(8,128)(2,1)}, u32[]{:S(2)}) copy-start(bf16[384,448]{1,0:T(8,128)(2,1)} %constant.44.clone.low_ref) | copy-start | bytes 1032196
  22.3 22.4 %copy-start.19 = (bf16[384,448]{1,0:T(8,128)(2,1)S(1)}, bf16[384,448]{1,0:T(8,128)(2,1)}, u32[]{:S(2)}) copy-start(bf16[384,448]{1,0:T(8,128)(2,1)} %constant.43.clone.high_ref) | copy-start | bytes 1032196
  44.7 181.6 %slice-start = ((s8[9437184]{0:T(1024)(128)(4,1)}), s8[4194304]{0:T(1024)(128)(4,1)S(1)}, s32[]{:S(2)}) async-start(s8[9437184]{0:T(1024)(128)(4,1)} %bitcast.44), calls=%async_computation.6 | async-start | bytes 8388608
  44.7 181.6 %slice-start.1 = ((s8[9437184]{0:T(1024)(128)(4,1)}), s8[1048576]{0:T(1024)(128)(4,1)S(1)}, s32[]{:S(2)}) async-start(s8[9437184]{0:T(1024)(128)(4,1)} %bitcast.44), calls=%async_computation.7 | async-start | bytes 2097152
  64.6 161.8 %slice-start.2 = ((s8[9437184]{0:T(1024)(128)(4,1)}), s8[4194304]{0:T(1024)(128)(4,1)S(1)}, s32[]{:S(2)}) async-start(s8[9437184]{0:T(1024)(128)(4,1)} %bitcast.44), calls=%async_computation.8 | async-start | bytes 8388608
  226.4 215.2 %copy-start.30 = (f32[2,512]{1,0:T(2,128)S(1)}, f32[2,512]{1,0:T(2,128)}, u32[]{:S(2)}) copy-start(f32[2,512]{1,0:T(2,128)} %param.24) | copy-start | bytes 12292
  226.4 215.2 %copy-start.31 = (f32[2,512]{1,0:T(2,128)S(1)}, f32[2,512]{1,0:T(2,128)}, u32[]{:S(2)}) copy-start(f32[2,512]{1,0:T(2,128)} %param.22) | copy-start | bytes 12292
  226.4 215.2 %copy-start.28 = (bf16[2,512,128]{2,1,0:T(8,128)(2,1)S(1)}, bf16[2,512,128]{2,1,0:T(8,128)(2,1)}, u32[]{:S(2)}) copy-start(bf16[2,512,128]{2,1,0:T(8,128)(2,1)} %param.21) | copy-start | bytes 786436
  435.6 6.4 copy-start.29
  435.6 8.2 copy-start.32
  435.6 8.2 copy-start.24
  435.6 8.2 copy-start.26
  435.6 54.6 %all-to-all-start = ((f32[16,1,12,24,128]{4,3,2,1,0:T(8,128)}), f32[16,1,12,24,128]{4,3,2,1,0:T(8,128)}, u32[]{:S(2)}, u32[]{:S(2)}) async-start(f32[16,1,12,24,128]{4,3,2,1,0:T(8,128)} %get-tuple-element.20), calls=%async_computation | async-start | bytes 4718592 | tf_op jit(solution)/shard_map/all_to_all | solution.py:339
  443.3 46.9 %copy-start.12 = (bf16[4,256,256]{2,1,0:T(8,128)(2,1)}, bf16[4,256,256]{2,1,0:T(8,128)(2,1)S(1)}, u32[]{:S(2)}) copy-start(bf16[4,256,256]{2,1,0:T(8,128)(2,1)S(1)} %get-tuple-element.48.w_one_t_ref) | copy-start | bytes 1572868
  443.5 46.7 %copy-start.6 = (bf16[4,256,256]{2,1,0:T(8,128)(2,1)}, bf16[4,256,256]{2,1,0:T(8,128)(2,1)S(1)}, u32[]{:S(2)}) copy-start(bf16[4,256,256]{2,1,0:T(8,128)(2,1)S(1)} %copy.45.w_two_ref) | copy-start | bytes 1572868
  443.8 46.5 %copy-start.8 = (bf16[4,256,256]{2,1,0:T(8,128)(2,1)}, bf16[4,256,256]{2,1,0:T(8,128)(2,1)S(1)}, u32[]{:S(2)}) copy-start(bf16[4,256,256]{2,1,0:T(8,128)(2,1)S(1)} %copy.44.w_one_ref) | copy-start | bytes 1572868
  443.8 1.2 copy-start.10
  490.2 9.6 %copy-start.27 = (bf16[384,384]{1,0:T(8,128)(2,1)S(1)}, bf16[384,384]{1,0:T(8,128)(2,1)}, u32[]{:S(2)}) copy-start(bf16[384,384]{1,0:T(8,128)(2,1)} %constant.45.clone.fwd_high_ref) | copy-start | bytes 884740
  490.2 137.4 %all-to-all-start.4 = ((f32[16,3,12,24,128]{4,3,2,1,0:T(8,128)}), f32[16,3,12,24,128]{4,3,2,1,0:T(8,128)}, u32[]{:S(2)}, u32[]{:S(2)}) async-start(f32[16,3,12,24,128]{4,3,2,1,0:T(8,128)} %bitcast.49), calls=%async_computation.4 | async-start | bytes 14155776 | tf_op jit(solution)/shard_map/all_to_all | solution.py:339
  499.8 1.0 copy-start.7
  500.8 1.0 copy-start.9
  522.3 1.4 copy-start.4
  627.7 180.1 %all-to-all-start.2 = ((f32[16,1,12,24,128]{4,3,2,1,0:T(8,128)}), f32[16,1,12,24,128]{4,3,2,1,0:T(8,128)S(1)}, u32[]{:S(2)}, u32[]{:S(2)}) async-start(f32[16,1,12,24,128]{4,3,2,1,0:T(8,128)} %bitcast.40), calls=%async_computation.2 | async-start | bytes 4718592 | tf_op jit(solution)/shard_map/all_to_all | solution.py:339
  658.9 132.9 %copy-start.5 = (bf16[448,384]{1,0:T(8,128)(2,1)S(1)}, bf16[448,384]{1,0:T(8,128)(2,1)}, u32[]{:S(2)}) copy-start(bf16[448,384]{1,0:T(8,128)(2,1)} %constant.49.clone.table_ref) | copy-start | bytes 1032196
  658.9 126.5 %all-reduce.4.cloned.1.call-start = ((), (), s32[]{:S(2)}) async-start(), calls=%async_computation.5 | async-start | bytes 2129920 | tf_op jit(solution)/shard_map/psum | solution.py:465
  791.8 2.6 copy-start.1
  818.7 1.6 copy-start.2
  828.8 1.8 copy-start.3
  (8 other events, 7.6 us)
Sparse Core Ops, SparseCore 0:
  663.2 122.1 all-reduce.3

commit v2 on v1

--- a/solution.py
+++ b/solution.py
@@ -16,7 +16,7 @@
 ROOT_TWO_PI = math.sqrt(2.0 / math.pi)
 BF16 = jnp.bfloat16
 F32 = jnp.float32
-VMEM_LIMIT = 48 * 1024 * 1024
+VMEM_LIMIT = 60 * 1024 * 1024
 
 
 def gelu_parts(values):
@@ -102,29 +102,32 @@
     return [wide[:, i * 128 : (i + 1) * 128] for i in range(count)]
 
 
-def cot_lon_kernel(high_ref, low_ref, cot_ref, out_ref):
-    owners, blocks, _, padded, _ = out_ref.shape
-    values = cot_ref[0, 0]
-    result = dot(high_ref[...], values) + dot(low_ref[...], values)
-    for b in range(blocks):
-        out_ref[:, b, 0] = result[:, b * BS : (b + 1) * BS].reshape(owners, padded, BS)
-
-
-def input_lon_kernel(high_ref, low_ref, in_ref, stat_ref, gain_ref, *out_refs):
-    mean, rstd = columns_of(stat_ref[0])
-    at = 0
-    for out_ref in out_refs:
-        owners, blocks, _, padded, _ = out_ref.shape
-        pieces = []
-        for b in range(at, at + blocks):
-            lanes = slice(b * BS, (b + 1) * BS)
-            values = in_ref[0, 0, :, lanes].astype(F32)
-            pieces.append((values - mean) * rstd * gain_ref[:, lanes])
-        at += blocks
-        high, low = split(jnp.concatenate(pieces, 1))
-        result = dot(high_ref[...], high) + dot(high_ref[...], low) + dot(low_ref[...], high)
+def cot_lon_kernel(table_ref, cot_ref, out_ref):
+    owners, blocks, rows, padded, _ = out_ref.shape
+    for r in range(rows):
+        result = dot(table_ref[...], cot_ref[0, r])
         for b in range(blocks):
-            out_ref[:, b, 0] = result[:, b * BS : (b + 1) * BS].reshape(owners, padded, BS)
+            out_ref[:, b, r] = result[:, b * BS : (b + 1) * BS].reshape(owners, padded, BS)
+
+
+def input_lon_kernel(table_ref, in_ref, stat_ref, gain_ref, *out_refs):
+    tall = table_ref.shape[0] // 2
+    for r in range(in_ref.shape[1]):
+        mean, rstd = columns_of(stat_ref[r])
+        at = 0
+        for out_ref in out_refs:
+            owners, blocks, _, padded, _ = out_ref.shape
+            pieces = []
+            for b in range(at, at + blocks):
+                lanes = slice(b * BS, (b + 1) * BS)
+                values = in_ref[0, r, :, lanes].astype(F32)
+                pieces.append((values - mean) * rstd * gain_ref[:, lanes])
+            at += blocks
+            high, low = split(jnp.concatenate(pieces, 1))
+            both = dot(table_ref[...], high)
+            result = both[:tall] + both[tall:] + dot(table_ref[:tall], low)
+            for b in range(blocks):
+                out_ref[:, b, r] = result[:, b * BS : (b + 1) * BS].reshape(owners, padded, BS)
 
 
 def mixer_kernel(
@@ -252,50 +255,93 @@
     )
 
 
-def lon_back_kernel(offset, carry_in, table_ref, grad_ref, in_ref, stat_ref, gain_ref, *refs):
+def lon_back_kernel(
+    offset, carry_in, table_ref, grad_ref, in_ref, cot_ref, stat_ref, gain_ref, *refs
+):
     if carry_in:
         before_ref, out_ref, sums_ref = refs
     else:
         out_ref, sums_ref = refs
-    sources, blocks, _, padded, _ = grad_ref.shape
-    mean, rstd = columns_of(stat_ref[0])
-    pieces = [grad_ref[:, b, 0].reshape(sources * padded, BS).astype(BF16) for b in range(blocks)]
-    mixed = dot(table_ref[...], jnp.concatenate(pieces, 1))
+    sources, blocks, rows, padded, _ = grad_ref.shape
     ones = jnp.ones((16, BS), BF16)
-    grads = jnp.zeros((in_ref.shape[2], BS), F32)
-    products = jnp.zeros((in_ref.shape[2], BS), F32)
-    for b in range(blocks):
-        lanes = slice((offset + b) * BS, (offset + b + 1) * BS)
-        grad = mixed[:, b * BS : (b + 1) * BS] * gain_ref[:, lanes]
-        values = in_ref[0, 0, :, b * BS : (b + 1) * BS].astype(F32)
-        out_ref[0, :, b * BS : (b + 1) * BS] = grad
-        grads = grads + grad
-        products = products + grad * ((values - mean) * rstd)
-    rows = []
-    for values in (grads, products):
-        high, low = split(values)
-        rows.append((dot_cols(ones, high) + dot_cols(ones, low))[0:1])
-    sums = jnp.concatenate(rows, 0)
-    if carry_in:
-        sums = sums + before_ref[0]
-    sums_ref[0] = sums
+    for r in range(rows):
+        mean, rstd = columns_of(stat_ref[r])
+        pieces = [
+            grad_ref[:, b, r].reshape(sources * padded, BS).astype(BF16) for b in range(blocks)
+        ]
+        mixed = dot(table_ref[...], jnp.concatenate(pieces, 1))
+        grads = jnp.zeros((in_ref.shape[2], BS), F32)
+        products = jnp.zeros((in_ref.shape[2], BS), F32)
+        for b in range(blocks):
+            lanes = slice((offset + b) * BS, (offset + b + 1) * BS)
+            grad = mixed[:, b * BS : (b + 1) * BS] * gain_ref[:, lanes]
+            values = in_ref[0, r, :, b * BS : (b + 1) * BS].astype(F32)
+            cot = cot_ref[0, r, :, b * BS : (b + 1) * BS].astype(F32)
+            out_ref[r, :, b * BS : (b + 1) * BS] = cot + rstd * grad
+            grads = grads + grad
+            products = products + grad * ((values - mean) * rstd)
+        both = []
+        for values in (grads, products):
+            high, low = split(values)
+            both.append((dot_cols(ones, high) + dot_cols(ones, low))[0:1])
+        sums = jnp.concatenate(both, 0)
+        if carry_in:
+            sums = sums + before_ref[r]
+        sums_ref[r] = sums
 
 
 def finish_kernel(chunks, channels, *refs):
-    in_ref, cot_ref, stat_ref, sums_ref = refs[:4]
-    grad_refs = refs[4 : 4 + len(chunks)]
+    in_ref, stat_ref, sums_ref = refs[:3]
+    base_refs = refs[3 : 3 + len(chunks)]
     out_ref = refs[-1]
-    stats = jnp.concatenate([stat_ref[0], sums_ref[0] / channels], 0)
-    mean, rstd, one, two = columns_of(stats)
-    at = 0
-    for grad_ref, blocks in zip(grad_refs, chunks):
-        for b in range(blocks):
-            lanes = slice(at * BS, (at + 1) * BS)
-            normed = (in_ref[0, 0, :, lanes].astype(F32) - mean) * rstd
-            grad = grad_ref[0, :, b * BS : (b + 1) * BS]
-            cot = cot_ref[0, 0, :, lanes].astype(F32)
-            out_ref[0, 0, :, lanes] = (cot + rstd * (grad - one - normed * two)).astype(BF16)
-            at += 1
+    for r in range(in_ref.shape[1]):
+        mean, rstd = stat_ref[r, 0:1], stat_ref[r, 1:2]
+        slope = rstd * rstd * (sums_ref[r, 1:2] / channels)
+        level = rstd * (sums_ref[r, 0:1] / channels) - mean * slope
+        level, slope = columns_of(jnp.concatenate([level, slope], 0))
+        at = 0
+        for base_ref, blocks in zip(base_refs, chunks):
+            for b in range(blocks):
+                lanes = slice(at * BS, (at + 1) * BS)
+                values = in_ref[0, r, :, lanes].astype(F32)
+                base = base_ref[r, :, b * BS : (b + 1) * BS]
+                out_ref[0, r, :, lanes] = (base - level - slope * values).astype(BF16)
+                at += 1
+
+
+def xor_permute(piece, axis, bit):
+    size = lax.axis_size(axis)
+    return lax.ppermute(piece, axis, [(i, i ^ bit) for i in range(size)])
+
+
+def sum_small(piece, axis):
+    bit = 1
+    while bit < lax.axis_size(axis):
+        piece = piece + xor_permute(piece, axis, bit)
+        bit *= 2
+    return piece
+
+
+def sum_halving(piece, axis):
+    size = lax.axis_size(axis)
+    index = lax.axis_index(axis)
+    bits = [1 << i for i in range(size.bit_length() - 1)]
+    for bit in bits:
+        half = piece.shape[0] // 2
+        low, high = piece[:half], piece[half:]
+        upper = (index & bit) != 0
+        piece = jnp.where(upper, high, low) + xor_permute(jnp.where(upper, low, high), axis, bit)
+    for bit in reversed(bits):
+        other = xor_permute(piece, axis, bit)
+        upper = (index & bit) != 0
+        piece = jnp.concatenate(
+            [jnp.where(upper, other, piece), jnp.where(upper, piece, other)], 0
+        )
+    return piece
+
+
+def divisor(count, limit):
+    return max(n for n in range(1, limit + 1) if count % n == 0)
 
 
 def params():
@@ -330,7 +376,8 @@
 
     lon = lon_table(width, owners, padded)
     lon_high, lon_low = high_low(lon)
-    cot_high, cot_low = high_low(lon * kept_scale(owners, padded))
+    lon_both = np.concatenate([lon_high, lon_low], 0)
+    cot_high, _ = high_low(lon * kept_scale(owners, padded))
     back = np.ascontiguousarray(lon.T).astype(np.float32).astype(jnp.bfloat16)
     fwd_high, fwd_low = high_low(lat_table(height))
     inv_high, inv_low = high_low(lat_table(height).T)
@@ -338,11 +385,20 @@
     def exchange(piece):
         return lax.all_to_all(piece, "row", split_axis=0, concat_axis=0, tiled=True)
 
-    row_spec = pl.BlockSpec((1, 1, width, local), lambda h: (0, h, 0, 0))
-    stat_spec = pl.BlockSpec((1, 2, width), lambda h: (h, 0, 0))
-
-    def spectrum_spec(count):
-        return pl.BlockSpec((owners, count, 1, padded, BS), lambda h: (0, 0, h, 0, 0))
+    few = divisor(rows, 2)
+    many = divisor(rows, 4)
+
+    def row_spec(step):
+        return pl.BlockSpec((1, step, width, local), lambda h: (0, h, 0, 0))
+
+    def stat_spec(step):
+        return pl.BlockSpec((step, 2, width), lambda h: (h, 0, 0))
+
+    def grad_spec(step, count):
+        return pl.BlockSpec((step, width, count * BS), lambda h: (h, 0, 0))
+
+    def spectrum_spec(step, count):
+        return pl.BlockSpec((owners, count, step, padded, BS), lambda h: (0, 0, h, 0, 0))
 
     def spectrum_shape(count):
         return jax.ShapeDtypeStruct((owners, count, rows, padded, BS), F32)
@@ -350,14 +406,14 @@
     lon_flops = 2 * rows * tall * width * local
     cot_lon = pl.pallas_call(
         cot_lon_kernel,
-        grid=(rows,),
-        in_specs=[whole((tall, width)), whole((tall, width)), row_spec],
-        out_specs=spectrum_spec(blocks),
+        grid=(rows // few,),
+        in_specs=[whole((tall, width)), row_spec(few)],
+        out_specs=spectrum_spec(few, blocks),
         out_shape=spectrum_shape(blocks),
         compiler_params=params(),
-        cost_estimate=cost(2 * lon_flops, rows * local * (2 * width + 4 * tall)),
+        cost_estimate=cost(lon_flops, rows * local * (2 * width + 4 * tall)),
         name="cot_lon",
-    )(cot_high, cot_low, cotangent)
+    )(cot_high, cotangent)
     cot_lon, inputs = lax.optimization_barrier((cot_lon, inputs))
     cot_spec = exchange(cot_lon)
 
@@ -369,20 +425,16 @@
 
     input_lon = pl.pallas_call(
         input_lon_kernel,
-        grid=(rows,),
-        in_specs=[
-            whole((tall, width)),
-            whole((tall, width)),
-            row_spec,
-            stat_spec,
-            whole((1, local)),
-        ],
-        out_specs=[spectrum_spec(count) for count in chunks],
+        grid=(rows // few,),
+        in_specs=[whole((2 * tall, width)), row_spec(few), stat_spec(few), whole((1, local))],
+        out_specs=[spectrum_spec(few, count) for count in chunks],
         out_shape=[spectrum_shape(count) for count in chunks],
         compiler_params=params(),
         cost_estimate=cost(3 * lon_flops, rows * local * (2 * width + 4 * tall)),
         name="input_lon",
-    )(lon_high, lon_low, inputs, stats, gain)
+    )(lon_both, inputs, stats, gain)
+    first_piece, cot_spec = lax.optimization_barrier((input_lon[0], cot_spec))
+    input_lon = [first_piece, *input_lon[1:]]
 
     def square(weight):
         re, im = weight.reshape(2, blocks, BS, BS)
@@ -462,29 +514,39 @@
         )
 
     mixed = [mix(i, exchange(piece)) for i, piece in enumerate(input_lon)]
-    param_sums = lax.psum(jnp.concatenate([m[1] for m in mixed], 0), "row")
+    param_rows = 4 * BS + 8
+    unit = 8 * owners // math.gcd(8 * owners, blocks)
+    tail = -(blocks * param_rows) % (unit * blocks)
+    flat = jnp.concatenate([m[1].reshape(-1, BS) for m in mixed], 0)
+    flat = jnp.pad(flat, ((0, tail), (0, 0)))
+    param_sums = sum_halving(flat, "row")[: blocks * param_rows]
+    param_sums = param_sums.reshape(blocks, param_rows, BS)
 
     grads = []
     sums = None
     for index, count in enumerate(chunks):
         start = starts[index]
-        piece = exchange(mixed[index][0].reshape(owners, count, rows, padded, BS))
+        piece = mixed[index][0].reshape(owners, count, rows, padded, BS)
+        carry_in = sums is not None
+        if index == len(chunks) - 1 and carry_in:
+            piece, param_sums = lax.optimization_barrier((piece, param_sums))
+        piece = exchange(piece)
         in_spec = pl.BlockSpec(
-            (1, 1, width, count * BS), lambda h, at=start // count: (0, h, 0, at)
+            (1, many, width, count * BS), lambda h, at=start // count: (0, h, 0, at)
         )
-        carry_in = sums is not None
         grad, sums = pl.pallas_call(
             functools.partial(lon_back_kernel, start, carry_in),
-            grid=(rows,),
+            grid=(rows // many,),
             in_specs=[
                 whole((width, tall)),
-                spectrum_spec(count),
+                spectrum_spec(many, count),
                 in_spec,
-                stat_spec,
+                in_spec,
+                stat_spec(many),
                 whole((1, local)),
             ]
-            + [stat_spec] * carry_in,
-            out_specs=[pl.BlockSpec((1, width, count * BS), lambda h: (h, 0, 0)), stat_spec],
+            + [stat_spec(many)] * carry_in,
+            out_specs=[grad_spec(many, count), stat_spec(many)],
             out_shape=[
                 jax.ShapeDtypeStruct((rows, width, count * BS), F32),
                 jax.ShapeDtypeStruct((rows, 2, width), F32),
@@ -494,20 +556,20 @@
                 2 * rows * tall * width * count * BS, rows * count * BS * (6 * width + 4 * tall)
             ),
             name=f"lon_back_{index}",
-        )(back, piece, inputs, stats, gain, *([sums] * carry_in))
+        )(back, piece, inputs, cotangent, stats, gain, *([sums] * carry_in))
         grads.append(grad)
 
     input_grad = pl.pallas_call(
         functools.partial(finish_kernel, chunks, total_chan),
-        grid=(rows,),
-        in_specs=[row_spec, row_spec, stat_spec, stat_spec]
-        + [pl.BlockSpec((1, width, count * BS), lambda h: (h, 0, 0)) for count in chunks],
-        out_specs=row_spec,
+        grid=(rows // few,),
+        in_specs=[row_spec(few), stat_spec(few), stat_spec(few)]
+        + [grad_spec(few, count) for count in chunks],
+        out_specs=row_spec(few),
         out_shape=jax.ShapeDtypeStruct(inputs.shape, BF16),
         compiler_params=params(),
         cost_estimate=cost(10 * rows * width * local, rows * width * local * 10),
         name="finish",
-    )(inputs, cotangent, stats, lax.psum(sums, "chan"), *grads)
+    )(inputs, stats, sum_small(sums, "chan"), *grads)
 
     spec_scale = 1.0 / math.sqrt(batch * height * K)
     dw = param_sums[:, : 4 * BS].reshape(blocks, 2, 2, BS, BS).transpose(1, 2, 0, 3, 4) * spec_scale

time: 854 us -> 709 us (0.83)
  blocking collectives: 396 us -> 212 us
  waiting for transfers between devices: 228 us -> 310 us
  local copies, waits for them, and re-layouts: 25.4 us -> 10.6 us
  between operations: 14.5 us -> 0.98 us
  Pallas kernels: 130 us -> 117 us
  starting transfers between devices: 46.8 us -> 34.4 us
    all_to_all x2 -> x1, blocking collectives: 371 us -> 196 us  [exchange(): return lax.all_to_all(piece, 'row', split_axis=0, concat_axis=0, tiled=True)]
    ppermute x0 -> x9, waiting for transfers between devices: none -> 151 us  [xor_permute(): return lax.ppermute(piece, axis, [(i, i ^ bit) for i in range(size)])]
    psum x1 -> x0, waiting for transfers between devices: 124 us -> none  [on_device(): param_sums = lax.psum(jnp.concatenate([m[1] for m in mixed], 0), 'row')]
    all_to_all x3 -> x4, waiting for transfers between devices: 103 us -> 160 us  [exchange(): return lax.all_to_all(piece, 'row', split_axis=0, concat_axis=0, tiled=True)]
    all_to_all x3 -> x4, starting transfers between devices: 46.7 us -> 24.2 us  [exchange(): return lax.all_to_all(piece, 'row', split_axis=0, concat_axis=0, tiled=True)]
    unnamed x73 -> x19, local copies, waits for them, and re-layouts: 20.6 us -> 2.84 us
    ppermute x0 -> x9, starting transfers between devices: none -> 10.2 us  [xor_permute(): return lax.ppermute(piece, axis, [(i, i ^ bit) for i in range(size)])]
    psum x1 -> x0, blocking collectives: 8.58 us -> none  [on_device(): lax.psum(sums, 'chan')]
  transfers between devices with their start and end apart: 4 -> 13, of which waited for: 2 -> 11; matrix products, arithmetic and copies ran while one was open for 1% -> 3% of each run, Pallas kernels for 8% -> 13%
where the time goes in v2:
time: 709 us; the launch traced here: 701 us
  waiting for transfers between devices  310 us (44%)
  blocking collectives  212 us (30%)
  Pallas kernels  117 us (17%)
  starting transfers between devices  34.4 us (5%)
  other arithmetic  16.3 us (2%)
  local copies, waits for them, and re-layouts  10.6 us (1%)
    all_to_all x1, blocking collectives, exchange(): return lax.all_to_all(piece, 'row', split_axis=0, concat_axis=0, tiled=True)  196 us
    all_to_all x4, waiting for transfers between devices, exchange(): return lax.all_to_all(piece, 'row', split_axis=0, concat_axis=0, tiled=True)  160 us
    ppermute x9, waiting for transfers between devices, xor_permute(): return lax.ppermute(piece, axis, [(i, i ^ bit) for i in range(size)])  151 us
    pallas_call x2, Pallas kernels, mix(): pl.pallas_call(functools.partial(mixer_kernel, own, group), grid=(count,)...  60.8 us
    all_to_all x4, starting transfers between devices, exchange(): return lax.all_to_all(piece, 'row', split_axis=0, concat_axis=0, tiled=True)  24.2 us
    pallas_call x2, Pallas kernels, on_device(): pl.pallas_call(functools.partial(lon_back_kernel, start, carry_in), grid=...  20.9 us
    pallas_call x1, Pallas kernels, on_device(): pl.pallas_call(input_lon_kernel, grid=(rows // few,), in_specs=[whole((2...  16.8 us
  transfers between devices with their start and end apart: 13, of which 11 were waited for; matrix products, arithmetic and copies ran while one was open for 3% of the time, Pallas kernels for 13%

profile of v2, /device:TPU:0, one launch (start us, length us, event | category | flops | bytes accessed | tf_op | source)
XLA Modules:
  0.0 701.5 jit_solution(3009848186793788682)
XLA Ops:
  0.6 8.8 %cot_lon.1 = f32[16,4,12,24,128]{4,3,2,1,0:T(8,128)} custom-call(bf16[384,448]{1,0:T(8,128)(2,1)} %constant.46.clone.table_ref, bf16[1,12,448,512]{3,2,1,0:T(8,128)(2,1)} %cot_ref.5), custom_call_target="tpu_custom_call" | custom-call | flops 2113929216 | bytes 14942208 | tf_op jit(solution)/shard_map/cot_lon/pallas_call | solution.py:407
  9.4 7.4 %all-to-all-start.1 = ((f32[16,4,12,24,128]{4,3,2,1,0:T(8,128)}), f32[16,4,12,24,128]{4,3,2,1,0:T(8,128)}, u32[]{:S(2)}, u32[]{:S(2)}) async-start(f32[16,4,12,24,128]{4,3,2,1,0:T(8,128)} %cot_lon.1), calls=%async_computation.1 | async-start | bytes 18874368 | tf_op jit(solution)/shard_map/all_to_all | solution.py:386
  16.9 3.5 convert_reduce_fusion
  20.4 8.3 %psum.14 = f32[1,12,448]{2,0,1:T(1,128)S(1)} all-reduce(f32[1,12,448]{2,0,1:T(1,128)S(1)} %reduce_sum.23), channel_id=1, replica_groups=mesh['chan'=2,'row'=16] {'chan'}, use_global_device_ids=true, to_apply=%region_1.0 | all-reduce | flops 5376 | bytes 43008 | tf_op jit(solution)/shard_map/psum | solution.py:421
  28.7 4.6 fusion.1
  33.3 7.3 %psum.15 = f32[1,12,448]{2,0,1:T(1,128)S(1)} all-reduce(f32[1,12,448]{2,0,1:T(1,128)S(1)} %reduce_sum.25), channel_id=1, replica_groups=mesh['chan'=2,'row'=16] {'chan'}, use_global_device_ids=true, to_apply=%region_3.0 | all-reduce | flops 5376 | bytes 43008 | tf_op jit(solution)/shard_map/psum | solution.py:423
  41.4 16.8 %input_lon.1 = (f32[16,3,12,24,128]{4,3,2,1,0:T(8,128)}, f32[16,1,12,24,128]{4,3,2,1,0:T(8,128)}) custom-call(bf16[768,448]{1,0:T(8,128)(2,1)} %constant.47.clone.table_ref, bf16[1,12,448,512]{3,2,1,0:T(8,128)(2,1)} %refs_0_, f32[12,2,448]{2,1,0:T(2,128)} %pad_maximum_fusion.4.stat_ref.refs_1_, f32[1,512]{1,0:T(1,128)} %bitcast.63), custom_call_target="tpu_custom_call" | custom-call | flops 6341787648 | bytes 14942208 | tf_op jit(solution)/shard_map/input_lon/pallas_call | solution.py:426
  58.2 127.6 %all-to-all-done.1 = f32[16,4,12,24,128]{4,3,2,1,0:T(8,128)} async-done(((f32[16,4,12,24,128]{4,3,2,1,0:T(8,128)}), f32[16,4,12,24,128]{4,3,2,1,0:T(8,128)}, u32[]{:S(2)}, u32[]{:S(2)}) %all-to-all-start.1) | async-done | bytes 9437216 | tf_op jit(solution)/shard_map/all_to_all | solution.py:386
  185.9 196.0 %all_to_all.25 = f32[16,3,12,24,128]{4,3,2,1,0:T(8,128)} all-to-all(f32[16,3,12,24,128]{4,3,2,1,0:T(8,128)} %get-tuple-element.29), channel_id=1, replica_groups=mesh['chan'=2,'row'=16] {'row'}, dimensions={0} | all-to-all | bytes 14155776 | tf_op jit(solution)/shard_map/all_to_all | solution.py:386
  381.9 4.7 all-to-all-start
  387.9 2.2 fusion.4
  390.1 2.0 copy.55.w_one_ref
  394.4 43.8 %mixer_0.1 = (f32[16,3,288,128]{3,2,1,0:T(8,128)}, f32[3,520,128]{2,1,0:T(8,128)}) custom-call(bf16[384,384]{1,0:T(8,128)(2,1)} %constant.48.clone.fwd_high_ref, bf16[384,384]{1,0:T(8,128)(2,1)} %constant.49.clone.fwd_low_ref, bf16[384,384]{1,0:T(8,128)(2,1)} %constant.50.clone.inv_high_ref, bf16[384,384]{1,0:T(8,128)(2,1)} %constant.51.clone.inv_low_ref, ...), custom_call_target="tpu_custom_call" | custom-call | flops 17666408448 | bytes 21233664 | tf_op jit(solution)/shard_map/mixer_0/pallas_call | solution.py:468
  439.6 6.4 all-to-all-start.4
  446.0 17.0 %mixer_1.1 = (f32[16,1,288,128]{3,2,1,0:T(8,128)}, f32[1,520,128]{2,1,0:T(8,128)}) custom-call(bf16[384,384]{1,0:T(8,128)(2,1)} %constant.48.clone.fwd_high_ref, bf16[384,384]{1,0:T(8,128)(2,1)} %constant.49.clone.fwd_low_ref, bf16[384,384]{1,0:T(8,128)(2,1)} %constant.50.clone.inv_high_ref, bf16[384,384]{1,0:T(8,128)(2,1)} %constant.51.clone.inv_low_ref, ...), custom_call_target="tpu_custom_call" | custom-call | flops 5888802816 | bytes 7077888 | tf_op jit(solution)/shard_map/mixer_1/pallas_call | solution.py:468
  464.4 1.6 collective-permute-done
  467.1 1.9 collective-permute-start.1
  469.1 24.9 %collective-permute-done.1 = f32[544,128]{1,0:T(8,128)S(1)} collective-permute-done((f32[544,128]{1,0:T(8,128)S(1)}, f32[544,128]{1,0:T(8,128)S(1)}, u32[]{:S(2)}, u32[]{:S(2)}) %collective-permute-start.1) | collective-permute-done | bytes 278560 | tf_op jit(solution)/shard_map/ppermute | solution.py:314
  494.1 69.8 %collective-permute-done.2 = f32[272,128]{1,0:T(8,128)S(1)} collective-permute-done((f32[272,128]{1,0:T(8,128)S(1)}, f32[272,128]{1,0:T(8,128)S(1)}, u32[]{:S(2)}, u32[]{:S(2)}) %collective-permute-start.2) | collective-permute-done | bytes 139296 | tf_op jit(solution)/shard_map/ppermute | solution.py:314
  564.0 4.6 collective-permute-start.3
  568.5 36.2 %collective-permute-done.3 = f32[136,128]{1,0:T(8,128)S(1)} collective-permute-done((f32[136,128]{1,0:T(8,128)S(1)}, f32[136,128]{1,0:T(8,128)S(1)}, u32[]{:S(2)}, u32[]{:S(2)}) %collective-permute-start.3) | collective-permute-done | bytes 69664 | tf_op jit(solution)/shard_map/ppermute | solution.py:314
  604.9 5.2 collective-permute-done.4
  610.2 5.0 collective-permute-done.5
  615.3 1.5 collective-permute-start.6
  616.8 5.1 collective-permute-done.6
  622.1 1.9 collective-permute-done.7
  624.2 5.7 all-to-all-start.3
  631.2 12.4 %lon_back_0.1 = (f32[12,448,384]{2,1,0:T(8,128)}, f32[12,2,448]{2,1,0:T(2,128)}) custom-call(bf16[448,384]{1,0:T(8,128)(2,1)} %constant.52.clone.table_ref, f32[16,3,12,24,128]{4,3,2,1,0:T(8,128)} %all-to-all-done.4.grad_ref, bf16[1,12,448,512]{3,2,1,0:T(8,128)(2,1)} %refs_0_, bf16[1,12,448,512]{3,2,1,0:T(8,128)(2,1)} %cot_ref.5, ...), custom_call_target="tpu_custom_call" | custom-call | flops 1585446912 | bytes 19464192 | tf_op jit(solution)/shard_map/lon_back_0/pallas_call | solution.py:537
  643.6 31.9 %all-to-all-done.3.grad_ref = f32[16,1,12,24,128]{4,3,2,1,0:T(8,128)S(1)} async-done(((f32[16,1,12,24,128]{4,3,2,1,0:T(8,128)}), f32[16,1,12,24,128]{4,3,2,1,0:T(8,128)S(1)}, u32[]{:S(2)}, u32[]{:S(2)}) %all-to-all-start.3) | async-done | bytes 2359328 | tf_op jit(solution)/shard_map/all_to_all | solution.py:386
  676.9 8.4 %lon_back_1.1 = (f32[12,448,128]{2,1,0:T(8,128)}, f32[12,2,448]{2,1,0:T(2,128)}) custom-call(bf16[448,384]{1,0:T(8,128)(2,1)} %constant.52.clone.table_ref, f32[16,1,12,24,128]{4,3,2,1,0:T(8,128)} %copy-done, bf16[1,12,448,512]{3,2,1,0:T(8,128)(2,1)} %refs_0_, bf16[1,12,448,512]{3,2,1,0:T(8,128)(2,1)} %cot_ref.5, ...), custom_call_target="tpu_custom_call" | custom-call | flops 528482304 | bytes 6488064 | tf_op jit(solution)/shard_map/lon_back_1/pallas_call | solution.py:537
  685.4 1.5 collective-permute-start.8
  691.5 10.0 %finish.1 = bf16[1,12,448,512]{3,2,1,0:T(8,128)(2,1)} custom-call(bf16[1,12,448,512]{3,2,1,0:T(8,128)(2,1)} %refs_0_, f32[12,2,448]{2,1,0:T(2,128)} %pad_maximum_fusion.4.stat_ref.refs_1_, f32[12,2,448]{2,1,0:T(2,128)} %add.37.refs_2_, f32[12,448,384]{2,1,0:T(8,128)} %get-tuple-element.36.refs_3_, f32[12,448,128]{2,1,0:T(8,128)} %get-tuple-element.37.refs_4_), custom_call_target="tpu_custom_call" | custom-call | flops 27525120 | bytes 27525120 | tf_op jit(solution)/shard_map/finish/pallas_call | solution.py:562
  (70 shorter events, 16.2 us)
Async XLA Ops:
  9.4 176.4 %all-to-all-start.1 = ((f32[16,4,12,24,128]{4,3,2,1,0:T(8,128)}), f32[16,4,12,24,128]{4,3,2,1,0:T(8,128)}, u32[]{:S(2)}, u32[]{:S(2)}) async-start(f32[16,4,12,24,128]{4,3,2,1,0:T(8,128)} %cot_lon.1), calls=%async_computation.1 | async-start | bytes 18874368 | tf_op jit(solution)/shard_map/all_to_all | solution.py:386
  185.8 200.7 %copy-start.3 = (bf16[2,512,128]{2,1,0:T(8,128)(2,1)S(1)}, bf16[2,512,128]{2,1,0:T(8,128)(2,1)}, u32[]{:S(2)}) copy-start(bf16[2,512,128]{2,1,0:T(8,128)(2,1)} %param.19) | copy-start | bytes 786436
  381.9 4.9 copy-start.4
  381.9 11.3 %copy-start.6 = (f32[2,512]{1,0:T(2,128)S(1)}, f32[2,512]{1,0:T(2,128)}, u32[]{:S(2)}) copy-start(f32[2,512]{1,0:T(2,128)} %param.22) | copy-start | bytes 12292
  381.9 11.3 %copy-start.7 = (f32[2,512]{1,0:T(2,128)S(1)}, f32[2,512]{1,0:T(2,128)}, u32[]{:S(2)}) copy-start(f32[2,512]{1,0:T(2,128)} %param.20) | copy-start | bytes 12292
  381.9 11.9 %copy-start.8 = (f32[512]{0:T(512)S(1)}, f32[512]{0:T(512)}, u32[]{:S(2)}) copy-start(f32[512]{0:T(512)} %param.18) | copy-start | bytes 6148
  381.9 56.3 %all-to-all-start = ((f32[16,1,12,24,128]{4,3,2,1,0:T(8,128)}), f32[16,1,12,24,128]{4,3,2,1,0:T(8,128)S(1)}, u32[]{:S(2)}, u32[]{:S(2)}) async-start(f32[16,1,12,24,128]{4,3,2,1,0:T(8,128)} %get-tuple-element.24), calls=%async_computation | async-start | bytes 4718592 | tf_op jit(solution)/shard_map/all_to_all | solution.py:386
  438.2 1.4 copy-start.2
  439.6 184.6 %all-to-all-start.4 = ((f32[16,3,12,24,128]{4,3,2,1,0:T(8,128)}), f32[16,3,12,24,128]{4,3,2,1,0:T(8,128)}, u32[]{:S(2)}, u32[]{:S(2)}) async-start(f32[16,3,12,24,128]{4,3,2,1,0:T(8,128)} %bitcast.45), calls=%async_computation.4 | async-start | bytes 14155776 | tf_op jit(solution)/shard_map/all_to_all | solution.py:386
  446.0 17.0 %copy-start.1 = (f32[3,520,128]{2,1,0:T(8,128)S(1)}, f32[3,520,128]{2,1,0:T(8,128)}, u32[]{:S(2)}) copy-start(f32[3,520,128]{2,1,0:T(8,128)} %get-tuple-element.30) | copy-start | bytes 2396164
  464.0 2.0 collective-permute-start
  467.1 26.8 %collective-permute-start.1 = (f32[544,128]{1,0:T(8,128)S(1)}, f32[544,128]{1,0:T(8,128)S(1)}, u32[]{:S(2)}, u32[]{:S(2)}) collective-permute-start(f32[544,128]{1,0:T(8,128)S(1)} %slice_select_fusion.1), channel_id=1, source_target_pairs={{0,2},{1,3},{2,0},{3,1},{4,6},{5,7},{6,4},{7,5},{8,10},{9,11},{10,... | collective-permute-start | bytes 835592 | tf_op jit(solution)/shard_map/ppermute | solution.py:314
  494.0 69.9 %collective-permute-start.2 = (f32[272,128]{1,0:T(8,128)S(1)}, f32[272,128]{1,0:T(8,128)S(1)}, u32[]{:S(2)}, u32[]{:S(2)}) collective-permute-start(f32[272,128]{1,0:T(8,128)S(1)} %slice_select_fusion.2), channel_id=1, source_target_pairs={{0,4},{1,5},{2,6},{3,7},{4,0},{5,1},{6,2},{7,3},{8,12},{9,13},{10,... | collective-permute-start | bytes 417800 | tf_op jit(solution)/shard_map/ppermute | solution.py:314
  564.0 40.8 %collective-permute-start.3 = (f32[136,128]{1,0:T(8,128)S(1)}, f32[136,128]{1,0:T(8,128)S(1)}, u32[]{:S(2)}, u32[]{:S(2)}) collective-permute-start(f32[136,128]{1,0:T(8,128)S(1)} %slice_select_fusion.3), channel_id=1, source_target_pairs={{0,8},{1,9},{2,10},{3,11},{4,12},{5,13},{6,14},{7,15},{8,0},{9,1},... | collective-permute-start | bytes 208904 | tf_op jit(solution)/shard_map/ppermute | solution.py:314
  604.8 5.3 collective-permute-start.4
  610.1 5.1 collective-permute-start.5
  615.3 6.6 collective-permute-start.6
  622.0 2.0 collective-permute-start.7
  624.2 51.4 %all-to-all-start.3 = ((f32[16,1,12,24,128]{4,3,2,1,0:T(8,128)}), f32[16,1,12,24,128]{4,3,2,1,0:T(8,128)S(1)}, u32[]{:S(2)}, u32[]{:S(2)}) async-start(f32[16,1,12,24,128]{4,3,2,1,0:T(8,128)} %bitcast.51), calls=%async_computation.3 | async-start | bytes 4718592 | tf_op jit(solution)/shard_map/all_to_all | solution.py:386
  675.5 1.4 copy-start
  676.9 9.9 %copy-start.5 = (f32[512]{0:T(512)S(1)}, f32[512]{0:T(512)}, u32[]{:S(2)}) copy-start(f32[512]{0:T(512)} %param.17) | copy-start | bytes 6148
  685.4 4.6 collective-permute-start.8

commit v3 on v2

--- a/solution.py
+++ b/solution.py
@@ -280,10 +280,7 @@
             out_ref[r, :, b * BS : (b + 1) * BS] = cot + rstd * grad
             grads = grads + grad
             products = products + grad * ((values - mean) * rstd)
-        both = []
-        for values in (grads, products):
-            high, low = split(values)
-            both.append((dot_cols(ones, high) + dot_cols(ones, low))[0:1])
+        both = [dot_cols(ones, values.astype(BF16))[0:1] for values in (grads, products)]
         sums = jnp.concatenate(both, 0)
         if carry_in:
             sums = sums + before_ref[r]
@@ -322,18 +319,41 @@
     return piece
 
 
-def sum_halving(piece, axis):
+def scatter_sum(piece, axis):
     size = lax.axis_size(axis)
     index = lax.axis_index(axis)
-    bits = [1 << i for i in range(size.bit_length() - 1)]
-    for bit in bits:
+    low_bits = (size.bit_length() - 1) // 2
+    for i in range(low_bits):
         half = piece.shape[0] // 2
         low, high = piece[:half], piece[half:]
-        upper = (index & bit) != 0
-        piece = jnp.where(upper, high, low) + xor_permute(jnp.where(upper, low, high), axis, bit)
-    for bit in reversed(bits):
-        other = xor_permute(piece, axis, bit)
-        upper = (index & bit) != 0
+        upper = (index & (1 << i)) != 0
+        piece = jnp.where(upper, high, low) + xor_permute(
+            jnp.where(upper, low, high), axis, 1 << i
+        )
+    far = size >> low_bits
+    parts = piece.reshape(far, -1, piece.shape[-1])
+    place = index >> low_bits
+    total = lax.dynamic_index_in_dim(parts, place, 0, False)
+    for d in range(1, far):
+        part = lax.dynamic_index_in_dim(parts, place ^ d, 0, False)
+        total = total + xor_permute(part, axis, d << low_bits)
+    return total
+
+
+def gather_sum(total, axis):
+    size = lax.axis_size(axis)
+    index = lax.axis_index(axis)
+    low_bits = (size.bit_length() - 1) // 2
+    far = size >> low_bits
+    place = index >> low_bits
+    parts = [total] + [xor_permute(total, axis, d << low_bits) for d in range(1, far)]
+    parts = jnp.stack(parts)
+    piece = jnp.concatenate(
+        [lax.dynamic_index_in_dim(parts, place ^ d, 0, False) for d in range(far)], 0
+    )
+    for i in reversed(range(low_bits)):
+        other = xor_permute(piece, axis, 1 << i)
+        upper = (index & (1 << i)) != 0
         piece = jnp.concatenate(
             [jnp.where(upper, other, piece), jnp.where(upper, piece, other)], 0
         )
@@ -519,8 +539,7 @@
     tail = -(blocks * param_rows) % (unit * blocks)
     flat = jnp.concatenate([m[1].reshape(-1, BS) for m in mixed], 0)
     flat = jnp.pad(flat, ((0, tail), (0, 0)))
-    param_sums = sum_halving(flat, "row")[: blocks * param_rows]
-    param_sums = param_sums.reshape(blocks, param_rows, BS)
+    param_part = scatter_sum(flat, "row")
 
     grads = []
     sums = None
@@ -529,7 +548,7 @@
         piece = mixed[index][0].reshape(owners, count, rows, padded, BS)
         carry_in = sums is not None
         if index == len(chunks) - 1 and carry_in:
-            piece, param_sums = lax.optimization_barrier((piece, param_sums))
+            piece, param_part = lax.optimization_barrier((piece, param_part))
         piece = exchange(piece)
         in_spec = pl.BlockSpec(
             (1, many, width, count * BS), lambda h, at=start // count: (0, h, 0, at)
@@ -571,6 +590,8 @@
         name="finish",
     )(inputs, stats, sum_small(sums, "chan"), *grads)
 
+    param_sums = gather_sum(param_part, "row")[: blocks * param_rows]
+    param_sums = param_sums.reshape(blocks, param_rows, BS)
     spec_scale = 1.0 / math.sqrt(batch * height * K)
     dw = param_sums[:, : 4 * BS].reshape(blocks, 2, 2, BS, BS).transpose(1, 2, 0, 3, 4) * spec_scale
     db = param_sums[:, 4 * BS : 4 * BS + 4].reshape(blocks, 2, 2, BS).transpose(1, 2, 0, 3)

time: 709 us -> 720 us (1.016)
  waiting for transfers between devices: 310 us -> 326 us
    ppermute x9 -> x11, waiting for transfers between devices: 151 us -> 199 us  [xor_permute(): return lax.ppermute(piece, axis, [(i, i ^ bit) for i in range(size)])]
    all_to_all x4, waiting for transfers between devices: 160 us -> 128 us  [exchange(): return lax.all_to_all(piece, 'row', split_axis=0, concat_axis=0, tiled=True)]
  transfers between devices with their start and end apart: 13 -> 15, of which waited for: 11 -> 10; matrix products, arithmetic and copies ran while one was open for 3% -> 3% of each run, Pallas kernels for 13% -> 13%
where the time goes in v3:
time: 720 us; the launch traced here: 719 us
  waiting for transfers between devices  326 us (45%)
  blocking collectives  212 us (29%)
  Pallas kernels  116 us (16%)
  starting transfers between devices  36.6 us (5%)
  other arithmetic  16.2 us (2%)
  local copies, waits for them, and re-layouts  10.7 us (1%)
    ppermute x11, waiting for transfers between devices, xor_permute(): return lax.ppermute(piece, axis, [(i, i ^ bit) for i in range(size)])  199 us
    all_to_all x1, blocking collectives, exchange(): return lax.all_to_all(piece, 'row', split_axis=0, concat_axis=0, tiled=True)  196 us
    all_to_all x4, waiting for transfers between devices, exchange(): return lax.all_to_all(piece, 'row', split_axis=0, concat_axis=0, tiled=True)  128 us
    pallas_call x2, Pallas kernels, mix(): pl.pallas_call(functools.partial(mixer_kernel, own, group), grid=(count,)...  60.9 us
    all_to_all x4, starting transfers between devices, exchange(): return lax.all_to_all(piece, 'row', split_axis=0, concat_axis=0, tiled=True)  22.3 us
    pallas_call x2, Pallas kernels, on_device(): pl.pallas_call(functools.partial(lon_back_kernel, start, carry_in), grid=...  19.8 us
    pallas_call x1, Pallas kernels, on_device(): pl.pallas_call(input_lon_kernel, grid=(rows // few,), in_specs=[whole((2...  16.8 us
  transfers between devices with their start and end apart: 15, of which 10 were waited for; matrix products, arithmetic and copies ran while one was open for 3% of the time, Pallas kernels for 13%

profile of v3, /device:TPU:0, one launch (start us, length us, event | category | flops | bytes accessed | tf_op | source)
XLA Modules:
  0.0 718.7 jit_solution(503634836933592010)
XLA Ops:
  0.6 8.7 %cot_lon.1 = f32[16,4,12,24,128]{4,3,2,1,0:T(8,128)} custom-call(bf16[384,448]{1,0:T(8,128)(2,1)} %constant.63.clone.table_ref, bf16[1,12,448,512]{3,2,1,0:T(8,128)(2,1)} %cot_ref.5), custom_call_target="tpu_custom_call" | custom-call | flops 2113929216 | bytes 14942208 | tf_op jit(solution)/shard_map/cot_lon/pallas_call | solution.py:427
  9.3 7.4 %all-to-all-start.1 = ((f32[16,4,12,24,128]{4,3,2,1,0:T(8,128)}), f32[16,4,12,24,128]{4,3,2,1,0:T(8,128)}, u32[]{:S(2)}, u32[]{:S(2)}) async-start(f32[16,4,12,24,128]{4,3,2,1,0:T(8,128)} %cot_lon.1), calls=%async_computation.1 | async-start | bytes 18874368 | tf_op jit(solution)/shard_map/all_to_all | solution.py:406
  16.8 3.5 convert_reduce_fusion
  20.2 8.3 %psum.14 = f32[1,12,448]{2,0,1:T(1,128)S(1)} all-reduce(f32[1,12,448]{2,0,1:T(1,128)S(1)} %reduce_sum.23), channel_id=1, replica_groups=mesh['chan'=2,'row'=16] {'chan'}, use_global_device_ids=true, to_apply=%region_1.0 | all-reduce | flops 5376 | bytes 43008 | tf_op jit(solution)/shard_map/psum | solution.py:441
  28.6 4.6 fusion.1
  33.2 7.3 %psum.15 = f32[1,12,448]{2,0,1:T(1,128)S(1)} all-reduce(f32[1,12,448]{2,0,1:T(1,128)S(1)} %reduce_sum.25), channel_id=1, replica_groups=mesh['chan'=2,'row'=16] {'chan'}, use_global_device_ids=true, to_apply=%region_3.0 | all-reduce | flops 5376 | bytes 43008 | tf_op jit(solution)/shard_map/psum | solution.py:443
  41.3 16.8 %input_lon.1 = (f32[16,3,12,24,128]{4,3,2,1,0:T(8,128)}, f32[16,1,12,24,128]{4,3,2,1,0:T(8,128)}) custom-call(bf16[768,448]{1,0:T(8,128)(2,1)} %constant.64.clone.table_ref, bf16[1,12,448,512]{3,2,1,0:T(8,128)(2,1)} %refs_0_, f32[12,2,448]{2,1,0:T(2,128)} %pad_maximum_fusion.4.stat_ref.refs_1_, f32[1,512]{1,0:T(1,128)} %bitcast.94), custom_call_target="tpu_custom_call" | custom-call | flops 6341787648 | bytes 14942208 | tf_op jit(solution)/shard_map/input_lon/pallas_call | solution.py:446
  58.1 127.6 %all-to-all-done.1 = f32[16,4,12,24,128]{4,3,2,1,0:T(8,128)} async-done(((f32[16,4,12,24,128]{4,3,2,1,0:T(8,128)}), f32[16,4,12,24,128]{4,3,2,1,0:T(8,128)}, u32[]{:S(2)}, u32[]{:S(2)}) %all-to-all-start.1) | async-done | bytes 9437216 | tf_op jit(solution)/shard_map/all_to_all | solution.py:406
  185.7 196.0 %all_to_all.25 = f32[16,3,12,24,128]{4,3,2,1,0:T(8,128)} all-to-all(f32[16,3,12,24,128]{4,3,2,1,0:T(8,128)} %get-tuple-element.29), channel_id=1, replica_groups=mesh['chan'=2,'row'=16] {'row'}, dimensions={0} | all-to-all | bytes 14155776 | tf_op jit(solution)/shard_map/all_to_all | solution.py:406
  381.8 4.7 all-to-all-start
  387.8 2.2 fusion.6
  390.0 2.0 copy.55.w_one_ref
  394.3 43.9 %mixer_0.1 = (f32[16,3,288,128]{3,2,1,0:T(8,128)}, f32[3,520,128]{2,1,0:T(8,128)}) custom-call(bf16[384,384]{1,0:T(8,128)(2,1)} %constant.65.clone.fwd_high_ref, bf16[384,384]{1,0:T(8,128)(2,1)} %constant.66.clone.fwd_low_ref, bf16[384,384]{1,0:T(8,128)(2,1)} %constant.67.clone.inv_high_ref, bf16[384,384]{1,0:T(8,128)(2,1)} %constant.68.clone.inv_low_ref, ...), custom_call_target="tpu_custom_call" | custom-call | flops 17666408448 | bytes 21233664 | tf_op jit(solution)/shard_map/mixer_0/pallas_call | solution.py:488
  439.6 6.3 all-to-all-start.4
  445.9 17.0 %mixer_1.1 = (f32[16,1,288,128]{3,2,1,0:T(8,128)}, f32[1,520,128]{2,1,0:T(8,128)}) custom-call(bf16[384,384]{1,0:T(8,128)(2,1)} %constant.65.clone.fwd_high_ref, bf16[384,384]{1,0:T(8,128)(2,1)} %constant.66.clone.fwd_low_ref, bf16[384,384]{1,0:T(8,128)(2,1)} %constant.67.clone.inv_high_ref, bf16[384,384]{1,0:T(8,128)(2,1)} %constant.68.clone.inv_low_ref, ...), custom_call_target="tpu_custom_call" | custom-call | flops 5888802816 | bytes 7077888 | tf_op jit(solution)/shard_map/mixer_1/pallas_call | solution.py:488
  464.3 1.6 collective-permute-done
  467.0 1.9 collective-permute-start.1
  468.9 24.9 %collective-permute-done.1 = f32[544,128]{1,0:T(8,128)S(1)} collective-permute-done((f32[544,128]{1,0:T(8,128)S(1)}, f32[544,128]{1,0:T(8,128)S(1)}, u32[]{:S(2)}, u32[]{:S(2)}) %collective-permute-start.1) | collective-permute-done | bytes 278560 | tf_op jit(solution)/shard_map/ppermute | solution.py:311
  494.0 3.3 collective-permute-start.3
  498.4 64.1 %collective-permute-done.2 = f32[136,128]{1,0:T(8,128)S(1)} collective-permute-done((f32[136,128]{1,0:T(8,128)S(1)}, f32[136,128]{1,0:T(8,128)S(1)}, u32[]{:S(2)}, u32[]{:S(2)}) %collective-permute-start.2) | collective-permute-done | bytes 69664 | tf_op jit(solution)/shard_map/ppermute | solution.py:311
  562.5 44.1 %collective-permute-done.3 = f32[136,128]{1,0:T(8,128)S(1)} collective-permute-done((f32[136,128]{1,0:T(8,128)S(1)}, f32[136,128]{1,0:T(8,128)S(1)}, u32[]{:S(2)}, u32[]{:S(2)}) %collective-permute-start.3) | collective-permute-done | bytes 69664 | tf_op jit(solution)/shard_map/ppermute | solution.py:311
  606.6 3.9 all-to-all-start.3
  610.6 1.9 collective-permute-start.6
  612.5 2.4 collective-permute-start.7
  615.0 36.3 %collective-permute-done.6 = f32[136,128]{1,0:T(8,128)S(1)} collective-permute-done((f32[136,128]{1,0:T(8,128)S(1)}, f32[136,128]{1,0:T(8,128)S(1)}, u32[]{:S(2)}, u32[]{:S(2)}) %collective-permute-start.6) | collective-permute-done | bytes 69664 | tf_op jit(solution)/shard_map/ppermute | solution.py:311
  651.4 18.8 %collective-permute-done.7 = f32[136,128]{1,0:T(8,128)S(1)} collective-permute-done((f32[136,128]{1,0:T(8,128)S(1)}, f32[136,128]{1,0:T(8,128)S(1)}, u32[]{:S(2)}, u32[]{:S(2)}) %collective-permute-start.7) | collective-permute-done | bytes 69664 | tf_op jit(solution)/shard_map/ppermute | solution.py:311
  670.3 1.6 collective-permute-start.9
  671.9 6.2 collective-permute-done.9
  678.3 1.9 collective-permute-done.10
  681.7 12.4 %lon_back_0.1 = (f32[12,448,384]{2,1,0:T(8,128)}, f32[12,2,448]{2,1,0:T(2,128)}) custom-call(bf16[448,384]{1,0:T(8,128)(2,1)} %constant.69.clone.table_ref, f32[16,3,12,24,128]{4,3,2,1,0:T(8,128)} %all-to-all-done.4.grad_ref, bf16[1,12,448,512]{3,2,1,0:T(8,128)(2,1)} %refs_0_, bf16[1,12,448,512]{3,2,1,0:T(8,128)(2,1)} %cot_ref.5, ...), custom_call_target="tpu_custom_call" | custom-call | flops 1585446912 | bytes 19464192 | tf_op jit(solution)/shard_map/lon_back_0/pallas_call | solution.py:556
  695.6 7.4 %lon_back_1.1 = (f32[12,448,128]{2,1,0:T(8,128)}, f32[12,2,448]{2,1,0:T(2,128)}) custom-call(bf16[448,384]{1,0:T(8,128)(2,1)} %constant.69.clone.table_ref, f32[16,1,12,24,128]{4,3,2,1,0:T(8,128)} %copy-done, bf16[1,12,448,512]{3,2,1,0:T(8,128)(2,1)} %refs_0_, bf16[1,12,448,512]{3,2,1,0:T(8,128)(2,1)} %cot_ref.5, ...), custom_call_target="tpu_custom_call" | custom-call | flops 528482304 | bytes 6488064 | tf_op jit(solution)/shard_map/lon_back_1/pallas_call | solution.py:556
  708.7 10.0 %finish.1 = bf16[1,12,448,512]{3,2,1,0:T(8,128)(2,1)} custom-call(bf16[1,12,448,512]{3,2,1,0:T(8,128)(2,1)} %refs_0_, f32[12,2,448]{2,1,0:T(2,128)} %pad_maximum_fusion.4.stat_ref.refs_1_, f32[12,2,448]{2,1,0:T(2,128)} %add.62.refs_2_, f32[12,448,384]{2,1,0:T(8,128)} %get-tuple-element.36.refs_3_, f32[12,448,128]{2,1,0:T(8,128)} %get-tuple-element.37.refs_4_), custom_call_target="tpu_custom_call" | custom-call | flops 27525120 | bytes 27525120 | tf_op jit(solution)/shard_map/finish/pallas_call | solution.py:581
  (71 shorter events, 18.5 us)
Async XLA Ops:
  9.3 176.4 %all-to-all-start.1 = ((f32[16,4,12,24,128]{4,3,2,1,0:T(8,128)}), f32[16,4,12,24,128]{4,3,2,1,0:T(8,128)}, u32[]{:S(2)}, u32[]{:S(2)}) async-start(f32[16,4,12,24,128]{4,3,2,1,0:T(8,128)} %cot_lon.1), calls=%async_computation.1 | async-start | bytes 18874368 | tf_op jit(solution)/shard_map/all_to_all | solution.py:406
  185.7 200.7 %copy-start.3 = (bf16[2,512,128]{2,1,0:T(8,128)(2,1)S(1)}, bf16[2,512,128]{2,1,0:T(8,128)(2,1)}, u32[]{:S(2)}) copy-start(bf16[2,512,128]{2,1,0:T(8,128)(2,1)} %param.19) | copy-start | bytes 786436
  381.8 4.9 copy-start.4
  381.8 11.3 %copy-start.6 = (f32[2,512]{1,0:T(2,128)S(1)}, f32[2,512]{1,0:T(2,128)}, u32[]{:S(2)}) copy-start(f32[2,512]{1,0:T(2,128)} %param.22) | copy-start | bytes 12292
  381.8 11.3 %copy-start.7 = (f32[2,512]{1,0:T(2,128)S(1)}, f32[2,512]{1,0:T(2,128)}, u32[]{:S(2)}) copy-start(f32[2,512]{1,0:T(2,128)} %param.20) | copy-start | bytes 12292
  381.8 11.9 %copy-start.8 = (f32[512]{0:T(512)S(1)}, f32[512]{0:T(512)}, u32[]{:S(2)}) copy-start(f32[512]{0:T(512)} %param.18) | copy-start | bytes 6148
  381.8 56.4 %all-to-all-start = ((f32[16,1,12,24,128]{4,3,2,1,0:T(8,128)}), f32[16,1,12,24,128]{4,3,2,1,0:T(8,128)S(1)}, u32[]{:S(2)}, u32[]{:S(2)}) async-start(f32[16,1,12,24,128]{4,3,2,1,0:T(8,128)} %get-tuple-element.24), calls=%async_computation | async-start | bytes 4718592 | tf_op jit(solution)/shard_map/all_to_all | solution.py:406
  438.2 1.4 copy-start.2
  439.6 167.0 %all-to-all-start.4 = ((f32[16,3,12,24,128]{4,3,2,1,0:T(8,128)}), f32[16,3,12,24,128]{4,3,2,1,0:T(8,128)}, u32[]{:S(2)}, u32[]{:S(2)}) async-start(f32[16,3,12,24,128]{4,3,2,1,0:T(8,128)} %bitcast.70), calls=%async_computation.4 | async-start | bytes 14155776 | tf_op jit(solution)/shard_map/all_to_all | solution.py:406
  445.9 17.0 %copy-start.1 = (f32[3,520,128]{2,1,0:T(8,128)S(1)}, f32[3,520,128]{2,1,0:T(8,128)}, u32[]{:S(2)}) copy-start(f32[3,520,128]{2,1,0:T(8,128)} %get-tuple-element.30) | copy-start | bytes 2396164
  463.9 2.0 collective-permute-start
  467.0 26.8 %collective-permute-start.1 = (f32[544,128]{1,0:T(8,128)S(1)}, f32[544,128]{1,0:T(8,128)S(1)}, u32[]{:S(2)}, u32[]{:S(2)}) collective-permute-start(f32[544,128]{1,0:T(8,128)S(1)} %slice_select_fusion.1), channel_id=1, source_target_pairs={{0,2},{1,3},{2,0},{3,1},{4,6},{5,7},{6,4},{7,5},{8,10},{9,11},{10,... | collective-permute-start | bytes 835592 | tf_op jit(solution)/shard_map/ppermute | solution.py:311
  493.9 68.6 %collective-permute-start.2 = (f32[136,128]{1,0:T(8,128)S(1)}, f32[136,128]{1,0:T(8,128)S(1)}, u32[]{:S(2)}, u32[]{:S(2)}) collective-permute-start(f32[136,128]{1,0:T(8,128)S(1)} %get-tuple-element.55), channel_id=1, source_target_pairs={{0,4},{1,5},{2,6},{3,7},{4,0},{5,1},{6,2},{7,3},{8,12},{9,13},{10,... | collective-permute-start | bytes 208904 | tf_op jit(solution)/shard_map/ppermute | solution.py:311
  494.0 112.6 %collective-permute-start.3 = (f32[136,128]{1,0:T(8,128)S(1)}, f32[136,128]{1,0:T(8,128)S(1)}, u32[]{:S(2)}, u32[]{:S(2)}) collective-permute-start(f32[136,128]{1,0:T(8,128)S(1)} %get-tuple-element.57), channel_id=1, source_target_pairs={{0,8},{1,9},{2,10},{3,11},{4,12},{5,13},{6,14},{7,15},{8,0},{9,1},... | collective-permute-start | bytes 208904 | tf_op jit(solution)/shard_map/ppermute | solution.py:311
  497.3 109.3 %collective-permute-start.4 = (f32[136,128]{1,0:T(8,128)S(1)}, f32[136,128]{1,0:T(8,128)S(1)}, u32[]{:S(2)}, u32[]{:S(2)}) collective-permute-start(f32[136,128]{1,0:T(8,128)S(1)} %get-tuple-element.56), channel_id=1, source_target_pairs={{0,12},{1,13},{2,14},{3,15},{4,8},{5,9},{6,10},{7,11},{8,4},{9,5},... | collective-permute-start | bytes 208904 | tf_op jit(solution)/shard_map/ppermute | solution.py:311
  606.6 87.5 %all-to-all-start.3 = ((f32[16,1,12,24,128]{4,3,2,1,0:T(8,128)}), f32[16,1,12,24,128]{4,3,2,1,0:T(8,128)S(1)}, u32[]{:S(2)}, u32[]{:S(2)}) async-start(f32[16,1,12,24,128]{4,3,2,1,0:T(8,128)} %bitcast.76), calls=%async_computation.3 | async-start | bytes 4718592 | tf_op jit(solution)/shard_map/all_to_all | solution.py:406
  610.6 40.8 %collective-permute-start.6 = (f32[136,128]{1,0:T(8,128)S(1)}, f32[136,128]{1,0:T(8,128)S(1)}, u32[]{:S(2)}, u32[]{:S(2)}) collective-permute-start(f32[136,128]{1,0:T(8,128)S(1)} %fusion.4), channel_id=1, source_target_pairs={{0,4},{1,5},{2,6},{3,7},{4,0},{5,1},{6,2},{7,3},{8,12},{9,13},{10,... | collective-permute-start | bytes 208904 | tf_op jit(solution)/shard_map/ppermute | solution.py:311
  612.5 57.7 %collective-permute-start.7 = (f32[136,128]{1,0:T(8,128)S(1)}, f32[136,128]{1,0:T(8,128)S(1)}, u32[]{:S(2)}, u32[]{:S(2)}) collective-permute-start(f32[136,128]{1,0:T(8,128)S(1)} %fusion.4), channel_id=1, source_target_pairs={{0,8},{1,9},{2,10},{3,11},{4,12},{5,13},{6,14},{7,15},{8,0},{9,1},... | collective-permute-start | bytes 208904 | tf_op jit(solution)/shard_map/ppermute | solution.py:311
  614.9 55.3 %collective-permute-start.8 = (f32[136,128]{1,0:T(8,128)S(1)}, f32[136,128]{1,0:T(8,128)S(1)}, u32[]{:S(2)}, u32[]{:S(2)}) collective-permute-start(f32[136,128]{1,0:T(8,128)S(1)} %fusion.4), channel_id=1, source_target_pairs={{0,12},{1,13},{2,14},{3,15},{4,8},{5,9},{6,10},{7,11},{8,4},{9,5},... | collective-permute-start | bytes 208904 | tf_op jit(solution)/shard_map/ppermute | solution.py:311
  670.3 7.8 %collective-permute-start.9 = (f32[544,128]{1,0:T(8,128)S(1)}, f32[544,128]{1,0:T(8,128)S(1)}, u32[]{:S(2)}, u32[]{:S(2)}) collective-permute-start(f32[544,128]{1,0:T(8,128)S(1)} %pad_maximum_fusion.3), channel_id=1, source_target_pairs={{0,2},{1,3},{2,0},{3,1},{4,6},{5,7},{6,4},{7,5},{8,10},{9,11},{10,... | collective-permute-start | bytes 835592 | tf_op jit(solution)/shard_map/ppermute | solution.py:311
  678.2 2.0 collective-permute-start.10
  694.2 1.4 copy-start
  695.6 8.9 %copy-start.5 = (f32[512]{0:T(512)S(1)}, f32[512]{0:T(512)}, u32[]{:S(2)}) copy-start(f32[512]{0:T(512)} %param.17) | copy-start | bytes 6148
  703.0 4.3 collective-permute-start.5

commit v4 on v3

--- a/solution.py
+++ b/solution.py
@@ -277,7 +277,7 @@
             grad = mixed[:, b * BS : (b + 1) * BS] * gain_ref[:, lanes]
             values = in_ref[0, r, :, b * BS : (b + 1) * BS].astype(F32)
             cot = cot_ref[0, r, :, b * BS : (b + 1) * BS].astype(F32)
-            out_ref[r, :, b * BS : (b + 1) * BS] = cot + rstd * grad
+            out_ref[r, :, b * BS : (b + 1) * BS] = (cot + rstd * grad).astype(BF16)
             grads = grads + grad
             products = products + grad * ((values - mean) * rstd)
         both = [dot_cols(ones, values.astype(BF16))[0:1] for values in (grads, products)]
@@ -288,20 +288,21 @@
 
 
 def finish_kernel(chunks, channels, *refs):
-    in_ref, stat_ref, sums_ref = refs[:3]
-    base_refs = refs[3 : 3 + len(chunks)]
+    in_ref, stat_ref, sums_ref, more_ref = refs[:4]
+    base_refs = refs[4 : 4 + len(chunks)]
     out_ref = refs[-1]
     for r in range(in_ref.shape[1]):
         mean, rstd = stat_ref[r, 0:1], stat_ref[r, 1:2]
-        slope = rstd * rstd * (sums_ref[r, 1:2] / channels)
-        level = rstd * (sums_ref[r, 0:1] / channels) - mean * slope
+        sums = (sums_ref[r] + more_ref[r]) / channels
+        slope = rstd * rstd * sums[1:2]
+        level = rstd * sums[0:1] - mean * slope
         level, slope = columns_of(jnp.concatenate([level, slope], 0))
         at = 0
         for base_ref, blocks in zip(base_refs, chunks):
             for b in range(blocks):
                 lanes = slice(at * BS, (at + 1) * BS)
                 values = in_ref[0, r, :, lanes].astype(F32)
-                base = base_ref[r, :, b * BS : (b + 1) * BS]
+                base = base_ref[r, :, b * BS : (b + 1) * BS].astype(F32)
                 out_ref[0, r, :, lanes] = (base - level - slope * values).astype(BF16)
                 at += 1
 
@@ -311,53 +312,58 @@
     return lax.ppermute(piece, axis, [(i, i ^ bit) for i in range(size)])
 
 
-def sum_small(piece, axis):
+def pair_small(piece, axis):
+    other = jnp.zeros_like(piece)
     bit = 1
     while bit < lax.axis_size(axis):
-        piece = piece + xor_permute(piece, axis, bit)
+        piece = piece + other if bit > 1 else piece
+        other = xor_permute(piece, axis, bit)
         bit *= 2
-    return piece
-
-
-def scatter_sum(piece, axis):
-    size = lax.axis_size(axis)
+    return piece, other
+
+
+def halve(piece, axis):
     index = lax.axis_index(axis)
-    low_bits = (size.bit_length() - 1) // 2
-    for i in range(low_bits):
+    for i in range(low_bits(axis)):
         half = piece.shape[0] // 2
         low, high = piece[:half], piece[half:]
         upper = (index & (1 << i)) != 0
         piece = jnp.where(upper, high, low) + xor_permute(
             jnp.where(upper, low, high), axis, 1 << i
         )
-    far = size >> low_bits
+    return piece
+
+
+def low_bits(axis):
+    return (lax.axis_size(axis).bit_length() - 1) // 2
+
+
+def scatter_far(piece, axis):
+    low = low_bits(axis)
+    far = lax.axis_size(axis) >> low
     parts = piece.reshape(far, -1, piece.shape[-1])
-    place = index >> low_bits
+    place = lax.axis_index(axis) >> low
     total = lax.dynamic_index_in_dim(parts, place, 0, False)
-    for d in range(1, far):
-        part = lax.dynamic_index_in_dim(parts, place ^ d, 0, False)
-        total = total + xor_permute(part, axis, d << low_bits)
-    return total
-
-
-def gather_sum(total, axis):
-    size = lax.axis_size(axis)
-    index = lax.axis_index(axis)
-    low_bits = (size.bit_length() - 1) // 2
-    far = size >> low_bits
-    place = index >> low_bits
-    parts = [total] + [xor_permute(total, axis, d << low_bits) for d in range(1, far)]
+    others = [lax.dynamic_index_in_dim(parts, place ^ d, 0, False) for d in range(1, far)]
+    others = [xor_permute(part, axis, d << low) for d, part in enumerate(others, 1)]
+    return total + others[0], others[1:]
+
+
+def gather_far(total, axis):
+    low = low_bits(axis)
+    far = lax.axis_size(axis) >> low
+    place = lax.axis_index(axis) >> low
+    parts = [total] + [xor_permute(total, axis, d << low) for d in range(1, far)]
     parts = jnp.stack(parts)
-    piece = jnp.concatenate(
+    return jnp.concatenate(
         [lax.dynamic_index_in_dim(parts, place ^ d, 0, False) for d in range(far)], 0
     )
-    for i in reversed(range(low_bits)):
-        other = xor_permute(piece, axis, 1 << i)
-        upper = (index & (1 << i)) != 0
-        piece = jnp.concatenate(
-            [jnp.where(upper, other, piece), jnp.where(upper, piece, other)], 0
-        )
-    return piece
+
+
+def double(piece, axis, bit):
+    other = xor_permute(piece, axis, bit)
+    upper = (lax.axis_index(axis) & bit) != 0
+    return jnp.concatenate([jnp.where(upper, other, piece), jnp.where(upper, piece, other)], 0)
 
 
 def divisor(count, limit):
@@ -453,8 +459,6 @@
         cost_estimate=cost(3 * lon_flops, rows * local * (2 * width + 4 * tall)),
         name="input_lon",
     )(lon_both, inputs, stats, gain)
-    first_piece, cot_spec = lax.optimization_barrier((input_lon[0], cot_spec))
-    input_lon = [first_piece, *input_lon[1:]]
 
     def square(weight):
         re, im = weight.reshape(2, blocks, BS, BS)
@@ -473,8 +477,11 @@
     shift = jnp.concatenate([shift, jnp.zeros_like(shift)], 2)
     shift = jnp.concatenate([shift, jnp.full_like(shift, is_origin)], 1)
 
+    weights = (w_one, w_one_t, w_two, w_two_t, bias, shift)
+    first_piece, cot_spec, weights = lax.optimization_barrier((input_lon[0], cot_spec, weights))
+    input_lon = [first_piece, *input_lon[1:]]
+
     span = rows * padded
-    mat = pl.BlockSpec((1, 2 * BS, 2 * BS), lambda b: (b, 0, 0))
 
     def mix(index, x_spec):
         count = chunks[index]
@@ -523,12 +530,7 @@
             fwd_low,
             inv_high,
             inv_low,
-            w_one,
-            w_one_t,
-            w_two,
-            w_two_t,
-            bias,
-            shift,
+            *weights,
             x_spec.reshape(owners, count, span, BS),
             cot_spec.reshape(owners, blocks, span, BS),
         )
@@ -539,7 +541,7 @@
     tail = -(blocks * param_rows) % (unit * blocks)
     flat = jnp.concatenate([m[1].reshape(-1, BS) for m in mixed], 0)
     flat = jnp.pad(flat, ((0, tail), (0, 0)))
-    param_part = scatter_sum(flat, "row")
+    param_part, far_parts = scatter_far(halve(flat, "row"), "row")
 
     grads = []
     sums = None
@@ -549,6 +551,7 @@
         carry_in = sums is not None
         if index == len(chunks) - 1 and carry_in:
             piece, param_part = lax.optimization_barrier((piece, param_part))
+            param_part, sums = lax.optimization_barrier((sum(far_parts, param_part), sums))
         piece = exchange(piece)
         in_spec = pl.BlockSpec(
             (1, many, width, count * BS), lambda h, at=start // count: (0, h, 0, at)
@@ -567,7 +570,7 @@
             + [stat_spec(many)] * carry_in,
             out_specs=[grad_spec(many, count), stat_spec(many)],
             out_shape=[
-                jax.ShapeDtypeStruct((rows, width, count * BS), F32),
+                jax.ShapeDtypeStruct((rows, width, count * BS), BF16),
                 jax.ShapeDtypeStruct((rows, 2, width), F32),
             ],
             compiler_params=params(),
@@ -578,20 +581,27 @@
         )(back, piece, inputs, cotangent, stats, gain, *([sums] * carry_in))
         grads.append(grad)
 
+    if len(chunks) == 1:
+        param_part = sum(far_parts, param_part)
+    param_sums = gather_far(param_part, "row")
+    for i in reversed(range(low_bits("row"))):
+        if i == 0:
+            param_sums, sums = lax.optimization_barrier((param_sums, sums))
+        param_sums = double(param_sums, "row", 1 << i)
+    param_sums = param_sums[: blocks * param_rows].reshape(blocks, param_rows, BS)
+
     input_grad = pl.pallas_call(
         functools.partial(finish_kernel, chunks, total_chan),
         grid=(rows // few,),
-        in_specs=[row_spec(few), stat_spec(few), stat_spec(few)]
+        in_specs=[row_spec(few), stat_spec(few), stat_spec(few), stat_spec(few)]
         + [grad_spec(few, count) for count in chunks],
         out_specs=row_spec(few),
         out_shape=jax.ShapeDtypeStruct(inputs.shape, BF16),
         compiler_params=params(),
         cost_estimate=cost(10 * rows * width * local, rows * width * local * 10),
         name="finish",
-    )(inputs, stats, sum_small(sums, "chan"), *grads)
-
-    param_sums = gather_sum(param_part, "row")[: blocks * param_rows]
-    param_sums = param_sums.reshape(blocks, param_rows, BS)
+    )(inputs, stats, *pair_small(sums, "chan"), *grads)
+
     spec_scale = 1.0 / math.sqrt(batch * height * K)
     dw = param_sums[:, : 4 * BS].reshape(blocks, 2, 2, BS, BS).transpose(1, 2, 0, 3, 4) * spec_scale
     db = param_sums[:, 4 * BS : 4 * BS + 4].reshape(blocks, 2, 2, BS).transpose(1, 2, 0, 3)

time: 720 us -> 714 us (level)
  starting transfers between devices: 36.6 us -> 68.1 us
  waiting for transfers between devices: 326 us -> 295 us
    ppermute x11, waiting for transfers between devices: 199 us -> 159 us  [xor_permute(): return lax.ppermute(piece, axis, [(i, i ^ bit) for i in range(size)])]
    all_to_all x4, starting transfers between devices: 22.3 us -> 54.4 us  [exchange(): return lax.all_to_all(piece, 'row', split_axis=0, concat_axis=0, tiled=True)]
    all_to_all x4, waiting for transfers between devices: 128 us -> 136 us  [exchange(): return lax.all_to_all(piece, 'row', split_axis=0, concat_axis=0, tiled=True)]
  transfers between devices with their start and end apart: 15 -> 15, of which waited for: 10 -> 10; matrix products, arithmetic and copies ran while one was open for 3% -> 2% of each run, Pallas kernels for 13% -> 15%
where the time goes in v4:
time: 714 us; the launch traced here: 713 us
  waiting for transfers between devices  295 us (41%)
  blocking collectives  212 us (30%)
  Pallas kernels  113 us (16%)
  starting transfers between devices  68.1 us (10%)
  other arithmetic  13.8 us (2%)
  local copies, waits for them, and re-layouts  10.7 us (1%)
    all_to_all x1, blocking collectives, exchange(): return lax.all_to_all(piece, 'row', split_axis=0, concat_axis=0, tiled=True)  196 us
    ppermute x11, waiting for transfers between devices, xor_permute(): return lax.ppermute(piece, axis, [(i, i ^ bit) for i in range(size)])  159 us
    all_to_all x4, waiting for transfers between devices, exchange(): return lax.all_to_all(piece, 'row', split_axis=0, concat_axis=0, tiled=True)  136 us
    pallas_call x2, Pallas kernels, mix(): pl.pallas_call(functools.partial(mixer_kernel, own, group), grid=(count,)...  60.8 us
    all_to_all x4, starting transfers between devices, exchange(): return lax.all_to_all(piece, 'row', split_axis=0, concat_axis=0, tiled=True)  54.4 us
    pallas_call x2, Pallas kernels, on_device(): pl.pallas_call(functools.partial(lon_back_kernel, start, carry_in), grid=...  17.9 us
    pallas_call x1, Pallas kernels, on_device(): pl.pallas_call(input_lon_kernel, grid=(rows // few,), in_specs=[whole((2...  16.8 us
  transfers between devices with their start and end apart: 15, of which 10 were waited for; matrix products, arithmetic and copies ran while one was open for 2% of the time, Pallas kernels for 15%

profile of v4, /device:TPU:0, one launch (start us, length us, event | category | flops | bytes accessed | tf_op | source)
XLA Modules:
  0.0 712.9 jit_solution(11241928954459756775)
XLA Ops:
  0.6 8.7 %cot_lon.1 = f32[16,4,12,24,128]{4,3,2,1,0:T(8,128)} custom-call(bf16[384,448]{1,0:T(8,128)(2,1)} %constant.63.clone.table_ref, bf16[1,12,448,512]{3,2,1,0:T(8,128)(2,1)} %cot_ref.5), custom_call_target="tpu_custom_call" | custom-call | flops 2113929216 | bytes 14942208 | tf_op jit(solution)/shard_map/cot_lon/pallas_call | solution.py:433
  9.3 7.4 %all-to-all-start = ((f32[16,4,12,24,128]{4,3,2,1,0:T(8,128)}), f32[16,4,12,24,128]{4,3,2,1,0:T(8,128)}, u32[]{:S(2)}, u32[]{:S(2)}) async-start(f32[16,4,12,24,128]{4,3,2,1,0:T(8,128)} %cot_lon.1), calls=%async_computation | async-start | bytes 18874368 | tf_op jit(solution)/shard_map/all_to_all | solution.py:412
  16.8 3.5 convert_reduce_fusion
  20.4 8.3 %psum.14 = f32[1,12,448]{2,0,1:T(1,128)S(1)} all-reduce(f32[1,12,448]{2,0,1:T(1,128)S(1)} %reduce_sum.23), channel_id=1, replica_groups=mesh['chan'=2,'row'=16] {'chan'}, use_global_device_ids=true, to_apply=%region_1.0 | all-reduce | flops 5376 | bytes 43008 | tf_op jit(solution)/shard_map/psum | solution.py:447
  28.7 4.6 fusion.1
  34.7 7.3 %psum.15 = f32[1,12,448]{2,0,1:T(1,128)S(1)} all-reduce(f32[1,12,448]{2,0,1:T(1,128)S(1)} %reduce_sum.25), channel_id=1, replica_groups=mesh['chan'=2,'row'=16] {'chan'}, use_global_device_ids=true, to_apply=%region_3.0 | all-reduce | flops 5376 | bytes 43008 | tf_op jit(solution)/shard_map/psum | solution.py:449
  44.6 16.8 %input_lon.1 = (f32[16,3,12,24,128]{4,3,2,1,0:T(8,128)}, f32[16,1,12,24,128]{4,3,2,1,0:T(8,128)}) custom-call(bf16[768,448]{1,0:T(8,128)(2,1)} %constant.64.clone.table_ref, bf16[1,12,448,512]{3,2,1,0:T(8,128)(2,1)} %refs_0_, f32[12,2,448]{2,1,0:T(2,128)} %pad_maximum_fusion.4.stat_ref.refs_1_, f32[1,512]{1,0:T(1,128)} %bitcast.90), custom_call_target="tpu_custom_call" | custom-call | flops 6341787648 | bytes 14942208 | tf_op jit(solution)/shard_map/input_lon/pallas_call | solution.py:452
  61.4 124.3 %all-to-all-done = f32[16,4,12,24,128]{4,3,2,1,0:T(8,128)} async-done(((f32[16,4,12,24,128]{4,3,2,1,0:T(8,128)}), f32[16,4,12,24,128]{4,3,2,1,0:T(8,128)}, u32[]{:S(2)}, u32[]{:S(2)}) %all-to-all-start) | async-done | bytes 9437216 | tf_op jit(solution)/shard_map/all_to_all | solution.py:412
  185.8 195.9 %all_to_all.25 = f32[16,3,12,24,128]{4,3,2,1,0:T(8,128)} all-to-all(f32[16,3,12,24,128]{4,3,2,1,0:T(8,128)} %get-tuple-element.45), channel_id=1, replica_groups=mesh['chan'=2,'row'=16] {'row'}, dimensions={0} | all-to-all | bytes 14155776 | tf_op jit(solution)/shard_map/all_to_all | solution.py:412
  381.7 4.5 all-to-all-start.1
  386.2 2.0 copy.55.w_one_ref
  389.2 43.8 %mixer_0.1 = (f32[16,3,288,128]{3,2,1,0:T(8,128)}, f32[3,520,128]{2,1,0:T(8,128)}) custom-call(bf16[384,384]{1,0:T(8,128)(2,1)} %constant.65.clone.fwd_high_ref, bf16[384,384]{1,0:T(8,128)(2,1)} %constant.66.clone.fwd_low_ref, bf16[384,384]{1,0:T(8,128)(2,1)} %constant.67.clone.inv_high_ref, bf16[384,384]{1,0:T(8,128)(2,1)} %constant.68.clone.inv_low_ref, ...), custom_call_target="tpu_custom_call" | custom-call | flops 17666408448 | bytes 21233664 | tf_op jit(solution)/shard_map/mixer_0/pallas_call | solution.py:495
  434.4 11.2 %all-to-all-start.3 = ((f32[16,3,12,24,128]{4,3,2,1,0:T(8,128)}), f32[16,3,12,24,128]{4,3,2,1,0:T(8,128)}, u32[]{:S(2)}, u32[]{:S(2)}) async-start(f32[16,3,12,24,128]{4,3,2,1,0:T(8,128)} %bitcast.66), calls=%async_computation.3 | async-start | bytes 14155776 | tf_op jit(solution)/shard_map/all_to_all | solution.py:412
  445.6 17.0 %mixer_1.1 = (f32[16,1,288,128]{3,2,1,0:T(8,128)}, f32[1,520,128]{2,1,0:T(8,128)}) custom-call(bf16[384,384]{1,0:T(8,128)(2,1)} %constant.65.clone.fwd_high_ref, bf16[384,384]{1,0:T(8,128)(2,1)} %constant.66.clone.fwd_low_ref, bf16[384,384]{1,0:T(8,128)(2,1)} %constant.67.clone.inv_high_ref, bf16[384,384]{1,0:T(8,128)(2,1)} %constant.68.clone.inv_low_ref, ...), custom_call_target="tpu_custom_call" | custom-call | flops 5888802816 | bytes 7077888 | tf_op jit(solution)/shard_map/mixer_1/pallas_call | solution.py:495
  464.0 1.6 collective-permute-done
  466.7 1.9 collective-permute-start.1
  468.6 24.9 %collective-permute-done.1 = f32[544,128]{1,0:T(8,128)S(1)} collective-permute-done((f32[544,128]{1,0:T(8,128)S(1)}, f32[544,128]{1,0:T(8,128)S(1)}, u32[]{:S(2)}, u32[]{:S(2)}) %collective-permute-start.1) | collective-permute-done | bytes 278560 | tf_op jit(solution)/shard_map/ppermute | solution.py:312
  493.7 68.3 %collective-permute-done.2 = f32[136,128]{1,0:T(8,128)S(1)} collective-permute-done((f32[136,128]{1,0:T(8,128)S(1)}, f32[136,128]{1,0:T(8,128)S(1)}, u32[]{:S(2)}, u32[]{:S(2)}) %collective-permute-start.2) | collective-permute-done | bytes 69664 | tf_op jit(solution)/shard_map/ppermute | solution.py:312
  562.0 11.5 %all-to-all-done.3.grad_ref = f32[16,3,12,24,128]{4,3,2,1,0:T(8,128)} async-done(((f32[16,3,12,24,128]{4,3,2,1,0:T(8,128)}), f32[16,3,12,24,128]{4,3,2,1,0:T(8,128)}, u32[]{:S(2)}, u32[]{:S(2)}) %all-to-all-start.3) | async-done | bytes 7077920 | tf_op jit(solution)/shard_map/all_to_all | solution.py:412
  573.5 31.2 %all-to-all-start.4 = ((f32[16,1,12,24,128]{4,3,2,1,0:T(8,128)}), f32[16,1,12,24,128]{4,3,2,1,0:T(8,128)S(1)}, u32[]{:S(2)}, u32[]{:S(2)}) async-start(f32[16,1,12,24,128]{4,3,2,1,0:T(8,128)} %bitcast.72), calls=%async_computation.4 | async-start | bytes 4718592 | tf_op jit(solution)/shard_map/all_to_all | solution.py:412
  604.8 3.7 collective-permute-start.4
  608.5 41.3 %collective-permute-done.4 = f32[136,128]{1,0:T(8,128)S(1)} collective-permute-done((f32[136,128]{1,0:T(8,128)S(1)}, f32[136,128]{1,0:T(8,128)S(1)}, u32[]{:S(2)}, u32[]{:S(2)}) %collective-permute-start.4) | collective-permute-done | bytes 69664 | tf_op jit(solution)/shard_map/ppermute | solution.py:312
  649.8 15.6 %collective-permute-done.3 = f32[136,128]{1,0:T(8,128)S(1)} collective-permute-done((f32[136,128]{1,0:T(8,128)S(1)}, f32[136,128]{1,0:T(8,128)S(1)}, u32[]{:S(2)}, u32[]{:S(2)}) %collective-permute-start.3) | collective-permute-done | bytes 69664 | tf_op jit(solution)/shard_map/ppermute | solution.py:312
  665.4 10.9 %lon_back_0.1 = (bf16[12,448,384]{2,1,0:T(8,128)(2,1)}, f32[12,2,448]{2,1,0:T(2,128)}) custom-call(bf16[448,384]{1,0:T(8,128)(2,1)} %constant.69.clone.table_ref, f32[16,3,12,24,128]{4,3,2,1,0:T(8,128)} %all-to-all-done.3.grad_ref, bf16[1,12,448,512]{3,2,1,0:T(8,128)(2,1)} %refs_0_, bf16[1,12,448,512]{3,2,1,0:T(8,128)(2,1)} %cot_ref.5, ...), custom_call_target="tpu_custom_call" | custom-call | flops 1585446912 | bytes 19464192 | tf_op jit(solution)/shard_map/lon_back_0/pallas_call | solution.py:559
  677.8 2.9 collective-permute-start.5
  680.7 2.6 collective-permute-done.7
  683.3 1.6 collective-permute-done.6
  685.0 1.6 collective-permute-start.8
  687.9 6.9 lon_back_1.1
  695.1 1.6 collective-permute-start.9
  696.6 2.8 collective-permute-done.9.refs_3_
  700.0 9.0 %finish.1 = bf16[1,12,448,512]{3,2,1,0:T(8,128)(2,1)} custom-call(bf16[1,12,448,512]{3,2,1,0:T(8,128)(2,1)} %refs_0_, f32[12,2,448]{2,1,0:T(2,128)} %pad_maximum_fusion.4.stat_ref.refs_1_, f32[12,2,448]{2,1,0:T(2,128)} %get-tuple-element.55.refs_2_, f32[12,2,448]{2,1,0:T(2,128)} %copy-done.5, bf16[12,448,384]{2,1,0:T(8,128)(2,1)} %get-tuple-element.56.refs_4_, ...), custom_call_target="tpu_custom_call" | custom-call | flops 27525120 | bytes 27525120 | tf_op jit(solution)/shard_map/finish/pallas_call | solution.py:593
  (73 shorter events, 16.4 us)
Async XLA Ops:
  9.3 176.4 %all-to-all-start = ((f32[16,4,12,24,128]{4,3,2,1,0:T(8,128)}), f32[16,4,12,24,128]{4,3,2,1,0:T(8,128)}, u32[]{:S(2)}, u32[]{:S(2)}) async-start(f32[16,4,12,24,128]{4,3,2,1,0:T(8,128)} %cot_lon.1), calls=%async_computation | async-start | bytes 18874368 | tf_op jit(solution)/shard_map/all_to_all | solution.py:412
  16.8 16.6 %copy-start.3 = (bf16[2,512,128]{2,1,0:T(8,128)(2,1)S(1)}, bf16[2,512,128]{2,1,0:T(8,128)(2,1)}, u32[]{:S(2)}) copy-start(bf16[2,512,128]{2,1,0:T(8,128)(2,1)} %param.21) | copy-start | bytes 786436
  16.8 16.9 %copy-start.4 = (bf16[2,512,128]{2,1,0:T(8,128)(2,1)S(1)}, bf16[2,512,128]{2,1,0:T(8,128)(2,1)}, u32[]{:S(2)}) copy-start(bf16[2,512,128]{2,1,0:T(8,128)(2,1)} %param.19) | copy-start | bytes 786436
  20.3 13.7 %copy-start.7 = (f32[2,512]{1,0:T(2,128)S(1)}, f32[2,512]{1,0:T(2,128)}, u32[]{:S(2)}) copy-start(f32[2,512]{1,0:T(2,128)} %param.22) | copy-start | bytes 12292
  20.3 13.7 %copy-start.8 = (f32[2,512]{1,0:T(2,128)S(1)}, f32[2,512]{1,0:T(2,128)}, u32[]{:S(2)}) copy-start(f32[2,512]{1,0:T(2,128)} %param.20) | copy-start | bytes 12292
  20.4 21.7 %copy-start.9 = (f32[512]{0:T(512)S(1)}, f32[512]{0:T(512)}, u32[]{:S(2)}) copy-start(f32[512]{0:T(512)} %param.18) | copy-start | bytes 6148
  381.7 51.3 %all-to-all-start.1 = ((f32[16,1,12,24,128]{4,3,2,1,0:T(8,128)}), f32[16,1,12,24,128]{4,3,2,1,0:T(8,128)S(1)}, u32[]{:S(2)}, u32[]{:S(2)}) async-start(f32[16,1,12,24,128]{4,3,2,1,0:T(8,128)} %get-tuple-element.42), calls=%async_computation.1 | async-start | bytes 4718592 | tf_op jit(solution)/shard_map/all_to_all | solution.py:412
  433.0 1.4 copy-start.2
  434.4 139.1 %all-to-all-start.3 = ((f32[16,3,12,24,128]{4,3,2,1,0:T(8,128)}), f32[16,3,12,24,128]{4,3,2,1,0:T(8,128)}, u32[]{:S(2)}, u32[]{:S(2)}) async-start(f32[16,3,12,24,128]{4,3,2,1,0:T(8,128)} %bitcast.66), calls=%async_computation.3 | async-start | bytes 14155776 | tf_op jit(solution)/shard_map/all_to_all | solution.py:412
  445.6 17.0 %copy-start.1 = (f32[3,520,128]{2,1,0:T(8,128)S(1)}, f32[3,520,128]{2,1,0:T(8,128)}, u32[]{:S(2)}) copy-start(f32[3,520,128]{2,1,0:T(8,128)} %get-tuple-element.46) | copy-start | bytes 2396164
  463.6 2.0 collective-permute-start
  466.7 26.8 %collective-permute-start.1 = (f32[544,128]{1,0:T(8,128)S(1)}, f32[544,128]{1,0:T(8,128)S(1)}, u32[]{:S(2)}, u32[]{:S(2)}) collective-permute-start(f32[544,128]{1,0:T(8,128)S(1)} %slice_select_fusion.1), channel_id=1, source_target_pairs={{0,2},{1,3},{2,0},{3,1},{4,6},{5,7},{6,4},{7,5},{8,10},{9,11},{10,... | collective-permute-start | bytes 835592 | tf_op jit(solution)/shard_map/ppermute | solution.py:312
  493.6 68.4 %collective-permute-start.2 = (f32[136,128]{1,0:T(8,128)S(1)}, f32[136,128]{1,0:T(8,128)S(1)}, u32[]{:S(2)}, u32[]{:S(2)}) collective-permute-start(f32[136,128]{1,0:T(8,128)S(1)} %get-tuple-element.77), channel_id=1, source_target_pairs={{0,4},{1,5},{2,6},{3,7},{4,0},{5,1},{6,2},{7,3},{8,12},{9,13},{10,... | collective-permute-start | bytes 208904 | tf_op jit(solution)/shard_map/ppermute | solution.py:312
  573.5 113.0 %all-to-all-start.4 = ((f32[16,1,12,24,128]{4,3,2,1,0:T(8,128)}), f32[16,1,12,24,128]{4,3,2,1,0:T(8,128)S(1)}, u32[]{:S(2)}, u32[]{:S(2)}) async-start(f32[16,1,12,24,128]{4,3,2,1,0:T(8,128)} %bitcast.72), calls=%async_computation.4 | async-start | bytes 4718592 | tf_op jit(solution)/shard_map/all_to_all | solution.py:412
  604.8 45.1 %collective-permute-start.4 = (f32[136,128]{1,0:T(8,128)S(1)}, f32[136,128]{1,0:T(8,128)S(1)}, u32[]{:S(2)}, u32[]{:S(2)}) collective-permute-start(f32[136,128]{1,0:T(8,128)S(1)} %get-tuple-element.76), channel_id=1, source_target_pairs={{0,12},{1,13},{2,14},{3,15},{4,8},{5,9},{6,10},{7,11},{8,4},{9,5},... | collective-permute-start | bytes 208904 | tf_op jit(solution)/shard_map/ppermute | solution.py:312
  608.5 56.9 %collective-permute-start.3 = (f32[136,128]{1,0:T(8,128)S(1)}, f32[136,128]{1,0:T(8,128)S(1)}, u32[]{:S(2)}, u32[]{:S(2)}) collective-permute-start(f32[136,128]{1,0:T(8,128)S(1)} %get-tuple-element.75), channel_id=1, source_target_pairs={{0,8},{1,9},{2,10},{3,11},{4,12},{5,13},{6,14},{7,15},{8,0},{9,1},... | collective-permute-start | bytes 208904 | tf_op jit(solution)/shard_map/ppermute | solution.py:312
  676.4 7.0 collective-permute-start.7
  677.8 7.0 collective-permute-start.6
  677.8 7.0 collective-permute-start.5
  685.0 9.9 %collective-permute-start.8 = (f32[544,128]{1,0:T(8,128)S(1)}, f32[544,128]{1,0:T(8,128)S(1)}, u32[]{:S(2)}, u32[]{:S(2)}) collective-permute-start(f32[544,128]{1,0:T(8,128)S(1)} %pad_maximum_fusion.3), channel_id=1, source_target_pairs={{0,2},{1,3},{2,0},{3,1},{4,6},{5,7},{6,4},{7,5},{8,10},{9,11},{10,... | collective-permute-start | bytes 835592 | tf_op jit(solution)/shard_map/ppermute | solution.py:312
  686.5 1.4 copy-start
  695.0 14.1 %collective-permute-start.10 = (f32[1088,128]{1,0:T(8,128)S(1)}, f32[1088,128]{1,0:T(8,128)S(1)}, u32[]{:S(2)}, u32[]{:S(2)}) collective-permute-start(f32[1088,128]{1,0:T(8,128)S(1)} %pad_maximum_fusion.1), channel_id=1, source_target_pairs={{0,1},{1,0},{2,3},{3,2},{4,5},{5,4},{6,7},{7,6},{8,9},{9,8},{10,11... | collective-permute-start | bytes 1671176 | tf_op jit(solution)/shard_map/ppermute | solution.py:312
  695.1 4.4 collective-permute-start.9
  699.4 0.6 copy-start.5
  709.1 3.2 copy-start.6

commit v5 on v4

--- a/solution.py
+++ b/solution.py
@@ -322,6 +322,10 @@
     return piece, other
 
 
+def low_bits(axis):
+    return max(lax.axis_size(axis).bit_length() - 2, 0)
+
+
 def halve(piece, axis):
     index = lax.axis_index(axis)
     for i in range(low_bits(axis)):
@@ -331,33 +335,9 @@
         piece = jnp.where(upper, high, low) + xor_permute(
             jnp.where(upper, low, high), axis, 1 << i
         )
+    if lax.axis_size(axis) > 1:
+        piece = piece + xor_permute(piece, axis, 1 << low_bits(axis))
     return piece
-
-
-def low_bits(axis):
-    return (lax.axis_size(axis).bit_length() - 1) // 2
-
-
-def scatter_far(piece, axis):
-    low = low_bits(axis)
-    far = lax.axis_size(axis) >> low
-    parts = piece.reshape(far, -1, piece.shape[-1])
-    place = lax.axis_index(axis) >> low
-    total = lax.dynamic_index_in_dim(parts, place, 0, False)
-    others = [lax.dynamic_index_in_dim(parts, place ^ d, 0, False) for d in range(1, far)]
-    others = [xor_permute(part, axis, d << low) for d, part in enumerate(others, 1)]
-    return total + others[0], others[1:]
-
-
-def gather_far(total, axis):
-    low = low_bits(axis)
-    far = lax.axis_size(axis) >> low
-    place = lax.axis_index(axis) >> low
-    parts = [total] + [xor_permute(total, axis, d << low) for d in range(1, far)]
-    parts = jnp.stack(parts)
-    return jnp.concatenate(
-        [lax.dynamic_index_in_dim(parts, place ^ d, 0, False) for d in range(far)], 0
-    )
 
 
 def double(piece, axis, bit):
@@ -541,7 +521,7 @@
     tail = -(blocks * param_rows) % (unit * blocks)
     flat = jnp.concatenate([m[1].reshape(-1, BS) for m in mixed], 0)
     flat = jnp.pad(flat, ((0, tail), (0, 0)))
-    param_part, far_parts = scatter_far(halve(flat, "row"), "row")
+    param_part = halve(flat, "row")
 
     grads = []
     sums = None
@@ -551,7 +531,7 @@
         carry_in = sums is not None
         if index == len(chunks) - 1 and carry_in:
             piece, param_part = lax.optimization_barrier((piece, param_part))
-            param_part, sums = lax.optimization_barrier((sum(far_parts, param_part), sums))
+            param_part, sums = lax.optimization_barrier((param_part, sums))
         piece = exchange(piece)
         in_spec = pl.BlockSpec(
             (1, many, width, count * BS), lambda h, at=start // count: (0, h, 0, at)
@@ -581,12 +561,8 @@
         )(back, piece, inputs, cotangent, stats, gain, *([sums] * carry_in))
         grads.append(grad)
 
-    if len(chunks) == 1:
-        param_part = sum(far_parts, param_part)
-    param_sums = gather_far(param_part, "row")
+    param_sums = param_part
     for i in reversed(range(low_bits("row"))):
-        if i == 0:
-            param_sums, sums = lax.optimization_barrier((param_sums, sums))
         param_sums = double(param_sums, "row", 1 << i)
     param_sums = param_sums[: blocks * param_rows].reshape(blocks, param_rows, BS)
 

time: 714 us -> 693 us (0.971)
  starting transfers between devices: 68.1 us -> 39.3 us
    all_to_all x4, starting transfers between devices: 54.4 us -> 26.7 us  [exchange(): return lax.all_to_all(piece, 'row', split_axis=0, concat_axis=0, tiled=True)]
    ppermute x11 -> x8, waiting for transfers between devices: 159 us -> 176 us  [xor_permute(): return lax.ppermute(piece, axis, [(i, i ^ bit) for i in range(size)])]
    all_to_all x4, waiting for transfers between devices: 136 us -> 124 us  [exchange(): return lax.all_to_all(piece, 'row', split_axis=0, concat_axis=0, tiled=True)]
  transfers between devices with their start and end apart: 15 -> 12, of which waited for: 10 -> 8; matrix products, arithmetic and copies ran while one was open for 2% -> 3% of each run, Pallas kernels for 15% -> 15%
where the time goes in v5:
time: 693 us; the launch traced here: 691 us
  waiting for transfers between devices  301 us (43%)
  blocking collectives  212 us (31%)
  Pallas kernels  113 us (16%)
  starting transfers between devices  39.3 us (6%)
  other arithmetic  14.7 us (2%)
  local copies, waits for them, and re-layouts  10.7 us (2%)
    all_to_all x1, blocking collectives, exchange(): return lax.all_to_all(piece, 'row', split_axis=0, concat_axis=0, tiled=True)  196 us
    ppermute x8, waiting for transfers between devices, xor_permute(): return lax.ppermute(piece, axis, [(i, i ^ bit) for i in range(size)])  176 us
    all_to_all x4, waiting for transfers between devices, exchange(): return lax.all_to_all(piece, 'row', split_axis=0, concat_axis=0, tiled=True)  124 us
    pallas_call x2, Pallas kernels, mix(): pl.pallas_call(functools.partial(mixer_kernel, own, group), grid=(count,)...  60.9 us
    all_to_all x4, starting transfers between devices, exchange(): return lax.all_to_all(piece, 'row', split_axis=0, concat_axis=0, tiled=True)  26.7 us
    pallas_call x2, Pallas kernels, on_device(): pl.pallas_call(functools.partial(lon_back_kernel, start, carry_in), grid=...  17.9 us
    pallas_call x1, Pallas kernels, on_device(): pl.pallas_call(input_lon_kernel, grid=(rows // few,), in_specs=[whole((2...  16.8 us
  transfers between devices with their start and end apart: 12, of which 8 were waited for; matrix products, arithmetic and copies ran while one was open for 3% of the time, Pallas kernels for 15%

profile of v5, /device:TPU:0, one launch (start us, length us, event | category | flops | bytes accessed | tf_op | source)
XLA Modules:
  0.0 691.2 jit_solution(6528157750162721996)
XLA Ops:
  0.6 8.7 %cot_lon.1 = f32[16,4,12,24,128]{4,3,2,1,0:T(8,128)} custom-call(bf16[384,448]{1,0:T(8,128)(2,1)} %constant.44.clone.table_ref, bf16[1,12,448,512]{3,2,1,0:T(8,128)(2,1)} %cot_ref.5), custom_call_target="tpu_custom_call" | custom-call | flops 2113929216 | bytes 14942208 | tf_op jit(solution)/shard_map/cot_lon/pallas_call | solution.py:413
  9.3 7.4 %all-to-all-start = ((f32[16,4,12,24,128]{4,3,2,1,0:T(8,128)}), f32[16,4,12,24,128]{4,3,2,1,0:T(8,128)}, u32[]{:S(2)}, u32[]{:S(2)}) async-start(f32[16,4,12,24,128]{4,3,2,1,0:T(8,128)} %cot_lon.1), calls=%async_computation | async-start | bytes 18874368 | tf_op jit(solution)/shard_map/all_to_all | solution.py:392
  16.8 3.5 convert_reduce_fusion
  20.4 8.3 %psum.14 = f32[1,12,448]{2,0,1:T(1,128)S(1)} all-reduce(f32[1,12,448]{2,0,1:T(1,128)S(1)} %reduce_sum.23), channel_id=1, replica_groups=mesh['chan'=2,'row'=16] {'chan'}, use_global_device_ids=true, to_apply=%region_1.0 | all-reduce | flops 5376 | bytes 43008 | tf_op jit(solution)/shard_map/psum | solution.py:427
  28.7 4.6 fusion.1
  34.7 7.3 %psum.15 = f32[1,12,448]{2,0,1:T(1,128)S(1)} all-reduce(f32[1,12,448]{2,0,1:T(1,128)S(1)} %reduce_sum.25), channel_id=1, replica_groups=mesh['chan'=2,'row'=16] {'chan'}, use_global_device_ids=true, to_apply=%region_3.0 | all-reduce | flops 5376 | bytes 43008 | tf_op jit(solution)/shard_map/psum | solution.py:429
  44.5 16.8 %input_lon.1 = (f32[16,3,12,24,128]{4,3,2,1,0:T(8,128)}, f32[16,1,12,24,128]{4,3,2,1,0:T(8,128)}) custom-call(bf16[768,448]{1,0:T(8,128)(2,1)} %constant.45.clone.table_ref, bf16[1,12,448,512]{3,2,1,0:T(8,128)(2,1)} %refs_0_, f32[12,2,448]{2,1,0:T(2,128)} %pad_maximum_fusion.3.stat_ref.refs_1_, f32[1,512]{1,0:T(1,128)} %bitcast.63), custom_call_target="tpu_custom_call" | custom-call | flops 6341787648 | bytes 14942208 | tf_op jit(solution)/shard_map/input_lon/pallas_call | solution.py:432
  61.4 124.4 %all-to-all-done = f32[16,4,12,24,128]{4,3,2,1,0:T(8,128)} async-done(((f32[16,4,12,24,128]{4,3,2,1,0:T(8,128)}), f32[16,4,12,24,128]{4,3,2,1,0:T(8,128)}, u32[]{:S(2)}, u32[]{:S(2)}) %all-to-all-start) | async-done | bytes 9437216 | tf_op jit(solution)/shard_map/all_to_all | solution.py:392
  185.7 195.9 %all_to_all.25 = f32[16,3,12,24,128]{4,3,2,1,0:T(8,128)} all-to-all(f32[16,3,12,24,128]{4,3,2,1,0:T(8,128)} %get-tuple-element.43), channel_id=1, replica_groups=mesh['chan'=2,'row'=16] {'row'}, dimensions={0} | all-to-all | bytes 14155776 | tf_op jit(solution)/shard_map/all_to_all | solution.py:392
  381.7 4.5 all-to-all-start.1
  386.2 2.0 copy.55.w_one_ref
  389.2 43.9 %mixer_0.1 = (f32[16,3,288,128]{3,2,1,0:T(8,128)}, f32[3,520,128]{2,1,0:T(8,128)}) custom-call(bf16[384,384]{1,0:T(8,128)(2,1)} %constant.46.clone.fwd_high_ref, bf16[384,384]{1,0:T(8,128)(2,1)} %constant.47.clone.fwd_low_ref, bf16[384,384]{1,0:T(8,128)(2,1)} %constant.48.clone.inv_high_ref, bf16[384,384]{1,0:T(8,128)(2,1)} %constant.49.clone.inv_low_ref, ...), custom_call_target="tpu_custom_call" | custom-call | flops 17666408448 | bytes 21233664 | tf_op jit(solution)/shard_map/mixer_0/pallas_call | solution.py:475
  433.1 1.4 copy-done.2
  434.5 11.1 %all-to-all-start.4 = ((f32[16,3,12,24,128]{4,3,2,1,0:T(8,128)}), f32[16,3,12,24,128]{4,3,2,1,0:T(8,128)}, u32[]{:S(2)}, u32[]{:S(2)}) async-start(f32[16,3,12,24,128]{4,3,2,1,0:T(8,128)} %bitcast.45), calls=%async_computation.4 | async-start | bytes 14155776 | tf_op jit(solution)/shard_map/all_to_all | solution.py:392
  445.6 17.0 %mixer_1.1 = (f32[16,1,288,128]{3,2,1,0:T(8,128)}, f32[1,520,128]{2,1,0:T(8,128)}) custom-call(bf16[384,384]{1,0:T(8,128)(2,1)} %constant.46.clone.fwd_high_ref, bf16[384,384]{1,0:T(8,128)(2,1)} %constant.47.clone.fwd_low_ref, bf16[384,384]{1,0:T(8,128)(2,1)} %constant.48.clone.inv_high_ref, bf16[384,384]{1,0:T(8,128)(2,1)} %constant.49.clone.inv_low_ref, ...), custom_call_target="tpu_custom_call" | custom-call | flops 5888802816 | bytes 7077888 | tf_op jit(solution)/shard_map/mixer_1/pallas_call | solution.py:475
  464.0 1.6 collective-permute-done
  466.7 1.9 collective-permute-start.1
  468.6 24.9 %collective-permute-done.1 = f32[544,128]{1,0:T(8,128)S(1)} collective-permute-done((f32[544,128]{1,0:T(8,128)S(1)}, f32[544,128]{1,0:T(8,128)S(1)}, u32[]{:S(2)}, u32[]{:S(2)}) %collective-permute-start.1) | collective-permute-done | bytes 278560 | tf_op jit(solution)/shard_map/ppermute | solution.py:312
  493.7 69.8 %collective-permute-done.2 = f32[272,128]{1,0:T(8,128)S(1)} collective-permute-done((f32[272,128]{1,0:T(8,128)S(1)}, f32[272,128]{1,0:T(8,128)S(1)}, u32[]{:S(2)}, u32[]{:S(2)}) %collective-permute-start.2) | collective-permute-done | bytes 139296 | tf_op jit(solution)/shard_map/ppermute | solution.py:312
  563.5 4.6 collective-permute-start.3
  568.1 39.2 %collective-permute-done.3 = f32[272,128]{1,0:T(8,128)S(1)} collective-permute-done((f32[272,128]{1,0:T(8,128)S(1)}, f32[272,128]{1,0:T(8,128)S(1)}, u32[]{:S(2)}, u32[]{:S(2)}) %collective-permute-start.3) | collective-permute-done | bytes 139296 | tf_op jit(solution)/shard_map/ppermute | solution.py:312
  607.4 3.7 all-to-all-start.3
  611.1 10.9 %lon_back_0.1 = (bf16[12,448,384]{2,1,0:T(8,128)(2,1)}, f32[12,2,448]{2,1,0:T(2,128)}) custom-call(bf16[448,384]{1,0:T(8,128)(2,1)} %constant.50.clone.table_ref, f32[16,3,12,24,128]{4,3,2,1,0:T(8,128)} %all-to-all-done.4.grad_ref, bf16[1,12,448,512]{3,2,1,0:T(8,128)(2,1)} %refs_0_, bf16[1,12,448,512]{3,2,1,0:T(8,128)(2,1)} %cot_ref.5, ...), custom_call_target="tpu_custom_call" | custom-call | flops 1585446912 | bytes 19464192 | tf_op jit(solution)/shard_map/lon_back_0/pallas_call | solution.py:539
  622.0 1.8 collective-permute-start.5
  623.9 29.3 %collective-permute-done.5 = f32[272,128]{1,0:T(8,128)S(1)} collective-permute-done((f32[272,128]{1,0:T(8,128)S(1)}, f32[272,128]{1,0:T(8,128)S(1)}, u32[]{:S(2)}, u32[]{:S(2)}) %collective-permute-start.5) | collective-permute-done | bytes 139296 | tf_op jit(solution)/shard_map/ppermute | solution.py:312
  653.2 2.3 collective-permute-start.6
  655.5 8.6 %collective-permute-done.6 = f32[544,128]{1,0:T(8,128)S(1)} collective-permute-done((f32[544,128]{1,0:T(8,128)S(1)}, f32[544,128]{1,0:T(8,128)S(1)}, u32[]{:S(2)}, u32[]{:S(2)}) %collective-permute-start.6) | collective-permute-done | bytes 278560 | tf_op jit(solution)/shard_map/ppermute | solution.py:312
  665.0 1.4 copy-done
  666.4 6.9 %lon_back_1.1 = (bf16[12,448,128]{2,1,0:T(8,128)(2,1)}, f32[12,2,448]{2,1,0:T(2,128)}) custom-call(bf16[448,384]{1,0:T(8,128)(2,1)} %constant.50.clone.table_ref, f32[16,1,12,24,128]{4,3,2,1,0:T(8,128)} %copy-done, bf16[1,12,448,512]{3,2,1,0:T(8,128)(2,1)} %refs_0_, bf16[1,12,448,512]{3,2,1,0:T(8,128)(2,1)} %cot_ref.5, ...), custom_call_target="tpu_custom_call" | custom-call | flops 528482304 | bytes 6488064 | tf_op jit(solution)/shard_map/lon_back_1/pallas_call | solution.py:539
  673.4 1.5 collective-permute-start.4
  674.9 2.9 collective-permute-done.4.refs_3_
  678.3 9.0 %finish.1 = bf16[1,12,448,512]{3,2,1,0:T(8,128)(2,1)} custom-call(bf16[1,12,448,512]{3,2,1,0:T(8,128)(2,1)} %refs_0_, f32[12,2,448]{2,1,0:T(2,128)} %pad_maximum_fusion.3.stat_ref.refs_1_, f32[12,2,448]{2,1,0:T(2,128)} %get-tuple-element.51.refs_2_, f32[12,2,448]{2,1,0:T(2,128)} %copy-done.5, bf16[12,448,384]{2,1,0:T(8,128)(2,1)} %get-tuple-element.52.refs_4_, ...), custom_call_target="tpu_custom_call" | custom-call | flops 27525120 | bytes 27525120 | tf_op jit(solution)/shard_map/finish/pallas_call | solution.py:569
  (66 shorter events, 12.9 us)
Async XLA Ops:
  9.3 176.4 %all-to-all-start = ((f32[16,4,12,24,128]{4,3,2,1,0:T(8,128)}), f32[16,4,12,24,128]{4,3,2,1,0:T(8,128)}, u32[]{:S(2)}, u32[]{:S(2)}) async-start(f32[16,4,12,24,128]{4,3,2,1,0:T(8,128)} %cot_lon.1), calls=%async_computation | async-start | bytes 18874368 | tf_op jit(solution)/shard_map/all_to_all | solution.py:392
  16.8 16.6 %copy-start.3 = (bf16[2,512,128]{2,1,0:T(8,128)(2,1)S(1)}, bf16[2,512,128]{2,1,0:T(8,128)(2,1)}, u32[]{:S(2)}) copy-start(bf16[2,512,128]{2,1,0:T(8,128)(2,1)} %param.21) | copy-start | bytes 786436
  16.8 16.9 %copy-start.4 = (bf16[2,512,128]{2,1,0:T(8,128)(2,1)S(1)}, bf16[2,512,128]{2,1,0:T(8,128)(2,1)}, u32[]{:S(2)}) copy-start(bf16[2,512,128]{2,1,0:T(8,128)(2,1)} %param.19) | copy-start | bytes 786436
  20.3 13.7 %copy-start.7 = (f32[2,512]{1,0:T(2,128)S(1)}, f32[2,512]{1,0:T(2,128)}, u32[]{:S(2)}) copy-start(f32[2,512]{1,0:T(2,128)} %param.22) | copy-start | bytes 12292
  20.3 13.7 %copy-start.8 = (f32[2,512]{1,0:T(2,128)S(1)}, f32[2,512]{1,0:T(2,128)}, u32[]{:S(2)}) copy-start(f32[2,512]{1,0:T(2,128)} %param.20) | copy-start | bytes 12292
  20.3 21.7 %copy-start.9 = (f32[512]{0:T(512)S(1)}, f32[512]{0:T(512)}, u32[]{:S(2)}) copy-start(f32[512]{0:T(512)} %param.18) | copy-start | bytes 6148
  381.7 51.4 %all-to-all-start.1 = ((f32[16,1,12,24,128]{4,3,2,1,0:T(8,128)}), f32[16,1,12,24,128]{4,3,2,1,0:T(8,128)S(1)}, u32[]{:S(2)}, u32[]{:S(2)}) async-start(f32[16,1,12,24,128]{4,3,2,1,0:T(8,128)} %get-tuple-element.40), calls=%async_computation.1 | async-start | bytes 4718592 | tf_op jit(solution)/shard_map/all_to_all | solution.py:392
  433.1 1.4 copy-start.2
  434.5 172.9 %all-to-all-start.4 = ((f32[16,3,12,24,128]{4,3,2,1,0:T(8,128)}), f32[16,3,12,24,128]{4,3,2,1,0:T(8,128)}, u32[]{:S(2)}, u32[]{:S(2)}) async-start(f32[16,3,12,24,128]{4,3,2,1,0:T(8,128)} %bitcast.45), calls=%async_computation.4 | async-start | bytes 14155776 | tf_op jit(solution)/shard_map/all_to_all | solution.py:392
  445.6 17.0 %copy-start.1 = (f32[3,520,128]{2,1,0:T(8,128)S(1)}, f32[3,520,128]{2,1,0:T(8,128)}, u32[]{:S(2)}) copy-start(f32[3,520,128]{2,1,0:T(8,128)} %get-tuple-element.44) | copy-start | bytes 2396164
  463.6 2.0 collective-permute-start
  466.7 26.8 %collective-permute-start.1 = (f32[544,128]{1,0:T(8,128)S(1)}, f32[544,128]{1,0:T(8,128)S(1)}, u32[]{:S(2)}, u32[]{:S(2)}) collective-permute-start(f32[544,128]{1,0:T(8,128)S(1)} %slice_select_fusion.1), channel_id=1, source_target_pairs={{0,2},{1,3},{2,0},{3,1},{4,6},{5,7},{6,4},{7,5},{8,10},{9,11},{10,... | collective-permute-start | bytes 835592 | tf_op jit(solution)/shard_map/ppermute | solution.py:312
  493.6 69.9 %collective-permute-start.2 = (f32[272,128]{1,0:T(8,128)S(1)}, f32[272,128]{1,0:T(8,128)S(1)}, u32[]{:S(2)}, u32[]{:S(2)}) collective-permute-start(f32[272,128]{1,0:T(8,128)S(1)} %slice_select_fusion.2), channel_id=1, source_target_pairs={{0,4},{1,5},{2,6},{3,7},{4,0},{5,1},{6,2},{7,3},{8,12},{9,13},{10,... | collective-permute-start | bytes 417800 | tf_op jit(solution)/shard_map/ppermute | solution.py:312
  563.5 43.8 %collective-permute-start.3 = (f32[272,128]{1,0:T(8,128)S(1)}, f32[272,128]{1,0:T(8,128)S(1)}, u32[]{:S(2)}, u32[]{:S(2)}) collective-permute-start(f32[272,128]{1,0:T(8,128)S(1)} %select_add_fusion.2), channel_id=1, source_target_pairs={{0,8},{1,9},{2,10},{3,11},{4,12},{5,13},{6,14},{7,15},{8,0},{9,1},... | collective-permute-start | bytes 417800 | tf_op jit(solution)/shard_map/ppermute | solution.py:312
  607.4 57.6 %all-to-all-start.3 = ((f32[16,1,12,24,128]{4,3,2,1,0:T(8,128)}), f32[16,1,12,24,128]{4,3,2,1,0:T(8,128)S(1)}, u32[]{:S(2)}, u32[]{:S(2)}) async-start(f32[16,1,12,24,128]{4,3,2,1,0:T(8,128)} %bitcast.51), calls=%async_computation.3 | async-start | bytes 4718592 | tf_op jit(solution)/shard_map/all_to_all | solution.py:392
  622.0 31.1 %collective-permute-start.5 = (f32[272,128]{1,0:T(8,128)S(1)}, f32[272,128]{1,0:T(8,128)S(1)}, u32[]{:S(2)}, u32[]{:S(2)}) collective-permute-start(f32[272,128]{1,0:T(8,128)S(1)} %add.33), channel_id=1, source_target_pairs={{0,4},{1,5},{2,6},{3,7},{4,0},{5,1},{6,2},{7,3},{8,12},{9,13},{10,... | collective-permute-start | bytes 417800 | tf_op jit(solution)/shard_map/ppermute | solution.py:312
  653.2 10.9 %collective-permute-start.6 = (f32[544,128]{1,0:T(8,128)S(1)}, f32[544,128]{1,0:T(8,128)S(1)}, u32[]{:S(2)}, u32[]{:S(2)}) collective-permute-start(f32[544,128]{1,0:T(8,128)S(1)} %pad_maximum_fusion.2), channel_id=1, source_target_pairs={{0,2},{1,3},{2,0},{3,1},{4,6},{5,7},{6,4},{7,5},{8,10},{9,11},{10,... | collective-permute-start | bytes 835592 | tf_op jit(solution)/shard_map/ppermute | solution.py:312
  665.0 22.4 %collective-permute-start.7 = (f32[1088,128]{1,0:T(8,128)}, f32[1088,128]{1,0:T(8,128)S(1)}, u32[]{:S(2)}, u32[]{:S(2)}) collective-permute-start(f32[1088,128]{1,0:T(8,128)} %pad_maximum_fusion.1), channel_id=1, source_target_pairs={{0,1},{1,0},{2,3},{3,2},{4,5},{5,4},{6,7},{7,6},{8,9},{9,8},{10,11... | collective-permute-start | bytes 1671176 | tf_op jit(solution)/shard_map/ppermute | solution.py:312
  665.0 1.4 copy-start
  673.4 4.4 collective-permute-start.4
  677.7 0.6 copy-start.5
  687.4 3.2 copy-start.6

commit v6 on v5

--- a/solution.py
+++ b/solution.py
@@ -110,13 +110,23 @@
             out_ref[:, b, r] = result[:, b * BS : (b + 1) * BS].reshape(owners, padded, BS)
 
 
-def input_lon_kernel(table_ref, in_ref, stat_ref, gain_ref, *out_refs):
+def piece_to(refs, me, i):
+    near = len(refs)
+    return refs[0].at[me ^ i] if near == 1 else refs[i % near].at[i // near]
+
+
+def piece_from(refs, me, i):
+    near = refs[0].shape[0]
+    return refs[0].at[me ^ i] if len(refs) == 1 else refs[i // near].at[i % near]
+
+
+def input_lon_kernel(chunks, me_ref, table_ref, in_ref, stat_ref, gain_ref, *refs):
+    out_refs, scratch = refs[:-1], refs[-1]
     tall = table_ref.shape[0] // 2
     for r in range(in_ref.shape[1]):
         mean, rstd = columns_of(stat_ref[r])
         at = 0
-        for out_ref in out_refs:
-            owners, blocks, _, padded, _ = out_ref.shape
+        for index, blocks in enumerate(chunks):
             pieces = []
             for b in range(at, at + blocks):
                 lanes = slice(b * BS, (b + 1) * BS)
@@ -126,13 +136,26 @@
             high, low = split(jnp.concatenate(pieces, 1))
             both = dot(table_ref[...], high)
             result = both[:tall] + both[tall:] + dot(table_ref[:tall], low)
-            for b in range(blocks):
-                out_ref[:, b, r] = result[:, b * BS : (b + 1) * BS].reshape(owners, padded, BS)
+            if index < len(chunks) - 1:
+                owners, _, _, padded, _ = out_refs[index].shape
+                for b in range(blocks):
+                    piece = result[:, b * BS : (b + 1) * BS].reshape(owners, padded, BS)
+                    out_refs[index][:, b, r] = piece
+            else:
+                last = out_refs[index:]
+                padded = last[0].shape[3]
+                scratch[r] = result
+                for i in range(tall // padded):
+                    place = pl.ds(pl.multiple_of((me_ref[0] ^ i) * padded, padded), padded)
+                    piece_to(last, me_ref[0], i)[0, r] = scratch[r, place]
 
 
 def mixer_kernel(
     own,
     group,
+    x_count,
+    grad_count,
+    me_ref,
     fwd_high_ref,
     fwd_low_ref,
     inv_high_ref,
@@ -143,27 +166,23 @@
     w_two_t_ref,
     bias_ref,
     shift_ref,
-    x_ref,
     c_ref,
-    grad_ref,
-    sums_ref,
-    x_scr,
-    c_scr,
-    high_scr,
-    low_scr,
-    spec_scr,
-    hid_scr,
-    two_scr,
-    pre_scr,
-    gain_scr,
+    *refs,
 ):
-    sources, _, span, _ = x_ref.shape
+    x_refs, grad_refs = refs[:x_count], refs[x_count : x_count + grad_count]
+    sums_ref, x_scr, c_scr, high_scr, low_scr, spec_scr, hid_scr, two_scr, pre_scr, gain_scr = refs[
+        x_count + grad_count :
+    ]
+    sources, _, span, _ = c_ref.shape
     length = fwd_high_ref.shape[0] // 2
     padded = sources * span // length
     steps = own // group
-    for s in range(sources):
-        x_scr[s * span : (s + 1) * span] = x_ref[s, 0]
-        c_scr[s * span : (s + 1) * span] = c_ref[s, 0]
+    places = [
+        pl.ds(pl.multiple_of((me_ref[0] ^ i) * span, span), span) for i in range(sources)
+    ]
+    for i, place in enumerate(places):
+        x_scr[place] = piece_from(x_refs, me_ref[0], i)[0]
+        c_scr[i * span : (i + 1) * span] = c_ref[i, 0]
     for k in range(own):
         step, place = divmod(k, group)
         for which, scr in enumerate((x_scr, c_scr)):
@@ -234,8 +253,8 @@
                 x_scr[pl.ds(part * own + k, length, stride=padded), :] = piece
     for k in range(2 * own, padded):
         x_scr[pl.ds(k, length, stride=padded), :] = jnp.zeros((length, BS), F32)
-    for s in range(sources):
-        grad_ref[s, 0] = x_scr[s * span : (s + 1) * span]
+    for i, place in enumerate(places):
+        piece_to(grad_refs, me_ref[0], i)[0] = x_scr[place]
     for i, (left, right) in enumerate(((spec_scr, pre_scr), (hid_scr, two_scr))):
         square = dot_rows(left[...], right[...])
         sums_ref[0, 2 * i * BS : (2 * i + 1) * BS] = square[:BS, :BS] + square[BS:, BS:]
@@ -256,20 +275,28 @@
 
 
 def lon_back_kernel(
-    offset, carry_in, table_ref, grad_ref, in_ref, cot_ref, stat_ref, gain_ref, *refs
+    offset, carry_in, count_in, me_ref, table_ref, in_ref, cot_ref, stat_ref, gain_ref, *refs
 ):
+    grad_refs = refs[:count_in]
     if carry_in:
-        before_ref, out_ref, sums_ref = refs
+        before_ref, out_ref, sums_ref, scratch = refs[count_in:]
     else:
-        out_ref, sums_ref = refs
-    sources, blocks, rows, padded, _ = grad_ref.shape
+        out_ref, sums_ref, scratch = refs[count_in:]
+    _, blocks, rows, padded, _ = grad_refs[0].shape
     ones = jnp.ones((16, BS), BF16)
     for r in range(rows):
         mean, rstd = columns_of(stat_ref[r])
-        pieces = [
-            grad_ref[:, b, r].reshape(sources * padded, BS).astype(BF16) for b in range(blocks)
-        ]
-        mixed = dot(table_ref[...], jnp.concatenate(pieces, 1))
+        if count_in == 1:
+            pieces = [grad_refs[0][:, b, r].reshape(-1, BS).astype(BF16) for b in range(blocks)]
+            spectrum = jnp.concatenate(pieces, 1)
+        else:
+            for i in range(table_ref.shape[1] // padded):
+                place = pl.ds(pl.multiple_of((me_ref[0] ^ i) * padded, padded), padded)
+                for b in range(blocks):
+                    lanes = slice(b * BS, (b + 1) * BS)
+                    scratch[r, place, lanes] = piece_from(grad_refs, me_ref[0], i)[b, r]
+            spectrum = scratch[r].astype(BF16)
+        mixed = dot(table_ref[...], spectrum)
         grads = jnp.zeros((in_ref.shape[2], BS), F32)
         products = jnp.zeros((in_ref.shape[2], BS), F32)
         for b in range(blocks):
@@ -335,8 +362,6 @@
         piece = jnp.where(upper, high, low) + xor_permute(
             jnp.where(upper, low, high), axis, 1 << i
         )
-    if lax.axis_size(axis) > 1:
-        piece = piece + xor_permute(piece, axis, 1 << low_bits(axis))
     return piece
 
 
@@ -391,6 +416,19 @@
     def exchange(piece):
         return lax.all_to_all(piece, "row", split_axis=0, concat_axis=0, tiled=True)
 
+    me = lax.axis_index("row").astype(jnp.int32).reshape(1)
+    me_spec = pl.BlockSpec(memory_space=pltpu.SMEM)
+    near = 1 << ((owners.bit_length() - 1) // 2)
+    far = owners // near
+
+    def exchange_near(pieces):
+        got = [pieces[0]] + [xor_permute(pieces[r], "row", r) for r in range(1, near)]
+        return [jnp.concatenate([g[s : s + 1] for g in got], 0) for s in range(far)]
+
+    def exchange_far(pieces):
+        got = [pieces[0]] + [xor_permute(pieces[s], "row", s * near) for s in range(1, far)]
+        return got
+
     few = divisor(rows, 2)
     many = divisor(rows, 4)
 
@@ -403,11 +441,11 @@
     def grad_spec(step, count):
         return pl.BlockSpec((step, width, count * BS), lambda h: (h, 0, 0))
 
-    def spectrum_spec(step, count):
-        return pl.BlockSpec((owners, count, step, padded, BS), lambda h: (0, 0, h, 0, 0))
-
-    def spectrum_shape(count):
-        return jax.ShapeDtypeStruct((owners, count, rows, padded, BS), F32)
+    def spectrum_spec(step, count, parts=owners):
+        return pl.BlockSpec((parts, count, step, padded, BS), lambda h: (0, 0, h, 0, 0))
+
+    def spectrum_shape(count, parts=owners):
+        return jax.ShapeDtypeStruct((parts, count, rows, padded, BS), F32)
 
     lon_flops = 2 * rows * tall * width * local
     cot_lon = pl.pallas_call(
@@ -430,15 +468,24 @@
     stats = jnp.stack([mean[0], lax.rsqrt(variance + EPS)[0]], 1)
 
     input_lon = pl.pallas_call(
-        input_lon_kernel,
+        functools.partial(input_lon_kernel, chunks),
         grid=(rows // few,),
-        in_specs=[whole((2 * tall, width)), row_spec(few), stat_spec(few), whole((1, local))],
-        out_specs=[spectrum_spec(few, count) for count in chunks],
-        out_shape=[spectrum_shape(count) for count in chunks],
+        in_specs=[
+            me_spec,
+            whole((2 * tall, width)),
+            row_spec(few),
+            stat_spec(few),
+            whole((1, local)),
+        ],
+        out_specs=[spectrum_spec(few, count) for count in chunks[:-1]]
+        + [spectrum_spec(few, 1, far)] * near,
+        out_shape=[spectrum_shape(count) for count in chunks[:-1]]
+        + [spectrum_shape(1, far)] * near,
+        scratch_shapes=[pltpu.VMEM((few, tall, BS), F32)],
         compiler_params=params(),
         cost_estimate=cost(3 * lon_flops, rows * local * (2 * width + 4 * tall)),
         name="input_lon",
-    )(lon_both, inputs, stats, gain)
+    )(me, lon_both, inputs, stats, gain)
 
     def square(weight):
         re, im = weight.reshape(2, blocks, BS, BS)
@@ -459,7 +506,10 @@
 
     weights = (w_one, w_one_t, w_two, w_two_t, bias, shift)
     first_piece, cot_spec, weights = lax.optimization_barrier((input_lon[0], cot_spec, weights))
+    last = len(chunks) - 1
     input_lon = [first_piece, *input_lon[1:]]
+    x_out = [[exchange(piece)] for piece in input_lon[:last]]
+    x_out.append(exchange_far(exchange_near(input_lon[last:])))
 
     span = rows * padded
 
@@ -470,27 +520,27 @@
         def at(shape):
             return pl.BlockSpec(shape, lambda b: (b + start,) + (0,) * (len(shape) - 1))
 
+        x_count, grad_count = (1 if index < last else far), 1
         tokens = own * height
         flops = 2 * count * tokens * 2 * BS * (3 * 2 * height * 3 + 6 * 2 * BS)
         return pl.pallas_call(
-            functools.partial(mixer_kernel, own, group),
+            functools.partial(mixer_kernel, own, group, x_count, grad_count),
             grid=(count,),
-            in_specs=[whole((2 * height, 2 * height))] * 4
+            in_specs=[me_spec]
+            + [whole((2 * height, 2 * height))] * 4
             + [at((1, 2 * BS, 2 * BS))] * 4
             + [
                 at((1, 2, 2 * BS)),
                 at((1, 2, 2 * BS)),
-                pl.BlockSpec((owners, 1, span, BS), lambda b: (0, b, 0, 0)),
                 pl.BlockSpec((owners, 1, span, BS), lambda b: (0, b + start, 0, 0)),
-            ],
-            out_specs=[
-                pl.BlockSpec((owners, 1, span, BS), lambda b: (0, b, 0, 0)),
-                pl.BlockSpec((1, 4 * BS + 8, BS), lambda b: (b, 0, 0)),
-            ],
-            out_shape=[
-                jax.ShapeDtypeStruct((owners, count, span, BS), F32),
-                jax.ShapeDtypeStruct((count, 4 * BS + 8, BS), F32),
-            ],
+            ]
+            + [pl.BlockSpec((owners // x_count, 1, span, BS), lambda b: (0, b, 0, 0))] * x_count,
+            out_specs=[pl.BlockSpec((owners // grad_count, 1, span, BS), lambda b: (0, b, 0, 0))]
+            * grad_count
+            + [pl.BlockSpec((1, 4 * BS + 8, BS), lambda b: (b, 0, 0))],
+            out_shape=[jax.ShapeDtypeStruct((owners // grad_count, count, span, BS), F32)]
+            * grad_count
+            + [jax.ShapeDtypeStruct((count, 4 * BS + 8, BS), F32)],
             scratch_shapes=[
                 pltpu.VMEM((owners * span, BS), F32),
                 pltpu.VMEM((owners * span, BS), F32),
@@ -506,20 +556,21 @@
             cost_estimate=cost(flops, 3 * count * owners * span * BS * 4, 4 * tokens * BS * count),
             name=f"mixer_{index}",
         )(
+            me,
             fwd_high,
             fwd_low,
             inv_high,
             inv_low,
             *weights,
-            x_spec.reshape(owners, count, span, BS),
             cot_spec.reshape(owners, blocks, span, BS),
+            *[x.reshape(-1, count, span, BS) for x in x_spec],
         )
 
-    mixed = [mix(i, exchange(piece)) for i, piece in enumerate(input_lon)]
+    mixed = [mix(i, pieces) for i, pieces in enumerate(x_out)]
     param_rows = 4 * BS + 8
     unit = 8 * owners // math.gcd(8 * owners, blocks)
     tail = -(blocks * param_rows) % (unit * blocks)
-    flat = jnp.concatenate([m[1].reshape(-1, BS) for m in mixed], 0)
+    flat = jnp.concatenate([m[-1].reshape(-1, BS) for m in mixed], 0)
     flat = jnp.pad(flat, ((0, tail), (0, 0)))
     param_part = halve(flat, "row")
 
@@ -527,27 +578,31 @@
     sums = None
     for index, count in enumerate(chunks):
         start = starts[index]
-        piece = mixed[index][0].reshape(owners, count, rows, padded, BS)
+        pieces = [p.reshape(-1, count, rows, padded, BS) for p in mixed[index][:-1]]
         carry_in = sums is not None
-        if index == len(chunks) - 1 and carry_in:
-            piece, param_part = lax.optimization_barrier((piece, param_part))
+        if index == last:
+            param_part = param_part + xor_permute(param_part, "row", 1 << low_bits("row"))
+            pieces[0], param_part = lax.optimization_barrier((pieces[0], param_part))
+        pieces = [exchange(pieces[0])]
+        if carry_in:
             param_part, sums = lax.optimization_barrier((param_part, sums))
-        piece = exchange(piece)
         in_spec = pl.BlockSpec(
             (1, many, width, count * BS), lambda h, at=start // count: (0, h, 0, at)
         )
         grad, sums = pl.pallas_call(
-            functools.partial(lon_back_kernel, start, carry_in),
+            functools.partial(lon_back_kernel, start, carry_in, len(pieces)),
             grid=(rows // many,),
             in_specs=[
+                me_spec,
                 whole((width, tall)),
-                spectrum_spec(many, count),
                 in_spec,
                 in_spec,
                 stat_spec(many),
                 whole((1, local)),
             ]
+            + [spectrum_spec(many, count, owners // len(pieces))] * len(pieces)
             + [stat_spec(many)] * carry_in,
+            scratch_shapes=[pltpu.VMEM((many, tall, count * BS), F32)],
             out_specs=[grad_spec(many, count), stat_spec(many)],
             out_shape=[
                 jax.ShapeDtypeStruct((rows, width, count * BS), BF16),
@@ -558,13 +613,30 @@
                 2 * rows * tall * width * count * BS, rows * count * BS * (6 * width + 4 * tall)
             ),
             name=f"lon_back_{index}",
-        )(back, piece, inputs, cotangent, stats, gain, *([sums] * carry_in))
+        )(me, back, inputs, cotangent, stats, gain, *pieces, *([sums] * carry_in))
         grads.append(grad)
 
     param_sums = param_part
     for i in reversed(range(low_bits("row"))):
         param_sums = double(param_sums, "row", 1 << i)
     param_sums = param_sums[: blocks * param_rows].reshape(blocks, param_rows, BS)
+
+    spec_scale = 1.0 / math.sqrt(batch * height * K)
+    dw = param_sums[:, : 4 * BS].reshape(blocks, 2, 2, BS, BS).transpose(1, 2, 0, 3, 4) * spec_scale
+    db = param_sums[:, 4 * BS : 4 * BS + 4].reshape(blocks, 2, 2, BS).transpose(1, 2, 0, 3)
+    db = db * spec_scale
+    ln_scale = 1.0 / math.sqrt(batch * height * width)
+    gain_grad = param_sums[:, 4 * BS + 4].reshape(local) / ln_gain * ln_scale
+    outputs = (
+        dw[0].reshape(2, local, BS),
+        db[0].reshape(2, local),
+        dw[1].reshape(2, local, BS),
+        db[1].reshape(2, local),
+        gain_grad,
+        param_sums[:, 4 * BS + 5].reshape(local),
+    )
+    first, second = pair_small(sums, "chan")
+    second, outputs = lax.optimization_barrier((second, outputs))
 
     input_grad = pl.pallas_call(
         functools.partial(finish_kernel, chunks, total_chan),
@@ -576,23 +648,8 @@
         compiler_params=params(),
         cost_estimate=cost(10 * rows * width * local, rows * width * local * 10),
         name="finish",
-    )(inputs, stats, *pair_small(sums, "chan"), *grads)
-
-    spec_scale = 1.0 / math.sqrt(batch * height * K)
-    dw = param_sums[:, : 4 * BS].reshape(blocks, 2, 2, BS, BS).transpose(1, 2, 0, 3, 4) * spec_scale
-    db = param_sums[:, 4 * BS : 4 * BS + 4].reshape(blocks, 2, 2, BS).transpose(1, 2, 0, 3)
-    db = db * spec_scale
-    ln_scale = 1.0 / math.sqrt(batch * height * width)
-    gain_grad = param_sums[:, 4 * BS + 4].reshape(local) / ln_gain * ln_scale
-    return (
-        input_grad,
-        dw[0].reshape(2, local, BS),
-        db[0].reshape(2, local),
-        dw[1].reshape(2, local, BS),
-        db[1].reshape(2, local),
-        gain_grad,
-        param_sums[:, 4 * BS + 5].reshape(local),
-    )
+    )(inputs, stats, first, second, *grads)
+    return (input_grad, *outputs)
 
 
 def solution(mesh):

time: 693 us -> 761 us (1.098)
  blocking collectives: 212 us -> 15.6 us
  waiting for transfers between devices: 301 us -> 493 us
  starting transfers between devices: 39.3 us -> 111 us
    all_to_all x1 -> x0, blocking collectives: 196 us -> none  [exchange(): return lax.all_to_all(piece, 'row', split_axis=0, concat_axis=0, tiled=True)]
    all_to_all x4, waiting for transfers between devices: 124 us -> 250 us  [exchange(): return lax.all_to_all(piece, 'row', split_axis=0, concat_axis=0, tiled=True)]
    ppermute x8 -> x14, waiting for transfers between devices: 176 us -> 243 us  [xor_permute(): return lax.ppermute(piece, axis, [(i, i ^ bit) for i in range(size)])]
    all_to_all x4, starting transfers between devices: 26.7 us -> 83.3 us  [exchange(): return lax.all_to_all(piece, 'row', split_axis=0, concat_axis=0, tiled=True)]
    ppermute x8 -> x14, starting transfers between devices: 12.6 us -> 28 us  [xor_permute(): return lax.ppermute(piece, axis, [(i, i ^ bit) for i in range(size)])]
  transfers between devices with their start and end apart: 12 -> 18, of which waited for: 8 -> 12; matrix products, arithmetic and copies ran while one was open for 3% -> 3% of each run, Pallas kernels for 15% -> 7%
where the time goes in v6:
time: 761 us; the launch traced here: 759 us
  waiting for transfers between devices  493 us (65%)
  Pallas kernels  113 us (15%)
  starting transfers between devices  111 us (15%)
  other arithmetic  15.7 us (2%)
  blocking collectives  15.6 us (2%)
  local copies, waits for them, and re-layouts  9.21 us (1%)
    all_to_all x4, waiting for transfers between devices, exchange(): return lax.all_to_all(piece, 'row', split_axis=0, concat_axis=0, tiled=True)  250 us
    ppermute x14, waiting for transfers between devices, xor_permute(): return lax.ppermute(piece, axis, [(i, i ^ bit) for i in range(size)])  243 us
    all_to_all x4, starting transfers between devices, exchange(): return lax.all_to_all(piece, 'row', split_axis=0, concat_axis=0, tiled=True)  83.3 us
    pallas_call x2, Pallas kernels, mix(): pl.pallas_call(functools.partial(mixer_kernel, own, group, x_count, grad_...  60.7 us
    ppermute x14, starting transfers between devices, xor_permute(): return lax.ppermute(piece, axis, [(i, i ^ bit) for i in range(size)])  28 us
    pallas_call x2, Pallas kernels, on_device(): pl.pallas_call(functools.partial(lon_back_kernel, start, carry_in, len(pi...  17.9 us
    pallas_call x1, Pallas kernels, on_device(): pl.pallas_call(functools.partial(input_lon_kernel, chunks), grid=(rows //...  17.1 us
  transfers between devices with their start and end apart: 18, of which 12 were waited for; matrix products, arithmetic and copies ran while one was open for 3% of the time, Pallas kernels for 7%

profile of v6, /device:TPU:0, one launch (start us, length us, event | category | flops | bytes accessed | tf_op | source)
XLA Modules:
  0.0 759.1 jit_solution(1962217709232577939)
XLA Ops:
  0.6 8.7 %cot_lon.1 = f32[16,4,12,24,128]{4,3,2,1,0:T(8,128)} custom-call(bf16[384,448]{1,0:T(8,128)(2,1)} %constant.44.clone.table_ref, bf16[1,12,448,512]{3,2,1,0:T(8,128)(2,1)} %cot_ref.5), custom_call_target="tpu_custom_call" | custom-call | flops 2113929216 | bytes 14942208 | tf_op jit(solution)/shard_map/cot_lon/pallas_call | solution.py:451
  9.3 7.4 all-to-all-start
  16.8 3.5 convert_reduce_fusion
  20.4 8.3 %psum.14 = f32[1,12,448]{2,0,1:T(1,128)S(1)} all-reduce(f32[1,12,448]{2,0,1:T(1,128)S(1)} %reduce_sum.23), channel_id=1, replica_groups=mesh['chan'=2,'row'=16] {'chan'}, use_global_device_ids=true, to_apply=%region_1.0 | all-reduce | flops 5376 | bytes 43008 | tf_op jit(solution)/shard_map/psum | solution.py:465
  28.7 4.6 fusion.1
  34.7 7.3 psum.15
  44.5 17.1 %input_lon.1 = (f32[16,3,12,24,128]{4,3,2,1,0:T(8,128)}, f32[4,1,12,24,128]{4,3,2,1,0:T(8,128)}, f32[4,1,12,24,128]{4,3,2,1,0:T(8,128)}, f32[4,1,12,24,128]{4,3,2,1,0:T(8,128)}, f32[4,1,12,24,128]{4,3,2,1,0:T(8,128)}) custom-call(s32[1]{0:T(128)} %bitcast.2.me_ref, bf16[768,448]{1,0:T(8,128)(2,1)} %constant.45.clone.table_ref, ...), custom_call_target="tpu_custom_call" | custom-call | flops 6341787648 | bytes 14942208 | tf_op jit(solution)/shard_map/input_lon/pallas_call | solution.py:470
  61.6 124.2 %all-to-all-done = f32[16,4,12,24,128]{4,3,2,1,0:T(8,128)} async-done(((f32[16,4,12,24,128]{4,3,2,1,0:T(8,128)}), f32[16,4,12,24,128]{4,3,2,1,0:T(8,128)}, u32[]{:S(2)}, u32[]{:S(2)}) %all-to-all-start) | async-done | bytes 9437216 | tf_op jit(solution)/shard_map/all_to_all | solution.py:417
  185.7 40.8 %all-to-all-start.1 = ((f32[16,3,12,24,128]{4,3,2,1,0:T(8,128)}), f32[16,3,12,24,128]{4,3,2,1,0:T(8,128)}, u32[]{:S(2)}, u32[]{:S(2)}) async-start(f32[16,3,12,24,128]{4,3,2,1,0:T(8,128)} %get-tuple-element.56), calls=%async_computation.1 | async-start | bytes 14155776 | tf_op jit(solution)/shard_map/all_to_all | solution.py:417
  228.5 125.9 %all-to-all-done.1 = f32[16,3,12,24,128]{4,3,2,1,0:T(8,128)} async-done(((f32[16,3,12,24,128]{4,3,2,1,0:T(8,128)}), f32[16,3,12,24,128]{4,3,2,1,0:T(8,128)}, u32[]{:S(2)}, u32[]{:S(2)}) %all-to-all-start.1) | async-done | bytes 7077920 | tf_op jit(solution)/shard_map/all_to_all | solution.py:417
  354.4 43.8 %mixer_0.1 = (f32[16,3,288,128]{3,2,1,0:T(8,128)}, f32[3,520,128]{2,1,0:T(8,128)}) custom-call(s32[1]{0:T(128)} %bitcast.2.me_ref, bf16[384,384]{1,0:T(8,128)(2,1)} %constant.46.clone.fwd_high_ref, bf16[384,384]{1,0:T(8,128)(2,1)} %constant.47.clone.fwd_low_ref, bf16[384,384]{1,0:T(8,128)(2,1)} %constant.48.clone.inv_high_ref, ...), custom_call_target="tpu_custom_call" | custom-call | flops 17666408448 | bytes 21233664 | tf_op jit(solution)/shard_map/mixer_0/pallas_call | solution.py:526
  398.2 31.4 %all-to-all-start.3 = ((f32[16,3,12,24,128]{4,3,2,1,0:T(8,128)}), f32[16,3,12,24,128]{4,3,2,1,0:T(8,128)}, u32[]{:S(2)}, u32[]{:S(2)}) async-start(f32[16,3,12,24,128]{4,3,2,1,0:T(8,128)} %bitcast.49), calls=%async_computation.3 | async-start | bytes 14155776 | tf_op jit(solution)/shard_map/all_to_all | solution.py:417
  431.8 62.4 %collective-permute-done.2 = f32[4,1,12,24,128]{4,3,2,1,0:T(8,128)S(1)} collective-permute-done((f32[4,1,12,24,128]{4,3,2,1,0:T(8,128)S(1)}, f32[4,1,12,24,128]{4,3,2,1,0:T(8,128)S(1)}, u32[]{:S(2)}, u32[]{:S(2)}) %collective-permute-start.2) | collective-permute-done | bytes 589856 | tf_op jit(solution)/shard_map/ppermute | solution.py:339
  494.3 20.6 %collective-permute-done.1 = f32[4,1,12,24,128]{4,3,2,1,0:T(8,128)S(1)} collective-permute-done((f32[4,1,12,24,128]{4,3,2,1,0:T(8,128)S(1)}, f32[4,1,12,24,128]{4,3,2,1,0:T(8,128)S(1)}, u32[]{:S(2)}, u32[]{:S(2)}) %collective-permute-start.1) | collective-permute-done | bytes 589856 | tf_op jit(solution)/shard_map/ppermute | solution.py:339
  515.2 3.9 collective-permute-start.4
  520.6 36.9 %collective-permute-done.3 = f32[4,1,12,24,128]{4,3,2,1,0:T(8,128)S(1)} collective-permute-done((f32[4,1,12,24,128]{4,3,2,1,0:T(8,128)S(1)}, f32[4,1,12,24,128]{4,3,2,1,0:T(8,128)S(1)}, u32[]{:S(2)}, u32[]{:S(2)}) %collective-permute-start.3) | collective-permute-done | bytes 589856 | tf_op jit(solution)/shard_map/ppermute | solution.py:339
  557.5 66.4 %collective-permute-done.4 = f32[4,1,12,24,128]{4,3,2,1,0:T(8,128)S(1)} collective-permute-done((f32[4,1,12,24,128]{4,3,2,1,0:T(8,128)S(1)}, f32[4,1,12,24,128]{4,3,2,1,0:T(8,128)S(1)}, u32[]{:S(2)}, u32[]{:S(2)}) %collective-permute-start.4) | collective-permute-done | bytes 589856 | tf_op jit(solution)/shard_map/ppermute | solution.py:339
  624.7 16.9 %mixer_1.1 = (f32[16,1,288,128]{3,2,1,0:T(8,128)}, f32[1,520,128]{2,1,0:T(8,128)}) custom-call(s32[1]{0:T(128)} %bitcast.2.me_ref, bf16[384,384]{1,0:T(8,128)(2,1)} %constant.46.clone.fwd_high_ref, bf16[384,384]{1,0:T(8,128)(2,1)} %constant.47.clone.fwd_low_ref, bf16[384,384]{1,0:T(8,128)(2,1)} %constant.48.clone.inv_high_ref, ...), custom_call_target="tpu_custom_call" | custom-call | flops 5888802816 | bytes 7077888 | tf_op jit(solution)/shard_map/mixer_1/pallas_call | solution.py:526
  642.7 1.9 collective-permute-done.6
  647.2 7.2 collective-permute-done.7
  654.5 12.1 %collective-permute-start.8 = (f32[272,128]{1,0:T(8,128)S(1)}, f32[272,128]{1,0:T(8,128)S(1)}, u32[]{:S(2)}, u32[]{:S(2)}) collective-permute-start(f32[272,128]{1,0:T(8,128)S(1)} %slice_select_fusion.2), channel_id=1, source_target_pairs={{0,4},{1,5},{2,6},{3,7},{4,0},{5,1},{6,2},{7,3},{8,12},{9,13},{10,... | collective-permute-start | bytes 417800 | tf_op jit(solution)/shard_map/ppermute | solution.py:339
  666.6 3.1 collective-permute-done.8
  669.8 2.0 collective-permute-start.9
  671.8 6.2 collective-permute-done.9
  678.1 3.7 all-to-all-start.2
  681.8 11.0 %lon_back_0.1 = (bf16[12,448,384]{2,1,0:T(8,128)(2,1)}, f32[12,2,448]{2,1,0:T(2,128)}) custom-call(s32[1]{0:T(128)} %bitcast.2.me_ref, bf16[448,384]{1,0:T(8,128)(2,1)} %constant.50.clone.table_ref, bf16[1,12,448,512]{3,2,1,0:T(8,128)(2,1)} %refs_0_, bf16[1,12,448,512]{3,2,1,0:T(8,128)(2,1)} %cot_ref.5, f32[12,2,448]{2,1,0:T(2,128)} %pad_maximum_fusion.7.stat_ref.refs_1_, ...), custom_call_target="tpu_custom_call" | custom-call | flops 1585446912 | bytes 19464192 | tf_op jit(solution)/shard_map/lon_back_0/pallas_call | solution.py:592
  692.8 1.8 collective-permute-start.11
  694.6 29.2 %collective-permute-done.11 = f32[272,128]{1,0:T(8,128)S(1)} collective-permute-done((f32[272,128]{1,0:T(8,128)S(1)}, f32[272,128]{1,0:T(8,128)S(1)}, u32[]{:S(2)}, u32[]{:S(2)}) %collective-permute-start.11) | collective-permute-done | bytes 139296 | tf_op jit(solution)/shard_map/ppermute | solution.py:339
  723.8 2.3 collective-permute-start.12
  726.1 8.7 %collective-permute-done.12 = f32[544,128]{1,0:T(8,128)S(1)} collective-permute-done((f32[544,128]{1,0:T(8,128)S(1)}, f32[544,128]{1,0:T(8,128)S(1)}, u32[]{:S(2)}, u32[]{:S(2)}) %collective-permute-start.12) | collective-permute-done | bytes 278560 | tf_op jit(solution)/shard_map/ppermute | solution.py:339
  737.1 7.0 lon_back_1.1
  750.1 9.0 %finish.1 = bf16[1,12,448,512]{3,2,1,0:T(8,128)(2,1)} custom-call(bf16[1,12,448,512]{3,2,1,0:T(8,128)(2,1)} %refs_0_, f32[12,2,448]{2,1,0:T(2,128)} %pad_maximum_fusion.7.stat_ref.refs_1_, f32[12,2,448]{2,1,0:T(2,128)} %get-tuple-element.64.refs_2_, f32[12,2,448]{2,1,0:T(2,128)} %copy-done.5, bf16[12,448,384]{2,1,0:T(8,128)(2,1)} %get-tuple-element.67.refs_4_, ...), custom_call_target="tpu_custom_call" | custom-call | flops 27525120 | bytes 27525120 | tf_op jit(solution)/shard_map/finish/pallas_call | solution.py:641
  (95 shorter events, 22.8 us)
Async XLA Ops:
  9.3 176.4 %all-to-all-start = ((f32[16,4,12,24,128]{4,3,2,1,0:T(8,128)}), f32[16,4,12,24,128]{4,3,2,1,0:T(8,128)}, u32[]{:S(2)}, u32[]{:S(2)}) async-start(f32[16,4,12,24,128]{4,3,2,1,0:T(8,128)} %cot_lon.1), calls=%async_computation | async-start | bytes 18874368 | tf_op jit(solution)/shard_map/all_to_all | solution.py:417
  16.8 16.6 %copy-start.3 = (bf16[2,512,128]{2,1,0:T(8,128)(2,1)S(1)}, bf16[2,512,128]{2,1,0:T(8,128)(2,1)}, u32[]{:S(2)}) copy-start(bf16[2,512,128]{2,1,0:T(8,128)(2,1)} %param.21) | copy-start | bytes 786436
  16.8 16.9 %copy-start.4 = (bf16[2,512,128]{2,1,0:T(8,128)(2,1)S(1)}, bf16[2,512,128]{2,1,0:T(8,128)(2,1)}, u32[]{:S(2)}) copy-start(bf16[2,512,128]{2,1,0:T(8,128)(2,1)} %param.19) | copy-start | bytes 786436
  20.3 13.7 %copy-start.7 = (f32[2,512]{1,0:T(2,128)S(1)}, f32[2,512]{1,0:T(2,128)}, u32[]{:S(2)}) copy-start(f32[2,512]{1,0:T(2,128)} %param.22) | copy-start | bytes 12292
  20.3 13.7 %copy-start.8 = (f32[2,512]{1,0:T(2,128)S(1)}, f32[2,512]{1,0:T(2,128)}, u32[]{:S(2)}) copy-start(f32[2,512]{1,0:T(2,128)} %param.20) | copy-start | bytes 12292
  20.3 21.7 %copy-start.9 = (f32[512]{0:T(512)S(1)}, f32[512]{0:T(512)}, u32[]{:S(2)}) copy-start(f32[512]{0:T(512)} %param.18) | copy-start | bytes 6148
  185.7 168.6 %all-to-all-start.1 = ((f32[16,3,12,24,128]{4,3,2,1,0:T(8,128)}), f32[16,3,12,24,128]{4,3,2,1,0:T(8,128)}, u32[]{:S(2)}, u32[]{:S(2)}) async-start(f32[16,3,12,24,128]{4,3,2,1,0:T(8,128)} %get-tuple-element.56), calls=%async_computation.1 | async-start | bytes 14155776 | tf_op jit(solution)/shard_map/all_to_all | solution.py:417
  398.2 31.5 %copy-start.13 = (f32[4,1,12,24,128]{4,3,2,1,0:T(8,128)S(1)}, f32[4,1,12,24,128]{4,3,2,1,0:T(8,128)}, u32[]{:S(2)}) copy-start(f32[4,1,12,24,128]{4,3,2,1,0:T(8,128)} %get-tuple-element.54) | copy-start | bytes 1769476
  398.2 33.2 %copy-start.11 = (f32[4,1,12,24,128]{4,3,2,1,0:T(8,128)S(1)}, f32[4,1,12,24,128]{4,3,2,1,0:T(8,128)}, u32[]{:S(2)}) copy-start(f32[4,1,12,24,128]{4,3,2,1,0:T(8,128)} %get-tuple-element.53) | copy-start | bytes 1769476
  398.2 33.5 %copy-start.10 = (f32[4,1,12,24,128]{4,3,2,1,0:T(8,128)S(1)}, f32[4,1,12,24,128]{4,3,2,1,0:T(8,128)}, u32[]{:S(2)}) copy-start(f32[4,1,12,24,128]{4,3,2,1,0:T(8,128)} %get-tuple-element.52) | copy-start | bytes 1769476
  398.2 33.6 %copy-start.2 = (f32[4,1,12,24,128]{4,3,2,1,0:T(8,128)S(1)}, f32[4,1,12,24,128]{4,3,2,1,0:T(8,128)}, u32[]{:S(2)}) copy-start(f32[4,1,12,24,128]{4,3,2,1,0:T(8,128)} %get-tuple-element.51) | copy-start | bytes 1769476
  398.2 279.8 %all-to-all-start.3 = ((f32[16,3,12,24,128]{4,3,2,1,0:T(8,128)}), f32[16,3,12,24,128]{4,3,2,1,0:T(8,128)}, u32[]{:S(2)}, u32[]{:S(2)}) async-start(f32[16,3,12,24,128]{4,3,2,1,0:T(8,128)} %bitcast.49), calls=%async_computation.3 | async-start | bytes 14155776 | tf_op jit(solution)/shard_map/all_to_all | solution.py:417
  429.7 64.6 %collective-permute-start.2 = (f32[4,1,12,24,128]{4,3,2,1,0:T(8,128)S(1)}, f32[4,1,12,24,128]{4,3,2,1,0:T(8,128)S(1)}, u32[]{:S(2)}, u32[]{:S(2)}) collective-permute-start(f32[4,1,12,24,128]{4,3,2,1,0:T(8,128)S(1)} %copy-done.13), channel_id=1, source_target_pairs={{0,3},{1,2},{2,1},{3,0},{4,7},{5,6},{6,5},{7,4},{8,11},{9,10},{10,... | collective-permute-start | bytes 1769480 | tf_op jit(solution)/shard_map/ppermute | solution.py:339
  431.4 83.5 %collective-permute-start.1 = (f32[4,1,12,24,128]{4,3,2,1,0:T(8,128)S(1)}, f32[4,1,12,24,128]{4,3,2,1,0:T(8,128)S(1)}, u32[]{:S(2)}, u32[]{:S(2)}) collective-permute-start(f32[4,1,12,24,128]{4,3,2,1,0:T(8,128)S(1)} %copy-done.11), channel_id=1, source_target_pairs={{0,2},{1,3},{2,0},{3,1},{4,6},{5,7},{6,4},{7,5},{8,10},{9,11},{10,... | collective-permute-start | bytes 1769480 | tf_op jit(solution)/shard_map/ppermute | solution.py:339
  431.7 83.2 %collective-permute-start = (f32[4,1,12,24,128]{4,3,2,1,0:T(8,128)S(1)}, f32[4,1,12,24,128]{4,3,2,1,0:T(8,128)S(1)}, u32[]{:S(2)}, u32[]{:S(2)}) collective-permute-start(f32[4,1,12,24,128]{4,3,2,1,0:T(8,128)S(1)} %copy-done.10), channel_id=1, source_target_pairs={{0,1},{1,0},{2,3},{3,2},{4,5},{5,4},{6,7},{7,6},{8,9},{9,8},{10,11... | collective-permute-start | bytes 1769480 | tf_op jit(solution)/shard_map/ppermute | solution.py:339
  515.0 42.5 %collective-permute-start.3 = (f32[4,1,12,24,128]{4,3,2,1,0:T(8,128)S(1)}, f32[4,1,12,24,128]{4,3,2,1,0:T(8,128)S(1)}, u32[]{:S(2)}, u32[]{:S(2)}) collective-permute-start(f32[4,1,12,24,128]{4,3,2,1,0:T(8,128)S(1)} %pad_maximum_fusion.2), channel_id=1, source_target_pairs={{0,4},{1,5},{2,6},{3,7},{4,0},{5,1},{6,2},{7,3},{8,12},{9,13},{10,... | collective-permute-start | bytes 1769480 | tf_op jit(solution)/shard_map/ppermute | solution.py:339
  515.2 108.7 %collective-permute-start.4 = (f32[4,1,12,24,128]{4,3,2,1,0:T(8,128)S(1)}, f32[4,1,12,24,128]{4,3,2,1,0:T(8,128)S(1)}, u32[]{:S(2)}, u32[]{:S(2)}) collective-permute-start(f32[4,1,12,24,128]{4,3,2,1,0:T(8,128)S(1)} %pad_maximum_fusion.3), channel_id=1, source_target_pairs={{0,8},{1,9},{2,10},{3,11},{4,12},{5,13},{6,14},{7,15},{8,0},{9,1},... | collective-permute-start | bytes 1769480 | tf_op jit(solution)/shard_map/ppermute | solution.py:339
  519.1 104.8 %collective-permute-start.5 = (f32[4,1,12,24,128]{4,3,2,1,0:T(8,128)S(1)}, f32[4,1,12,24,128]{4,3,2,1,0:T(8,128)}, u32[]{:S(2)}, u32[]{:S(2)}) collective-permute-start(f32[4,1,12,24,128]{4,3,2,1,0:T(8,128)S(1)} %pad_maximum_fusion.4), channel_id=1, source_target_pairs={{0,12},{1,13},{2,14},{3,15},{4,8},{5,9},{6,10},{7,11},{8,4},{9,5},... | collective-permute-start | bytes 1769480 | tf_op jit(solution)/shard_map/ppermute | solution.py:339
  557.5 66.4 %copy-start.12 = (f32[4,1,12,24,128]{4,3,2,1,0:T(8,128)}, f32[4,1,12,24,128]{4,3,2,1,0:T(8,128)S(1)}, u32[]{:S(2)}) copy-start(f32[4,1,12,24,128]{4,3,2,1,0:T(8,128)S(1)} %collective-permute-done.3) | copy-start | bytes 1769476
  623.9 0.8 copy-start.14
  624.7 16.9 %copy-start.1 = (f32[3,520,128]{2,1,0:T(8,128)S(1)}, f32[3,520,128]{2,1,0:T(8,128)}, u32[]{:S(2)}) copy-start(f32[3,520,128]{2,1,0:T(8,128)} %get-tuple-element.57) | copy-start | bytes 2396164
  642.6 2.0 collective-permute-start.6
  645.7 8.8 %collective-permute-start.7 = (f32[544,128]{1,0:T(8,128)S(1)}, f32[544,128]{1,0:T(8,128)S(1)}, u32[]{:S(2)}, u32[]{:S(2)}) collective-permute-start(f32[544,128]{1,0:T(8,128)S(1)} %slice_select_fusion.1), channel_id=1, source_target_pairs={{0,2},{1,3},{2,0},{3,1},{4,6},{5,7},{6,4},{7,5},{8,10},{9,11},{10,... | collective-permute-start | bytes 835592 | tf_op jit(solution)/shard_map/ppermute | solution.py:339
  654.5 15.2 %collective-permute-start.8 = (f32[272,128]{1,0:T(8,128)S(1)}, f32[272,128]{1,0:T(8,128)S(1)}, u32[]{:S(2)}, u32[]{:S(2)}) collective-permute-start(f32[272,128]{1,0:T(8,128)S(1)} %slice_select_fusion.2), channel_id=1, source_target_pairs={{0,4},{1,5},{2,6},{3,7},{4,0},{5,1},{6,2},{7,3},{8,12},{9,13},{10,... | collective-permute-start | bytes 417800 | tf_op jit(solution)/shard_map/ppermute | solution.py:339
  669.8 8.2 %collective-permute-start.9 = (f32[272,128]{1,0:T(8,128)S(1)}, f32[272,128]{1,0:T(8,128)S(1)}, u32[]{:S(2)}, u32[]{:S(2)}) collective-permute-start(f32[272,128]{1,0:T(8,128)S(1)} %select_add_fusion.2), channel_id=1, source_target_pairs={{0,8},{1,9},{2,10},{3,11},{4,12},{5,13},{6,14},{7,15},{8,0},{9,1},... | collective-permute-start | bytes 417800 | tf_op jit(solution)/shard_map/ppermute | solution.py:339
  678.1 57.6 %all-to-all-start.2 = ((f32[16,1,12,24,128]{4,3,2,1,0:T(8,128)}), f32[16,1,12,24,128]{4,3,2,1,0:T(8,128)S(1)}, u32[]{:S(2)}, u32[]{:S(2)}) async-start(f32[16,1,12,24,128]{4,3,2,1,0:T(8,128)} %bitcast.54), calls=%async_computation.2 | async-start | bytes 4718592 | tf_op jit(solution)/shard_map/all_to_all | solution.py:417
  692.8 31.0 %collective-permute-start.11 = (f32[272,128]{1,0:T(8,128)S(1)}, f32[272,128]{1,0:T(8,128)S(1)}, u32[]{:S(2)}, u32[]{:S(2)}) collective-permute-start(f32[272,128]{1,0:T(8,128)S(1)} %add.33), channel_id=1, source_target_pairs={{0,4},{1,5},{2,6},{3,7},{4,0},{5,1},{6,2},{7,3},{8,12},{9,13},{10,... | collective-permute-start | bytes 417800 | tf_op jit(solution)/shard_map/ppermute | solution.py:339
  723.8 11.0 %collective-permute-start.12 = (f32[544,128]{1,0:T(8,128)S(1)}, f32[544,128]{1,0:T(8,128)S(1)}, u32[]{:S(2)}, u32[]{:S(2)}) collective-permute-start(f32[544,128]{1,0:T(8,128)S(1)} %pad_maximum_fusion.6), channel_id=1, source_target_pairs={{0,2},{1,3},{2,0},{3,1},{4,6},{5,7},{6,4},{7,5},{8,10},{9,11},{10,... | collective-permute-start | bytes 835592 | tf_op jit(solution)/shard_map/ppermute | solution.py:339
  735.7 9.9 %collective-permute-start.13 = (f32[1088,128]{1,0:T(8,128)}, f32[1088,128]{1,0:T(8,128)S(1)}, u32[]{:S(2)}, u32[]{:S(2)}) collective-permute-start(f32[1088,128]{1,0:T(8,128)} %pad_maximum_fusion.5), channel_id=1, source_target_pairs={{0,1},{1,0},{2,3},{3,2},{4,5},{5,4},{6,7},{7,6},{8,9},{9,8},{10,11... | collective-permute-start | bytes 1671176 | tf_op jit(solution)/shard_map/ppermute | solution.py:339
  735.7 1.4 copy-start
  744.1 3.1 copy-start.6
  744.1 5.4 collective-permute-start.10
  (1 other events, 0.6 us)

commit v7 on v5

--- a/solution.py
+++ b/solution.py
@@ -16,7 +16,6 @@
 ROOT_TWO_PI = math.sqrt(2.0 / math.pi)
 BF16 = jnp.bfloat16
 F32 = jnp.float32
-VMEM_LIMIT = 60 * 1024 * 1024
 
 
 def gelu_parts(values):
@@ -350,8 +349,8 @@
     return max(n for n in range(1, limit + 1) if count % n == 0)
 
 
-def params():
-    return pltpu.CompilerParams(vmem_limit_bytes=VMEM_LIMIT)
+def params(mib=60):
+    return pltpu.CompilerParams(vmem_limit_bytes=mib * 1024 * 1024)
 
 
 def whole(shape):
@@ -412,9 +411,9 @@
     lon_flops = 2 * rows * tall * width * local
     cot_lon = pl.pallas_call(
         cot_lon_kernel,
-        grid=(rows // few,),
-        in_specs=[whole((tall, width)), row_spec(few)],
-        out_specs=spectrum_spec(few, blocks),
+        grid=(rows // many,),
+        in_specs=[whole((tall, width)), row_spec(many)],
+        out_specs=spectrum_spec(many, blocks),
         out_shape=spectrum_shape(blocks),
         compiler_params=params(),
         cost_estimate=cost(lon_flops, rows * local * (2 * width + 4 * tall)),
@@ -502,7 +501,7 @@
                 pltpu.VMEM((tokens, 2 * BS), BF16),
                 pltpu.VMEM((8, 2 * BS), F32),
             ],
-            compiler_params=params(),
+            compiler_params=params(60 if index < len(chunks) - 1 else 44),
             cost_estimate=cost(flops, 3 * count * owners * span * BS * 4, 4 * tokens * BS * count),
             name=f"mixer_{index}",
         )(
@@ -553,7 +552,7 @@
                 jax.ShapeDtypeStruct((rows, width, count * BS), BF16),
                 jax.ShapeDtypeStruct((rows, 2, width), F32),
             ],
-            compiler_params=params(),
+            compiler_params=params(59 if carry_in else 60),
             cost_estimate=cost(
                 2 * rows * tall * width * count * BS, rows * count * BS * (6 * width + 4 * tall)
             ),
@@ -566,26 +565,13 @@
         param_sums = double(param_sums, "row", 1 << i)
     param_sums = param_sums[: blocks * param_rows].reshape(blocks, param_rows, BS)
 
-    input_grad = pl.pallas_call(
-        functools.partial(finish_kernel, chunks, total_chan),
-        grid=(rows // few,),
-        in_specs=[row_spec(few), stat_spec(few), stat_spec(few), stat_spec(few)]
-        + [grad_spec(few, count) for count in chunks],
-        out_specs=row_spec(few),
-        out_shape=jax.ShapeDtypeStruct(inputs.shape, BF16),
-        compiler_params=params(),
-        cost_estimate=cost(10 * rows * width * local, rows * width * local * 10),
-        name="finish",
-    )(inputs, stats, *pair_small(sums, "chan"), *grads)
-
     spec_scale = 1.0 / math.sqrt(batch * height * K)
     dw = param_sums[:, : 4 * BS].reshape(blocks, 2, 2, BS, BS).transpose(1, 2, 0, 3, 4) * spec_scale
     db = param_sums[:, 4 * BS : 4 * BS + 4].reshape(blocks, 2, 2, BS).transpose(1, 2, 0, 3)
     db = db * spec_scale
     ln_scale = 1.0 / math.sqrt(batch * height * width)
     gain_grad = param_sums[:, 4 * BS + 4].reshape(local) / ln_gain * ln_scale
-    return (
-        input_grad,
+    outputs = (
         dw[0].reshape(2, local, BS),
         db[0].reshape(2, local),
         dw[1].reshape(2, local, BS),
@@ -593,6 +579,21 @@
         gain_grad,
         param_sums[:, 4 * BS + 5].reshape(local),
     )
+    first, second = pair_small(sums, "chan")
+    second, outputs = lax.optimization_barrier((second, outputs))
+
+    input_grad = pl.pallas_call(
+        functools.partial(finish_kernel, chunks, total_chan),
+        grid=(rows // many,),
+        in_specs=[row_spec(many), stat_spec(many), stat_spec(many), stat_spec(many)]
+        + [grad_spec(many, count) for count in chunks],
+        out_specs=row_spec(many),
+        out_shape=jax.ShapeDtypeStruct(inputs.shape, BF16),
+        compiler_params=params(),
+        cost_estimate=cost(10 * rows * width * local, rows * width * local * 10),
+        name="finish",
+    )(inputs, stats, first, second, *grads)
+    return (input_grad, *outputs)
 
 
 def solution(mesh):

time: 693 us -> 688 us (level)
  waiting for transfers between devices: 301 us -> 294 us
  transfers between devices with their start and end apart: 12 -> 12, of which waited for: 8 -> 7; matrix products, arithmetic and copies ran while one was open for 3% -> 3% of each run, Pallas kernels for 15% -> 14%
where the time goes in v7:
time: 688 us; the launch traced here: 686 us
  waiting for transfers between devices  294 us (43%)
  blocking collectives  212 us (31%)
  Pallas kernels  111 us (16%)
  starting transfers between devices  40.5 us (6%)
  local copies, waits for them, and re-layouts  14.3 us (2%)
  other arithmetic  13.9 us (2%)
    all_to_all x1, blocking collectives, exchange(): return lax.all_to_all(piece, 'row', split_axis=0, concat_axis=0, tiled=True)  196 us
    ppermute x8, waiting for transfers between devices, xor_permute(): return lax.ppermute(piece, axis, [(i, i ^ bit) for i in range(size)])  169 us
    all_to_all x4, waiting for transfers between devices, exchange(): return lax.all_to_all(piece, 'row', split_axis=0, concat_axis=0, tiled=True)  124 us
    pallas_call x2, Pallas kernels, mix(): pl.pallas_call(functools.partial(mixer_kernel, own, group), grid=(count,)...  59.5 us
    all_to_all x4, starting transfers between devices, exchange(): return lax.all_to_all(piece, 'row', split_axis=0, concat_axis=0, tiled=True)  27.8 us
    pallas_call x2, Pallas kernels, on_device(): pl.pallas_call(functools.partial(lon_back_kernel, start, carry_in), grid=...  17.9 us
    pallas_call x1, Pallas kernels, on_device(): pl.pallas_call(input_lon_kernel, grid=(rows // few,), in_specs=[whole((2...  16.8 us
  transfers between devices with their start and end apart: 12, of which 7 were waited for; matrix products, arithmetic and copies ran while one was open for 3% of the time, Pallas kernels for 14%

profile of v7, /device:TPU:0, one launch (start us, length us, event | category | flops | bytes accessed | tf_op | source)
XLA Modules:
  0.0 686.0 jit_solution(15021568836673994323)
XLA Ops:
  0.6 8.1 %cot_lon.1 = f32[16,4,12,24,128]{4,3,2,1,0:T(8,128)} custom-call(bf16[384,448]{1,0:T(8,128)(2,1)} %constant.44.clone.table_ref, bf16[1,12,448,512]{3,2,1,0:T(8,128)(2,1)} %cot_ref.5), custom_call_target="tpu_custom_call" | custom-call | flops 2113929216 | bytes 14942208 | tf_op jit(solution)/shard_map/cot_lon/pallas_call | solution.py:412
  8.7 7.4 %all-to-all-start = ((f32[16,4,12,24,128]{4,3,2,1,0:T(8,128)}), f32[16,4,12,24,128]{4,3,2,1,0:T(8,128)}, u32[]{:S(2)}, u32[]{:S(2)}) async-start(f32[16,4,12,24,128]{4,3,2,1,0:T(8,128)} %cot_lon.1), calls=%async_computation | async-start | bytes 18874368 | tf_op jit(solution)/shard_map/all_to_all | solution.py:391
  16.2 3.5 convert_reduce_fusion
  19.8 8.3 %psum.14 = f32[1,12,448]{2,0,1:T(1,128)S(1)} all-reduce(f32[1,12,448]{2,0,1:T(1,128)S(1)} %reduce_sum.23), channel_id=1, replica_groups=mesh['chan'=2,'row'=16] {'chan'}, use_global_device_ids=true, to_apply=%region_1.0 | all-reduce | flops 5376 | bytes 43008 | tf_op jit(solution)/shard_map/psum | solution.py:426
  28.1 4.6 fusion.1
  34.1 7.3 %psum.15 = f32[1,12,448]{2,0,1:T(1,128)S(1)} all-reduce(f32[1,12,448]{2,0,1:T(1,128)S(1)} %reduce_sum.25), channel_id=1, replica_groups=mesh['chan'=2,'row'=16] {'chan'}, use_global_device_ids=true, to_apply=%region_3.0 | all-reduce | flops 5376 | bytes 43008 | tf_op jit(solution)/shard_map/psum | solution.py:428
  42.7 1.2 fusion.4
  43.9 16.8 %input_lon.1 = (f32[16,3,12,24,128]{4,3,2,1,0:T(8,128)}, f32[16,1,12,24,128]{4,3,2,1,0:T(8,128)}) custom-call(bf16[768,448]{1,0:T(8,128)(2,1)} %constant.45.clone.table_ref, bf16[1,12,448,512]{3,2,1,0:T(8,128)(2,1)} %refs_0_, f32[12,2,448]{2,1,0:T(2,128)} %pad_maximum_fusion.3.stat_ref.refs_1_, f32[1,512]{1,0:T(1,128)} %bitcast.62), custom_call_target="tpu_custom_call" | custom-call | flops 6341787648 | bytes 14942208 | tf_op jit(solution)/shard_map/input_lon/pallas_call | solution.py:431
  60.7 124.4 %all-to-all-done = f32[16,4,12,24,128]{4,3,2,1,0:T(8,128)} async-done(((f32[16,4,12,24,128]{4,3,2,1,0:T(8,128)}), f32[16,4,12,24,128]{4,3,2,1,0:T(8,128)}, u32[]{:S(2)}, u32[]{:S(2)}) %all-to-all-start) | async-done | bytes 9437216 | tf_op jit(solution)/shard_map/all_to_all | solution.py:391
  185.1 195.9 %all_to_all.25 = f32[16,3,12,24,128]{4,3,2,1,0:T(8,128)} all-to-all(f32[16,3,12,24,128]{4,3,2,1,0:T(8,128)} %get-tuple-element.50), channel_id=1, replica_groups=mesh['chan'=2,'row'=16] {'row'}, dimensions={0} | all-to-all | bytes 14155776 | tf_op jit(solution)/shard_map/all_to_all | solution.py:391
  381.0 4.5 all-to-all-start.1
  385.6 1.1 copy.55.w_one_ref
  387.7 43.8 %mixer_0.1 = (f32[16,3,288,128]{3,2,1,0:T(8,128)}, f32[3,520,128]{2,1,0:T(8,128)}) custom-call(bf16[384,384]{1,0:T(8,128)(2,1)} %constant.46.clone.fwd_high_ref, bf16[384,384]{1,0:T(8,128)(2,1)} %constant.47.clone.fwd_low_ref, bf16[384,384]{1,0:T(8,128)(2,1)} %constant.48.clone.inv_high_ref, bf16[384,384]{1,0:T(8,128)(2,1)} %constant.49.clone.inv_low_ref, ...), custom_call_target="tpu_custom_call" | custom-call | flops 17666408448 | bytes 21233664 | tf_op jit(solution)/shard_map/mixer_0/pallas_call | solution.py:474
  431.6 12.1 %all-to-all-start.4 = ((f32[16,3,12,24,128]{4,3,2,1,0:T(8,128)}), f32[16,3,12,24,128]{4,3,2,1,0:T(8,128)}, u32[]{:S(2)}, u32[]{:S(2)}) async-start(f32[16,3,12,24,128]{4,3,2,1,0:T(8,128)} %bitcast.48), calls=%async_computation.4 | async-start | bytes 14155776 | tf_op jit(solution)/shard_map/all_to_all | solution.py:391
  449.8 15.7 %mixer_1.1 = (f32[16,1,288,128]{3,2,1,0:T(8,128)}, f32[1,520,128]{2,1,0:T(8,128)S(1)}) custom-call(bf16[384,384]{1,0:T(8,128)(2,1)S(1)} %copy-done.6, bf16[384,384]{1,0:T(8,128)(2,1)S(1)} %copy-done.7, bf16[384,384]{1,0:T(8,128)(2,1)S(1)} %copy-done.8, bf16[384,384]{1,0:T(8,128)(2,1)S(1)} %copy-done.9, bf16[4,256,256]{2,1,0:T(8,128)(2,1)S(1)} %copy-done, ...), custom_call_target="tpu_custom_call" | custom-call | flops 5888802816 | bytes 7077888 | tf_op jit(solution)/shard_map/mixer_1/pallas_call | solution.py:474
  465.9 1.6 collective-permute-done
  467.6 1.3 select_add_fusion
  468.9 1.9 collective-permute-start.1
  470.8 20.9 %collective-permute-done.1 = f32[544,128]{1,0:T(8,128)S(1)} collective-permute-done((f32[544,128]{1,0:T(8,128)S(1)}, f32[544,128]{1,0:T(8,128)S(1)}, u32[]{:S(2)}, u32[]{:S(2)}) %collective-permute-start.1) | collective-permute-done | bytes 278560 | tf_op jit(solution)/shard_map/ppermute | solution.py:311
  491.8 69.8 %collective-permute-done.2 = f32[272,128]{1,0:T(8,128)S(1)} collective-permute-done((f32[272,128]{1,0:T(8,128)S(1)}, f32[272,128]{1,0:T(8,128)S(1)}, u32[]{:S(2)}, u32[]{:S(2)}) %collective-permute-start.2) | collective-permute-done | bytes 139296 | tf_op jit(solution)/shard_map/ppermute | solution.py:311
  561.7 4.6 collective-permute-start.3
  566.2 39.2 %collective-permute-done.3 = f32[272,128]{1,0:T(8,128)S(1)} collective-permute-done((f32[272,128]{1,0:T(8,128)S(1)}, f32[272,128]{1,0:T(8,128)S(1)}, u32[]{:S(2)}, u32[]{:S(2)}) %collective-permute-start.3) | collective-permute-done | bytes 139296 | tf_op jit(solution)/shard_map/ppermute | solution.py:311
  605.5 3.7 all-to-all-start.3
  609.3 10.9 %lon_back_0.1 = (bf16[12,448,384]{2,1,0:T(8,128)(2,1)}, f32[12,2,448]{2,1,0:T(2,128)}) custom-call(bf16[448,384]{1,0:T(8,128)(2,1)} %constant.50.clone.table_ref, f32[16,3,12,24,128]{4,3,2,1,0:T(8,128)} %all-to-all-done.4.grad_ref, bf16[1,12,448,512]{3,2,1,0:T(8,128)(2,1)} %refs_0_, bf16[1,12,448,512]{3,2,1,0:T(8,128)(2,1)} %cot_ref.5, ...), custom_call_target="tpu_custom_call" | custom-call | flops 1585446912 | bytes 19464192 | tf_op jit(solution)/shard_map/lon_back_0/pallas_call | solution.py:538
  620.2 1.8 collective-permute-start.5
  622.0 29.3 %collective-permute-done.5 = f32[272,128]{1,0:T(8,128)S(1)} collective-permute-done((f32[272,128]{1,0:T(8,128)S(1)}, f32[272,128]{1,0:T(8,128)S(1)}, u32[]{:S(2)}, u32[]{:S(2)}) %collective-permute-start.5) | collective-permute-done | bytes 139296 | tf_op jit(solution)/shard_map/ppermute | solution.py:311
  651.3 2.3 collective-permute-start.6
  653.6 8.6 %collective-permute-done.6 = f32[544,128]{1,0:T(8,128)S(1)} collective-permute-done((f32[544,128]{1,0:T(8,128)S(1)}, f32[544,128]{1,0:T(8,128)S(1)}, u32[]{:S(2)}, u32[]{:S(2)}) %collective-permute-start.6) | collective-permute-done | bytes 278560 | tf_op jit(solution)/shard_map/ppermute | solution.py:311
  663.2 1.4 copy-done.10
  664.6 6.9 %lon_back_1.1 = (bf16[12,448,128]{2,1,0:T(8,128)(2,1)}, f32[12,2,448]{2,1,0:T(2,128)}) custom-call(bf16[448,384]{1,0:T(8,128)(2,1)} %constant.50.clone.table_ref, f32[16,1,12,24,128]{4,3,2,1,0:T(8,128)} %copy-done.10, bf16[1,12,448,512]{3,2,1,0:T(8,128)(2,1)} %refs_0_, bf16[1,12,448,512]{3,2,1,0:T(8,128)(2,1)} %cot_ref.5, ...), custom_call_target="tpu_custom_call" | custom-call | flops 528482304 | bytes 6488064 | tf_op jit(solution)/shard_map/lon_back_1/pallas_call | solution.py:538
  671.5 1.6 collective-permute-start.4
  677.5 8.5 %finish.1 = bf16[1,12,448,512]{3,2,1,0:T(8,128)(2,1)} custom-call(bf16[1,12,448,512]{3,2,1,0:T(8,128)(2,1)} %refs_0_, f32[12,2,448]{2,1,0:T(2,128)} %pad_maximum_fusion.3.stat_ref.refs_1_, f32[12,2,448]{2,1,0:T(2,128)} %get-tuple-element.58.refs_2_, f32[12,2,448]{2,1,0:T(2,128)} %copy-done.14, bf16[12,448,384]{2,1,0:T(8,128)(2,1)} %get-tuple-element.61.refs_4_, ...), custom_call_target="tpu_custom_call" | custom-call | flops 27525120 | bytes 27525120 | tf_op jit(solution)/shard_map/finish/pallas_call | solution.py:585
  (84 shorter events, 15.8 us)
Async XLA Ops:
  8.7 176.4 %all-to-all-start = ((f32[16,4,12,24,128]{4,3,2,1,0:T(8,128)}), f32[16,4,12,24,128]{4,3,2,1,0:T(8,128)}, u32[]{:S(2)}, u32[]{:S(2)}) async-start(f32[16,4,12,24,128]{4,3,2,1,0:T(8,128)} %cot_lon.1), calls=%async_computation | async-start | bytes 18874368 | tf_op jit(solution)/shard_map/all_to_all | solution.py:391
  16.2 16.6 %copy-start.12 = (bf16[2,512,128]{2,1,0:T(8,128)(2,1)S(1)}, bf16[2,512,128]{2,1,0:T(8,128)(2,1)}, u32[]{:S(2)}) copy-start(bf16[2,512,128]{2,1,0:T(8,128)(2,1)} %param.21) | copy-start | bytes 786436
  16.2 16.9 %copy-start.13 = (bf16[2,512,128]{2,1,0:T(8,128)(2,1)S(1)}, bf16[2,512,128]{2,1,0:T(8,128)(2,1)}, u32[]{:S(2)}) copy-start(bf16[2,512,128]{2,1,0:T(8,128)(2,1)} %param.19) | copy-start | bytes 786436
  19.7 13.7 %copy-start.16 = (f32[2,512]{1,0:T(2,128)S(1)}, f32[2,512]{1,0:T(2,128)}, u32[]{:S(2)}) copy-start(f32[2,512]{1,0:T(2,128)} %param.22) | copy-start | bytes 12292
  19.7 13.7 %copy-start.17 = (f32[2,512]{1,0:T(2,128)S(1)}, f32[2,512]{1,0:T(2,128)}, u32[]{:S(2)}) copy-start(f32[2,512]{1,0:T(2,128)} %param.20) | copy-start | bytes 12292
  19.7 21.7 %copy-start.18 = (f32[512]{0:T(512)S(1)}, f32[512]{0:T(512)}, u32[]{:S(2)}) copy-start(f32[512]{0:T(512)} %param.18) | copy-start | bytes 6148
  381.0 50.5 %all-to-all-start.1 = ((f32[16,1,12,24,128]{4,3,2,1,0:T(8,128)}), f32[16,1,12,24,128]{4,3,2,1,0:T(8,128)S(1)}, u32[]{:S(2)}, u32[]{:S(2)}) async-start(f32[16,1,12,24,128]{4,3,2,1,0:T(8,128)} %get-tuple-element.47), calls=%async_computation.1 | async-start | bytes 4718592 | tf_op jit(solution)/shard_map/all_to_all | solution.py:391
  431.5 12.2 %copy-start = (bf16[4,256,256]{2,1,0:T(8,128)(2,1)S(1)}, bf16[4,256,256]{2,1,0:T(8,128)(2,1)}, u32[]{:S(2)}) copy-start(bf16[4,256,256]{2,1,0:T(8,128)(2,1)} %copy.55.w_one_ref) | copy-start | bytes 1572868
  431.5 12.2 %copy-start.4 = (f32[4,2,256]{2,1,0:T(2,128)S(1)}, f32[4,2,256]{2,1,0:T(2,128)}, u32[]{:S(2)}) copy-start(f32[4,2,256]{2,1,0:T(2,128)} %reshape.75.bias_ref) | copy-start | bytes 24580
  431.5 12.2 %copy-start.5 = (f32[4,2,256]{2,1,0:T(2,128)S(1)}, f32[4,2,256]{2,1,0:T(2,128)}, u32[]{:S(2)}) copy-start(f32[4,2,256]{2,1,0:T(2,128)} %compare_select_fusion.shift_ref) | copy-start | bytes 24580
  431.6 12.2 %copy-start.6 = (bf16[384,384]{1,0:T(8,128)(2,1)S(1)}, bf16[384,384]{1,0:T(8,128)(2,1)}, u32[]{:S(2)}) copy-start(bf16[384,384]{1,0:T(8,128)(2,1)} %constant.46.clone.fwd_high_ref) | copy-start | bytes 884740
  431.6 173.9 %all-to-all-start.4 = ((f32[16,3,12,24,128]{4,3,2,1,0:T(8,128)}), f32[16,3,12,24,128]{4,3,2,1,0:T(8,128)}, u32[]{:S(2)}, u32[]{:S(2)}) async-start(f32[16,3,12,24,128]{4,3,2,1,0:T(8,128)} %bitcast.48), calls=%async_computation.4 | async-start | bytes 14155776 | tf_op jit(solution)/shard_map/all_to_all | solution.py:391
  443.8 1.0 copy-start.1
  444.8 1.0 copy-start.2
  445.8 1.0 copy-start.3
  446.9 1.0 copy-start.7
  447.8 1.0 copy-start.8
  448.8 1.0 copy-start.9
  449.8 15.7 %copy-start.11 = (f32[3,520,128]{2,1,0:T(8,128)S(1)}, f32[3,520,128]{2,1,0:T(8,128)}, u32[]{:S(2)}) copy-start(f32[3,520,128]{2,1,0:T(8,128)} %get-tuple-element.51) | copy-start | bytes 2396164
  465.5 2.0 collective-permute-start
  468.9 22.8 %collective-permute-start.1 = (f32[544,128]{1,0:T(8,128)S(1)}, f32[544,128]{1,0:T(8,128)S(1)}, u32[]{:S(2)}, u32[]{:S(2)}) collective-permute-start(f32[544,128]{1,0:T(8,128)S(1)} %slice_select_fusion.1), channel_id=1, source_target_pairs={{0,2},{1,3},{2,0},{3,1},{4,6},{5,7},{6,4},{7,5},{8,10},{9,11},{10,... | collective-permute-start | bytes 835592 | tf_op jit(solution)/shard_map/ppermute | solution.py:311
  491.8 69.9 %collective-permute-start.2 = (f32[272,128]{1,0:T(8,128)S(1)}, f32[272,128]{1,0:T(8,128)S(1)}, u32[]{:S(2)}, u32[]{:S(2)}) collective-permute-start(f32[272,128]{1,0:T(8,128)S(1)} %slice_select_fusion.2), channel_id=1, source_target_pairs={{0,4},{1,5},{2,6},{3,7},{4,0},{5,1},{6,2},{7,3},{8,12},{9,13},{10,... | collective-permute-start | bytes 417800 | tf_op jit(solution)/shard_map/ppermute | solution.py:311
  561.7 43.8 %collective-permute-start.3 = (f32[272,128]{1,0:T(8,128)S(1)}, f32[272,128]{1,0:T(8,128)S(1)}, u32[]{:S(2)}, u32[]{:S(2)}) collective-permute-start(f32[272,128]{1,0:T(8,128)S(1)} %select_add_fusion.2), channel_id=1, source_target_pairs={{0,8},{1,9},{2,10},{3,11},{4,12},{5,13},{6,14},{7,15},{8,0},{9,1},... | collective-permute-start | bytes 417800 | tf_op jit(solution)/shard_map/ppermute | solution.py:311
  605.5 57.7 %all-to-all-start.3 = ((f32[16,1,12,24,128]{4,3,2,1,0:T(8,128)}), f32[16,1,12,24,128]{4,3,2,1,0:T(8,128)S(1)}, u32[]{:S(2)}, u32[]{:S(2)}) async-start(f32[16,1,12,24,128]{4,3,2,1,0:T(8,128)} %bitcast.15), calls=%async_computation.3 | async-start | bytes 4718592 | tf_op jit(solution)/shard_map/all_to_all | solution.py:391
  620.2 31.1 %collective-permute-start.5 = (f32[272,128]{1,0:T(8,128)S(1)}, f32[272,128]{1,0:T(8,128)S(1)}, u32[]{:S(2)}, u32[]{:S(2)}) collective-permute-start(f32[272,128]{1,0:T(8,128)S(1)} %add.33), channel_id=1, source_target_pairs={{0,4},{1,5},{2,6},{3,7},{4,0},{5,1},{6,2},{7,3},{8,12},{9,13},{10,... | collective-permute-start | bytes 417800 | tf_op jit(solution)/shard_map/ppermute | solution.py:311
  651.3 10.9 %collective-permute-start.6 = (f32[544,128]{1,0:T(8,128)S(1)}, f32[544,128]{1,0:T(8,128)S(1)}, u32[]{:S(2)}, u32[]{:S(2)}) collective-permute-start(f32[544,128]{1,0:T(8,128)S(1)} %pad_maximum_fusion.2), channel_id=1, source_target_pairs={{0,2},{1,3},{2,0},{3,1},{4,6},{5,7},{6,4},{7,5},{8,10},{9,11},{10,... | collective-permute-start | bytes 835592 | tf_op jit(solution)/shard_map/ppermute | solution.py:311
  663.2 9.9 %collective-permute-start.7 = (f32[1088,128]{1,0:T(8,128)}, f32[1088,128]{1,0:T(8,128)S(1)}, u32[]{:S(2)}, u32[]{:S(2)}) collective-permute-start(f32[1088,128]{1,0:T(8,128)} %pad_maximum_fusion.1), channel_id=1, source_target_pairs={{0,1},{1,0},{2,3},{3,2},{4,5},{5,4},{6,7},{7,6},{8,9},{9,8},{10,11... | collective-permute-start | bytes 1671176 | tf_op jit(solution)/shard_map/ppermute | solution.py:311
  663.2 1.4 copy-start.10
  671.5 3.1 copy-start.15
  671.5 5.4 collective-permute-start.4
  676.9 0.6 copy-start.14

commit v8 on v7

--- a/solution.py
+++ b/solution.py
@@ -562,6 +562,8 @@
 
     param_sums = param_part
     for i in reversed(range(low_bits("row"))):
+        if i == 0:
+            param_sums, sums = lax.optimization_barrier((param_sums, sums))
         param_sums = double(param_sums, "row", 1 << i)
     param_sums = param_sums[: blocks * param_rows].reshape(blocks, param_rows, BS)
 

time: 688 us -> 686 us (level)
  waiting for transfers between devices: 294 us -> 287 us
    ppermute x8, waiting for transfers between devices: 169 us -> 161 us  [xor_permute(): return lax.ppermute(piece, axis, [(i, i ^ bit) for i in range(size)])]
  transfers between devices with their start and end apart: 12 -> 12, of which waited for: 7 -> 8; matrix products, arithmetic and copies ran while one was open for 3% -> 3% of each run, Pallas kernels for 14% -> 14%
where the time goes in v8:
time: 686 us; the launch traced here: 679 us
  waiting for transfers between devices  287 us (42%)
  blocking collectives  212 us (31%)
  Pallas kernels  111 us (16%)
  starting transfers between devices  41.2 us (6%)
  local copies, waits for them, and re-layouts  14.3 us (2%)
  other arithmetic  13.1 us (2%)
    all_to_all x1, blocking collectives, exchange(): return lax.all_to_all(piece, 'row', split_axis=0, concat_axis=0, tiled=True)  196 us
    ppermute x8, waiting for transfers between devices, xor_permute(): return lax.ppermute(piece, axis, [(i, i ^ bit) for i in range(size)])  161 us
    all_to_all x4, waiting for transfers between devices, exchange(): return lax.all_to_all(piece, 'row', split_axis=0, concat_axis=0, tiled=True)  126 us
    pallas_call x2, Pallas kernels, mix(): pl.pallas_call(functools.partial(mixer_kernel, own, group), grid=(count,)...  59.5 us
    all_to_all x4, starting transfers between devices, exchange(): return lax.all_to_all(piece, 'row', split_axis=0, concat_axis=0, tiled=True)  27.8 us
    pallas_call x2, Pallas kernels, on_device(): pl.pallas_call(functools.partial(lon_back_kernel, start, carry_in), grid=...  17.9 us
    pallas_call x1, Pallas kernels, on_device(): pl.pallas_call(input_lon_kernel, grid=(rows // few,), in_specs=[whole((2...  16.8 us
  transfers between devices with their start and end apart: 12, of which 8 were waited for; matrix products, arithmetic and copies ran while one was open for 3% of the time, Pallas kernels for 14%

profile of v8, /device:TPU:0, one launch (start us, length us, event | category | flops | bytes accessed | tf_op | source)
XLA Modules:
  0.0 678.7 jit_solution(9842500579816289124)
XLA Ops:
  0.6 8.1 %cot_lon.1 = f32[16,4,12,24,128]{4,3,2,1,0:T(8,128)} custom-call(bf16[384,448]{1,0:T(8,128)(2,1)} %constant.44.clone.table_ref, bf16[1,12,448,512]{3,2,1,0:T(8,128)(2,1)} %cot_ref.5), custom_call_target="tpu_custom_call" | custom-call | flops 2113929216 | bytes 14942208 | tf_op jit(solution)/shard_map/cot_lon/pallas_call | solution.py:412
  8.7 7.4 %all-to-all-start = ((f32[16,4,12,24,128]{4,3,2,1,0:T(8,128)}), f32[16,4,12,24,128]{4,3,2,1,0:T(8,128)}, u32[]{:S(2)}, u32[]{:S(2)}) async-start(f32[16,4,12,24,128]{4,3,2,1,0:T(8,128)} %cot_lon.1), calls=%async_computation | async-start | bytes 18874368 | tf_op jit(solution)/shard_map/all_to_all | solution.py:391
  16.2 3.5 convert_reduce_fusion
  19.8 8.3 %psum.14 = f32[1,12,448]{2,0,1:T(1,128)S(1)} all-reduce(f32[1,12,448]{2,0,1:T(1,128)S(1)} %reduce_sum.23), channel_id=1, replica_groups=mesh['chan'=2,'row'=16] {'chan'}, use_global_device_ids=true, to_apply=%region_1.0 | all-reduce | flops 5376 | bytes 43008 | tf_op jit(solution)/shard_map/psum | solution.py:426
  28.1 4.6 fusion.1
  34.1 7.3 %psum.15 = f32[1,12,448]{2,0,1:T(1,128)S(1)} all-reduce(f32[1,12,448]{2,0,1:T(1,128)S(1)} %reduce_sum.25), channel_id=1, replica_groups=mesh['chan'=2,'row'=16] {'chan'}, use_global_device_ids=true, to_apply=%region_3.0 | all-reduce | flops 5376 | bytes 43008 | tf_op jit(solution)/shard_map/psum | solution.py:428
  42.7 1.2 fusion.4
  43.9 16.8 %input_lon.1 = (f32[16,3,12,24,128]{4,3,2,1,0:T(8,128)}, f32[16,1,12,24,128]{4,3,2,1,0:T(8,128)}) custom-call(bf16[768,448]{1,0:T(8,128)(2,1)} %constant.45.clone.table_ref, bf16[1,12,448,512]{3,2,1,0:T(8,128)(2,1)} %refs_0_, f32[12,2,448]{2,1,0:T(2,128)} %pad_maximum_fusion.3.stat_ref.refs_1_, f32[1,512]{1,0:T(1,128)} %bitcast.62), custom_call_target="tpu_custom_call" | custom-call | flops 6341787648 | bytes 14942208 | tf_op jit(solution)/shard_map/input_lon/pallas_call | solution.py:431
  60.7 124.4 %all-to-all-done = f32[16,4,12,24,128]{4,3,2,1,0:T(8,128)} async-done(((f32[16,4,12,24,128]{4,3,2,1,0:T(8,128)}), f32[16,4,12,24,128]{4,3,2,1,0:T(8,128)}, u32[]{:S(2)}, u32[]{:S(2)}) %all-to-all-start) | async-done | bytes 9437216 | tf_op jit(solution)/shard_map/all_to_all | solution.py:391
  185.1 195.9 %all_to_all.25 = f32[16,3,12,24,128]{4,3,2,1,0:T(8,128)} all-to-all(f32[16,3,12,24,128]{4,3,2,1,0:T(8,128)} %get-tuple-element.52), channel_id=1, replica_groups=mesh['chan'=2,'row'=16] {'row'}, dimensions={0} | all-to-all | bytes 14155776 | tf_op jit(solution)/shard_map/all_to_all | solution.py:391
  381.0 4.5 all-to-all-start.1
  385.6 1.1 copy.55.w_one_ref
  387.7 43.8 %mixer_0.1 = (f32[16,3,288,128]{3,2,1,0:T(8,128)}, f32[3,520,128]{2,1,0:T(8,128)}) custom-call(bf16[384,384]{1,0:T(8,128)(2,1)} %constant.46.clone.fwd_high_ref, bf16[384,384]{1,0:T(8,128)(2,1)} %constant.47.clone.fwd_low_ref, bf16[384,384]{1,0:T(8,128)(2,1)} %constant.48.clone.inv_high_ref, bf16[384,384]{1,0:T(8,128)(2,1)} %constant.49.clone.inv_low_ref, ...), custom_call_target="tpu_custom_call" | custom-call | flops 17666408448 | bytes 21233664 | tf_op jit(solution)/shard_map/mixer_0/pallas_call | solution.py:474
  431.6 12.1 %all-to-all-start.3 = ((f32[16,3,12,24,128]{4,3,2,1,0:T(8,128)}), f32[16,3,12,24,128]{4,3,2,1,0:T(8,128)}, u32[]{:S(2)}, u32[]{:S(2)}) async-start(f32[16,3,12,24,128]{4,3,2,1,0:T(8,128)} %bitcast.48), calls=%async_computation.3 | async-start | bytes 14155776 | tf_op jit(solution)/shard_map/all_to_all | solution.py:391
  449.8 15.7 %mixer_1.1 = (f32[16,1,288,128]{3,2,1,0:T(8,128)}, f32[1,520,128]{2,1,0:T(8,128)S(1)}) custom-call(bf16[384,384]{1,0:T(8,128)(2,1)S(1)} %copy-done.6, bf16[384,384]{1,0:T(8,128)(2,1)S(1)} %copy-done.7, bf16[384,384]{1,0:T(8,128)(2,1)S(1)} %copy-done.8, bf16[384,384]{1,0:T(8,128)(2,1)S(1)} %copy-done.9, bf16[4,256,256]{2,1,0:T(8,128)(2,1)S(1)} %copy-done, ...), custom_call_target="tpu_custom_call" | custom-call | flops 5888802816 | bytes 7077888 | tf_op jit(solution)/shard_map/mixer_1/pallas_call | solution.py:474
  465.9 1.6 collective-permute-done
  467.6 1.3 select_add_fusion
  468.9 1.9 collective-permute-start.1
  470.8 20.9 %collective-permute-done.1 = f32[544,128]{1,0:T(8,128)S(1)} collective-permute-done((f32[544,128]{1,0:T(8,128)S(1)}, f32[544,128]{1,0:T(8,128)S(1)}, u32[]{:S(2)}, u32[]{:S(2)}) %collective-permute-start.1) | collective-permute-done | bytes 278560 | tf_op jit(solution)/shard_map/ppermute | solution.py:311
  491.8 69.8 %collective-permute-done.2 = f32[272,128]{1,0:T(8,128)S(1)} collective-permute-done((f32[272,128]{1,0:T(8,128)S(1)}, f32[272,128]{1,0:T(8,128)S(1)}, u32[]{:S(2)}, u32[]{:S(2)}) %collective-permute-start.2) | collective-permute-done | bytes 139296 | tf_op jit(solution)/shard_map/ppermute | solution.py:311
  561.7 4.6 collective-permute-start.3
  566.2 39.2 %collective-permute-done.3 = f32[272,128]{1,0:T(8,128)S(1)} collective-permute-done((f32[272,128]{1,0:T(8,128)S(1)}, f32[272,128]{1,0:T(8,128)S(1)}, u32[]{:S(2)}, u32[]{:S(2)}) %collective-permute-start.3) | collective-permute-done | bytes 139296 | tf_op jit(solution)/shard_map/ppermute | solution.py:311
  605.5 3.7 all-to-all-start.4
  609.3 10.9 %lon_back_0.1 = (bf16[12,448,384]{2,1,0:T(8,128)(2,1)}, f32[12,2,448]{2,1,0:T(2,128)}) custom-call(bf16[448,384]{1,0:T(8,128)(2,1)} %constant.50.clone.table_ref, f32[16,3,12,24,128]{4,3,2,1,0:T(8,128)} %all-to-all-done.3.grad_ref, bf16[1,12,448,512]{3,2,1,0:T(8,128)(2,1)} %refs_0_, bf16[1,12,448,512]{3,2,1,0:T(8,128)(2,1)} %cot_ref.5, ...), custom_call_target="tpu_custom_call" | custom-call | flops 1585446912 | bytes 19464192 | tf_op jit(solution)/shard_map/lon_back_0/pallas_call | solution.py:538
  620.2 1.8 collective-permute-start.4
  622.0 29.3 %collective-permute-done.4 = f32[272,128]{1,0:T(8,128)S(1)} collective-permute-done((f32[272,128]{1,0:T(8,128)S(1)}, f32[272,128]{1,0:T(8,128)S(1)}, u32[]{:S(2)}, u32[]{:S(2)}) %collective-permute-start.4) | collective-permute-done | bytes 139296 | tf_op jit(solution)/shard_map/ppermute | solution.py:311
  651.3 2.3 collective-permute-start.5
  653.6 1.3 all-to-all-done.4.grad_ref
  654.9 1.4 copy-done.10
  656.3 6.9 %lon_back_1.1 = (bf16[12,448,128]{2,1,0:T(8,128)(2,1)}, f32[12,2,448]{2,1,0:T(2,128)}) custom-call(bf16[448,384]{1,0:T(8,128)(2,1)} %constant.50.clone.table_ref, f32[16,1,12,24,128]{4,3,2,1,0:T(8,128)} %copy-done.10, bf16[1,12,448,512]{3,2,1,0:T(8,128)(2,1)} %refs_0_, bf16[1,12,448,512]{3,2,1,0:T(8,128)(2,1)} %cot_ref.5, ...), custom_call_target="tpu_custom_call" | custom-call | flops 528482304 | bytes 6488064 | tf_op jit(solution)/shard_map/lon_back_1/pallas_call | solution.py:538
  664.1 1.5 collective-permute-start.6
  670.1 8.5 %finish.1 = bf16[1,12,448,512]{3,2,1,0:T(8,128)(2,1)} custom-call(bf16[1,12,448,512]{3,2,1,0:T(8,128)(2,1)} %refs_0_, f32[12,2,448]{2,1,0:T(2,128)} %pad_maximum_fusion.3.stat_ref.refs_1_, f32[12,2,448]{2,1,0:T(2,128)} %get-tuple-element.62.refs_2_, f32[12,2,448]{2,1,0:T(2,128)} %copy-done.14, bf16[12,448,384]{2,1,0:T(8,128)(2,1)} %get-tuple-element.65.refs_4_, ...), custom_call_target="tpu_custom_call" | custom-call | flops 27525120 | bytes 27525120 | tf_op jit(solution)/shard_map/finish/pallas_call | solution.py:587
  (84 shorter events, 15.8 us)
Async XLA Ops:
  8.7 176.4 %all-to-all-start = ((f32[16,4,12,24,128]{4,3,2,1,0:T(8,128)}), f32[16,4,12,24,128]{4,3,2,1,0:T(8,128)}, u32[]{:S(2)}, u32[]{:S(2)}) async-start(f32[16,4,12,24,128]{4,3,2,1,0:T(8,128)} %cot_lon.1), calls=%async_computation | async-start | bytes 18874368 | tf_op jit(solution)/shard_map/all_to_all | solution.py:391
  16.2 16.6 %copy-start.12 = (bf16[2,512,128]{2,1,0:T(8,128)(2,1)S(1)}, bf16[2,512,128]{2,1,0:T(8,128)(2,1)}, u32[]{:S(2)}) copy-start(bf16[2,512,128]{2,1,0:T(8,128)(2,1)} %param.21) | copy-start | bytes 786436
  16.2 16.9 %copy-start.13 = (bf16[2,512,128]{2,1,0:T(8,128)(2,1)S(1)}, bf16[2,512,128]{2,1,0:T(8,128)(2,1)}, u32[]{:S(2)}) copy-start(bf16[2,512,128]{2,1,0:T(8,128)(2,1)} %param.19) | copy-start | bytes 786436
  19.7 13.7 %copy-start.16 = (f32[2,512]{1,0:T(2,128)S(1)}, f32[2,512]{1,0:T(2,128)}, u32[]{:S(2)}) copy-start(f32[2,512]{1,0:T(2,128)} %param.22) | copy-start | bytes 12292
  19.7 13.7 %copy-start.17 = (f32[2,512]{1,0:T(2,128)S(1)}, f32[2,512]{1,0:T(2,128)}, u32[]{:S(2)}) copy-start(f32[2,512]{1,0:T(2,128)} %param.20) | copy-start | bytes 12292
  19.7 21.7 %copy-start.18 = (f32[512]{0:T(512)S(1)}, f32[512]{0:T(512)}, u32[]{:S(2)}) copy-start(f32[512]{0:T(512)} %param.18) | copy-start | bytes 6148
  381.0 50.5 %all-to-all-start.1 = ((f32[16,1,12,24,128]{4,3,2,1,0:T(8,128)}), f32[16,1,12,24,128]{4,3,2,1,0:T(8,128)S(1)}, u32[]{:S(2)}, u32[]{:S(2)}) async-start(f32[16,1,12,24,128]{4,3,2,1,0:T(8,128)} %get-tuple-element.49), calls=%async_computation.1 | async-start | bytes 4718592 | tf_op jit(solution)/shard_map/all_to_all | solution.py:391
  431.5 12.2 %copy-start = (bf16[4,256,256]{2,1,0:T(8,128)(2,1)S(1)}, bf16[4,256,256]{2,1,0:T(8,128)(2,1)}, u32[]{:S(2)}) copy-start(bf16[4,256,256]{2,1,0:T(8,128)(2,1)} %copy.55.w_one_ref) | copy-start | bytes 1572868
  431.5 12.2 %copy-start.4 = (f32[4,2,256]{2,1,0:T(2,128)S(1)}, f32[4,2,256]{2,1,0:T(2,128)}, u32[]{:S(2)}) copy-start(f32[4,2,256]{2,1,0:T(2,128)} %reshape.75.bias_ref) | copy-start | bytes 24580
  431.5 12.2 %copy-start.5 = (f32[4,2,256]{2,1,0:T(2,128)S(1)}, f32[4,2,256]{2,1,0:T(2,128)}, u32[]{:S(2)}) copy-start(f32[4,2,256]{2,1,0:T(2,128)} %compare_select_fusion.shift_ref) | copy-start | bytes 24580
  431.6 12.2 %copy-start.6 = (bf16[384,384]{1,0:T(8,128)(2,1)S(1)}, bf16[384,384]{1,0:T(8,128)(2,1)}, u32[]{:S(2)}) copy-start(bf16[384,384]{1,0:T(8,128)(2,1)} %constant.46.clone.fwd_high_ref) | copy-start | bytes 884740
  431.6 173.9 %all-to-all-start.3 = ((f32[16,3,12,24,128]{4,3,2,1,0:T(8,128)}), f32[16,3,12,24,128]{4,3,2,1,0:T(8,128)}, u32[]{:S(2)}, u32[]{:S(2)}) async-start(f32[16,3,12,24,128]{4,3,2,1,0:T(8,128)} %bitcast.48), calls=%async_computation.3 | async-start | bytes 14155776 | tf_op jit(solution)/shard_map/all_to_all | solution.py:391
  443.8 1.0 copy-start.1
  444.8 1.0 copy-start.2
  445.8 1.0 copy-start.3
  446.9 1.0 copy-start.7
  447.8 1.0 copy-start.8
  448.8 1.0 copy-start.9
  449.8 15.7 %copy-start.11 = (f32[3,520,128]{2,1,0:T(8,128)S(1)}, f32[3,520,128]{2,1,0:T(8,128)}, u32[]{:S(2)}) copy-start(f32[3,520,128]{2,1,0:T(8,128)} %get-tuple-element.53) | copy-start | bytes 2396164
  465.5 2.0 collective-permute-start
  468.9 22.8 %collective-permute-start.1 = (f32[544,128]{1,0:T(8,128)S(1)}, f32[544,128]{1,0:T(8,128)S(1)}, u32[]{:S(2)}, u32[]{:S(2)}) collective-permute-start(f32[544,128]{1,0:T(8,128)S(1)} %slice_select_fusion.1), channel_id=1, source_target_pairs={{0,2},{1,3},{2,0},{3,1},{4,6},{5,7},{6,4},{7,5},{8,10},{9,11},{10,... | collective-permute-start | bytes 835592 | tf_op jit(solution)/shard_map/ppermute | solution.py:311
  491.8 69.9 %collective-permute-start.2 = (f32[272,128]{1,0:T(8,128)S(1)}, f32[272,128]{1,0:T(8,128)S(1)}, u32[]{:S(2)}, u32[]{:S(2)}) collective-permute-start(f32[272,128]{1,0:T(8,128)S(1)} %slice_select_fusion.2), channel_id=1, source_target_pairs={{0,4},{1,5},{2,6},{3,7},{4,0},{5,1},{6,2},{7,3},{8,12},{9,13},{10,... | collective-permute-start | bytes 417800 | tf_op jit(solution)/shard_map/ppermute | solution.py:311
  561.7 43.8 %collective-permute-start.3 = (f32[272,128]{1,0:T(8,128)S(1)}, f32[272,128]{1,0:T(8,128)S(1)}, u32[]{:S(2)}, u32[]{:S(2)}) collective-permute-start(f32[272,128]{1,0:T(8,128)S(1)} %select_add_fusion.2), channel_id=1, source_target_pairs={{0,8},{1,9},{2,10},{3,11},{4,12},{5,13},{6,14},{7,15},{8,0},{9,1},... | collective-permute-start | bytes 417800 | tf_op jit(solution)/shard_map/ppermute | solution.py:311
  605.5 49.4 %all-to-all-start.4 = ((f32[16,1,12,24,128]{4,3,2,1,0:T(8,128)}), f32[16,1,12,24,128]{4,3,2,1,0:T(8,128)S(1)}, u32[]{:S(2)}, u32[]{:S(2)}) async-start(f32[16,1,12,24,128]{4,3,2,1,0:T(8,128)} %bitcast.15), calls=%async_computation.4 | async-start | bytes 4718592 | tf_op jit(solution)/shard_map/all_to_all | solution.py:391
  620.2 31.1 %collective-permute-start.4 = (f32[272,128]{1,0:T(8,128)S(1)}, f32[272,128]{1,0:T(8,128)S(1)}, u32[]{:S(2)}, u32[]{:S(2)}) collective-permute-start(f32[272,128]{1,0:T(8,128)S(1)} %add.33), channel_id=1, source_target_pairs={{0,4},{1,5},{2,6},{3,7},{4,0},{5,1},{6,2},{7,3},{8,12},{9,13},{10,... | collective-permute-start | bytes 417800 | tf_op jit(solution)/shard_map/ppermute | solution.py:311
  651.3 12.0 %collective-permute-start.5 = (f32[544,128]{1,0:T(8,128)S(1)}, f32[544,128]{1,0:T(8,128)S(1)}, u32[]{:S(2)}, u32[]{:S(2)}) collective-permute-start(f32[544,128]{1,0:T(8,128)S(1)} %pad_maximum_fusion.2), channel_id=1, source_target_pairs={{0,2},{1,3},{2,0},{3,1},{4,6},{5,7},{6,4},{7,5},{8,10},{9,11},{10,... | collective-permute-start | bytes 835592 | tf_op jit(solution)/shard_map/ppermute | solution.py:311
  654.9 1.4 copy-start.10
  663.3 4.0 copy-start.15
  663.4 2.3 collective-permute-start.7
  664.1 5.4 collective-permute-start.6
  669.5 0.6 copy-start.14

commit v9 on v8

--- a/solution.py
+++ b/solution.py
@@ -392,6 +392,7 @@
 
     few = divisor(rows, 2)
     many = divisor(rows, 4)
+    most = divisor(rows, 6)
 
     def row_spec(step):
         return pl.BlockSpec((1, step, width, local), lambda h: (0, h, 0, 0))
@@ -411,9 +412,9 @@
     lon_flops = 2 * rows * tall * width * local
     cot_lon = pl.pallas_call(
         cot_lon_kernel,
-        grid=(rows // many,),
-        in_specs=[whole((tall, width)), row_spec(many)],
-        out_specs=spectrum_spec(many, blocks),
+        grid=(rows // most,),
+        in_specs=[whole((tall, width)), row_spec(most)],
+        out_specs=spectrum_spec(most, blocks),
         out_shape=spectrum_shape(blocks),
         compiler_params=params(),
         cost_estimate=cost(lon_flops, rows * local * (2 * width + 4 * tall)),
@@ -552,7 +553,7 @@
                 jax.ShapeDtypeStruct((rows, width, count * BS), BF16),
                 jax.ShapeDtypeStruct((rows, 2, width), F32),
             ],
-            compiler_params=params(59 if carry_in else 60),
+            compiler_params=params(44 if carry_in else 60),
             cost_estimate=cost(
                 2 * rows * tall * width * count * BS, rows * count * BS * (6 * width + 4 * tall)
             ),

time: 686 us -> 686 us (level)
  no operation moved by 1% of the time
where the time goes in v9:
time: 686 us; the launch traced here: 679 us
  waiting for transfers between devices  285 us (42%)
  blocking collectives  212 us (31%)
  Pallas kernels  108 us (16%)
  starting transfers between devices  41.2 us (6%)
  local copies, waits for them, and re-layouts  17.7 us (3%)
  other arithmetic  13.8 us (2%)
    all_to_all x1, blocking collectives, exchange(): return lax.all_to_all(piece, 'row', split_axis=0, concat_axis=0, tiled=True)  196 us
    ppermute x8, waiting for transfers between devices, xor_permute(): return lax.ppermute(piece, axis, [(i, i ^ bit) for i in range(size)])  160 us
    all_to_all x4, waiting for transfers between devices, exchange(): return lax.all_to_all(piece, 'row', split_axis=0, concat_axis=0, tiled=True)  125 us
    pallas_call x2, Pallas kernels, mix(): pl.pallas_call(functools.partial(mixer_kernel, own, group), grid=(count,)...  58.6 us
    all_to_all x4, starting transfers between devices, exchange(): return lax.all_to_all(piece, 'row', split_axis=0, concat_axis=0, tiled=True)  27.8 us
    pallas_call x2, Pallas kernels, on_device(): pl.pallas_call(functools.partial(lon_back_kernel, start, carry_in), grid=...  17 us
    pallas_call x1, Pallas kernels, on_device(): pl.pallas_call(input_lon_kernel, grid=(rows // few,), in_specs=[whole((2...  16.8 us
  transfers between devices with their start and end apart: 12, of which 8 were waited for; matrix products, arithmetic and copies ran while one was open for 3% of the time, Pallas kernels for 14%

profile of v9, /device:TPU:0, one launch (start us, length us, event | category | flops | bytes accessed | tf_op | source)
XLA Modules:
  0.0 678.6 jit_solution(4604859038454232977)
XLA Ops:
  0.6 6.9 %cot_lon.1 = f32[16,4,12,24,128]{4,3,2,1,0:T(8,128)} custom-call(bf16[384,448]{1,0:T(8,128)(2,1)} %constant.44.clone.table_ref, bf16[1,12,448,512]{3,2,1,0:T(8,128)(2,1)} %cot_ref.5), custom_call_target="tpu_custom_call" | custom-call | flops 2113929216 | bytes 14942208 | tf_op jit(solution)/shard_map/cot_lon/pallas_call | solution.py:413
  7.5 7.4 %all-to-all-start = ((f32[16,4,12,24,128]{4,3,2,1,0:T(8,128)}), f32[16,4,12,24,128]{4,3,2,1,0:T(8,128)}, u32[]{:S(2)}, u32[]{:S(2)}) async-start(f32[16,4,12,24,128]{4,3,2,1,0:T(8,128)} %cot_lon.1), calls=%async_computation | async-start | bytes 18874368 | tf_op jit(solution)/shard_map/all_to_all | solution.py:391
  15.0 3.5 convert_reduce_fusion
  18.6 8.3 %psum.14 = f32[1,12,448]{2,0,1:T(1,128)S(1)} all-reduce(f32[1,12,448]{2,0,1:T(1,128)S(1)} %reduce_sum.23), channel_id=1, replica_groups=mesh['chan'=2,'row'=16] {'chan'}, use_global_device_ids=true, to_apply=%region_1.0 | all-reduce | flops 5376 | bytes 43008 | tf_op jit(solution)/shard_map/psum | solution.py:427
  26.9 4.6 fusion.1
  32.9 7.3 %psum.15 = f32[1,12,448]{2,0,1:T(1,128)S(1)} all-reduce(f32[1,12,448]{2,0,1:T(1,128)S(1)} %reduce_sum.25), channel_id=1, replica_groups=mesh['chan'=2,'row'=16] {'chan'}, use_global_device_ids=true, to_apply=%region_3.0 | all-reduce | flops 5376 | bytes 43008 | tf_op jit(solution)/shard_map/psum | solution.py:429
  41.6 1.2 fusion.4
  42.7 16.8 %input_lon.1 = (f32[16,3,12,24,128]{4,3,2,1,0:T(8,128)}, f32[16,1,12,24,128]{4,3,2,1,0:T(8,128)}) custom-call(bf16[768,448]{1,0:T(8,128)(2,1)} %constant.45.clone.table_ref, bf16[1,12,448,512]{3,2,1,0:T(8,128)(2,1)} %refs_0_, f32[12,2,448]{2,1,0:T(2,128)} %pad_maximum_fusion.3.stat_ref.refs_1_, f32[1,512]{1,0:T(1,128)} %bitcast.47), custom_call_target="tpu_custom_call" | custom-call | flops 6341787648 | bytes 14942208 | tf_op jit(solution)/shard_map/input_lon/pallas_call | solution.py:432
  59.6 124.4 %all-to-all-done = f32[16,4,12,24,128]{4,3,2,1,0:T(8,128)} async-done(((f32[16,4,12,24,128]{4,3,2,1,0:T(8,128)}), f32[16,4,12,24,128]{4,3,2,1,0:T(8,128)}, u32[]{:S(2)}, u32[]{:S(2)}) %all-to-all-start) | async-done | bytes 9437216 | tf_op jit(solution)/shard_map/all_to_all | solution.py:391
  184.0 195.9 %all_to_all.25 = f32[16,3,12,24,128]{4,3,2,1,0:T(8,128)} all-to-all(f32[16,3,12,24,128]{4,3,2,1,0:T(8,128)} %get-tuple-element.52), channel_id=1, replica_groups=mesh['chan'=2,'row'=16] {'row'}, dimensions={0} | all-to-all | bytes 14155776 | tf_op jit(solution)/shard_map/all_to_all | solution.py:391
  379.9 4.5 all-to-all-start.1
  384.4 1.1 copy.55.w_one_ref
  386.5 43.8 %mixer_0.1 = (f32[16,3,288,128]{3,2,1,0:T(8,128)}, f32[3,520,128]{2,1,0:T(8,128)}) custom-call(bf16[384,384]{1,0:T(8,128)(2,1)} %constant.46.clone.fwd_high_ref, bf16[384,384]{1,0:T(8,128)(2,1)} %constant.47.clone.fwd_low_ref, bf16[384,384]{1,0:T(8,128)(2,1)} %constant.48.clone.inv_high_ref, bf16[384,384]{1,0:T(8,128)(2,1)} %constant.49.clone.inv_low_ref, ...), custom_call_target="tpu_custom_call" | custom-call | flops 17666408448 | bytes 21233664 | tf_op jit(solution)/shard_map/mixer_0/pallas_call | solution.py:475
  430.4 12.2 %all-to-all-start.3 = ((f32[16,3,12,24,128]{4,3,2,1,0:T(8,128)}), f32[16,3,12,24,128]{4,3,2,1,0:T(8,128)}, u32[]{:S(2)}, u32[]{:S(2)}) async-start(f32[16,3,12,24,128]{4,3,2,1,0:T(8,128)} %bitcast.52), calls=%async_computation.3 | async-start | bytes 14155776 | tf_op jit(solution)/shard_map/all_to_all | solution.py:391
  448.6 14.8 %mixer_1.1 = (f32[16,1,288,128]{3,2,1,0:T(8,128)S(1)}, f32[1,520,128]{2,1,0:T(8,128)S(1)}) custom-call(bf16[384,384]{1,0:T(8,128)(2,1)S(1)} %copy-done.14, bf16[384,384]{1,0:T(8,128)(2,1)S(1)} %copy-done.15, bf16[384,384]{1,0:T(8,128)(2,1)S(1)} %copy-done.16, bf16[384,384]{1,0:T(8,128)(2,1)S(1)} %copy-done.17, bf16[4,256,256]{2,1,0:T(8,128)(2,1)S(1)} %copy-done.5, ...), custom_call_target="tpu_custom_call" | custom-call | flops 5888802816 | bytes 7077888 | tf_op jit(solution)/shard_map/mixer_1/pallas_call | solution.py:475
  463.4 1.4 copy-done.1
  465.3 1.6 collective-permute-done
  466.9 1.3 select_add_fusion
  468.2 1.9 collective-permute-start.1
  470.2 20.3 %collective-permute-done.1 = f32[544,128]{1,0:T(8,128)S(1)} collective-permute-done((f32[544,128]{1,0:T(8,128)S(1)}, f32[544,128]{1,0:T(8,128)S(1)}, u32[]{:S(2)}, u32[]{:S(2)}) %collective-permute-start.1) | collective-permute-done | bytes 278560 | tf_op jit(solution)/shard_map/ppermute | solution.py:311
  490.7 69.8 %collective-permute-done.2 = f32[272,128]{1,0:T(8,128)S(1)} collective-permute-done((f32[272,128]{1,0:T(8,128)S(1)}, f32[272,128]{1,0:T(8,128)S(1)}, u32[]{:S(2)}, u32[]{:S(2)}) %collective-permute-start.2) | collective-permute-done | bytes 139296 | tf_op jit(solution)/shard_map/ppermute | solution.py:311
  560.5 4.6 collective-permute-start.3
  565.1 39.2 %collective-permute-done.3 = f32[272,128]{1,0:T(8,128)S(1)} collective-permute-done((f32[272,128]{1,0:T(8,128)S(1)}, f32[272,128]{1,0:T(8,128)S(1)}, u32[]{:S(2)}, u32[]{:S(2)}) %collective-permute-start.3) | collective-permute-done | bytes 139296 | tf_op jit(solution)/shard_map/ppermute | solution.py:311
  604.3 3.7 all-to-all-start.4
  608.1 11.0 %lon_back_0.1 = (bf16[12,448,384]{2,1,0:T(8,128)(2,1)}, f32[12,2,448]{2,1,0:T(2,128)}) custom-call(bf16[448,384]{1,0:T(8,128)(2,1)} %constant.50.clone.table_ref, f32[16,3,12,24,128]{4,3,2,1,0:T(8,128)} %all-to-all-done.3.grad_ref, bf16[1,12,448,512]{3,2,1,0:T(8,128)(2,1)} %refs_0_, bf16[1,12,448,512]{3,2,1,0:T(8,128)(2,1)} %cot_ref.5, ...), custom_call_target="tpu_custom_call" | custom-call | flops 1585446912 | bytes 19464192 | tf_op jit(solution)/shard_map/lon_back_0/pallas_call | solution.py:539
  619.1 1.8 collective-permute-start.4
  620.9 29.2 %collective-permute-done.4 = f32[272,128]{1,0:T(8,128)S(1)} collective-permute-done((f32[272,128]{1,0:T(8,128)S(1)}, f32[272,128]{1,0:T(8,128)S(1)}, u32[]{:S(2)}, u32[]{:S(2)}) %collective-permute-start.4) | collective-permute-done | bytes 139296 | tf_op jit(solution)/shard_map/ppermute | solution.py:311
  650.9 2.2 collective-permute-start.5
  653.7 2.6 copy-done
  657.1 6.0 lon_back_1.1
  664.1 1.5 collective-permute-start.6
  670.1 8.5 %finish.1 = bf16[1,12,448,512]{3,2,1,0:T(8,128)(2,1)} custom-call(bf16[1,12,448,512]{3,2,1,0:T(8,128)(2,1)} %refs_0_, f32[12,2,448]{2,1,0:T(2,128)} %pad_maximum_fusion.3.stat_ref.refs_1_, f32[12,2,448]{2,1,0:T(2,128)} %copy-done.9, f32[12,2,448]{2,1,0:T(2,128)} %copy-done.21, bf16[12,448,384]{2,1,0:T(8,128)(2,1)} %get-tuple-element.65.refs_4_, ...), custom_call_target="tpu_custom_call" | custom-call | flops 27525120 | bytes 27525120 | tf_op jit(solution)/shard_map/finish/pallas_call | solution.py:588
  (96 shorter events, 18.0 us)
Async XLA Ops:
  7.5 176.4 %all-to-all-start = ((f32[16,4,12,24,128]{4,3,2,1,0:T(8,128)}), f32[16,4,12,24,128]{4,3,2,1,0:T(8,128)}, u32[]{:S(2)}, u32[]{:S(2)}) async-start(f32[16,4,12,24,128]{4,3,2,1,0:T(8,128)} %cot_lon.1), calls=%async_computation | async-start | bytes 18874368 | tf_op jit(solution)/shard_map/all_to_all | solution.py:391
  15.0 16.6 %copy-start.19 = (bf16[2,512,128]{2,1,0:T(8,128)(2,1)S(1)}, bf16[2,512,128]{2,1,0:T(8,128)(2,1)}, u32[]{:S(2)}) copy-start(bf16[2,512,128]{2,1,0:T(8,128)(2,1)} %param.21) | copy-start | bytes 786436
  15.0 16.9 %copy-start.20 = (bf16[2,512,128]{2,1,0:T(8,128)(2,1)S(1)}, bf16[2,512,128]{2,1,0:T(8,128)(2,1)}, u32[]{:S(2)}) copy-start(bf16[2,512,128]{2,1,0:T(8,128)(2,1)} %param.19) | copy-start | bytes 786436
  18.5 13.7 %copy-start.22 = (f32[2,512]{1,0:T(2,128)S(1)}, f32[2,512]{1,0:T(2,128)}, u32[]{:S(2)}) copy-start(f32[2,512]{1,0:T(2,128)} %param.22) | copy-start | bytes 12292
  18.5 13.7 %copy-start.23 = (f32[2,512]{1,0:T(2,128)S(1)}, f32[2,512]{1,0:T(2,128)}, u32[]{:S(2)}) copy-start(f32[2,512]{1,0:T(2,128)} %param.20) | copy-start | bytes 12292
  18.6 21.7 %copy-start.24 = (f32[512]{0:T(512)S(1)}, f32[512]{0:T(512)}, u32[]{:S(2)}) copy-start(f32[512]{0:T(512)} %param.18) | copy-start | bytes 6148
  379.9 50.4 %all-to-all-start.1 = ((f32[16,1,12,24,128]{4,3,2,1,0:T(8,128)}), f32[16,1,12,24,128]{4,3,2,1,0:T(8,128)S(1)}, u32[]{:S(2)}, u32[]{:S(2)}) async-start(f32[16,1,12,24,128]{4,3,2,1,0:T(8,128)} %get-tuple-element.49), calls=%async_computation.1 | async-start | bytes 4718592 | tf_op jit(solution)/shard_map/all_to_all | solution.py:391
  430.3 12.2 %copy-start.5 = (bf16[4,256,256]{2,1,0:T(8,128)(2,1)S(1)}, bf16[4,256,256]{2,1,0:T(8,128)(2,1)}, u32[]{:S(2)}) copy-start(bf16[4,256,256]{2,1,0:T(8,128)(2,1)} %copy.55.w_one_ref) | copy-start | bytes 1572868
  430.3 12.2 %copy-start.12 = (f32[4,2,256]{2,1,0:T(2,128)S(1)}, f32[4,2,256]{2,1,0:T(2,128)}, u32[]{:S(2)}) copy-start(f32[4,2,256]{2,1,0:T(2,128)} %reshape.75.bias_ref) | copy-start | bytes 24580
  430.3 12.2 %copy-start.13 = (f32[4,2,256]{2,1,0:T(2,128)S(1)}, f32[4,2,256]{2,1,0:T(2,128)}, u32[]{:S(2)}) copy-start(f32[4,2,256]{2,1,0:T(2,128)} %compare_select_fusion.shift_ref) | copy-start | bytes 24580
  430.4 12.2 %copy-start.14 = (bf16[384,384]{1,0:T(8,128)(2,1)S(1)}, bf16[384,384]{1,0:T(8,128)(2,1)}, u32[]{:S(2)}) copy-start(bf16[384,384]{1,0:T(8,128)(2,1)} %constant.46.clone.fwd_high_ref) | copy-start | bytes 884740
  430.4 174.0 %all-to-all-start.3 = ((f32[16,3,12,24,128]{4,3,2,1,0:T(8,128)}), f32[16,3,12,24,128]{4,3,2,1,0:T(8,128)}, u32[]{:S(2)}, u32[]{:S(2)}) async-start(f32[16,3,12,24,128]{4,3,2,1,0:T(8,128)} %bitcast.52), calls=%async_computation.3 | async-start | bytes 14155776 | tf_op jit(solution)/shard_map/all_to_all | solution.py:391
  442.6 1.0 copy-start.6
  443.6 1.0 copy-start.7
  444.7 1.0 copy-start.8
  448.6 16.3 %copy-start.18 = (f32[3,520,128]{2,1,0:T(8,128)S(1)}, f32[3,520,128]{2,1,0:T(8,128)}, u32[]{:S(2)}) copy-start(f32[3,520,128]{2,1,0:T(8,128)} %get-tuple-element.53) | copy-start | bytes 2396164
  463.4 1.4 copy-start.1
  464.9 2.0 collective-permute-start
  468.2 22.3 %collective-permute-start.1 = (f32[544,128]{1,0:T(8,128)S(1)}, f32[544,128]{1,0:T(8,128)S(1)}, u32[]{:S(2)}, u32[]{:S(2)}) collective-permute-start(f32[544,128]{1,0:T(8,128)S(1)} %slice_select_fusion.1), channel_id=1, source_target_pairs={{0,2},{1,3},{2,0},{3,1},{4,6},{5,7},{6,4},{7,5},{8,10},{9,11},{10,... | collective-permute-start | bytes 835592 | tf_op jit(solution)/shard_map/ppermute | solution.py:311
  490.6 69.9 %collective-permute-start.2 = (f32[272,128]{1,0:T(8,128)S(1)}, f32[272,128]{1,0:T(8,128)S(1)}, u32[]{:S(2)}, u32[]{:S(2)}) collective-permute-start(f32[272,128]{1,0:T(8,128)S(1)} %slice_select_fusion.2), channel_id=1, source_target_pairs={{0,4},{1,5},{2,6},{3,7},{4,0},{5,1},{6,2},{7,3},{8,12},{9,13},{10,... | collective-permute-start | bytes 417800 | tf_op jit(solution)/shard_map/ppermute | solution.py:311
  560.5 43.8 %collective-permute-start.3 = (f32[272,128]{1,0:T(8,128)S(1)}, f32[272,128]{1,0:T(8,128)S(1)}, u32[]{:S(2)}, u32[]{:S(2)}) collective-permute-start(f32[272,128]{1,0:T(8,128)S(1)} %select_add_fusion.2), channel_id=1, source_target_pairs={{0,8},{1,9},{2,10},{3,11},{4,12},{5,13},{6,14},{7,15},{8,0},{9,1},... | collective-permute-start | bytes 417800 | tf_op jit(solution)/shard_map/ppermute | solution.py:311
  604.3 49.4 %all-to-all-start.4 = ((f32[16,1,12,24,128]{4,3,2,1,0:T(8,128)}), f32[16,1,12,24,128]{4,3,2,1,0:T(8,128)S(1)}, u32[]{:S(2)}, u32[]{:S(2)}) async-start(f32[16,1,12,24,128]{4,3,2,1,0:T(8,128)} %bitcast.43), calls=%async_computation.4 | async-start | bytes 4718592 | tf_op jit(solution)/shard_map/all_to_all | solution.py:391
  608.1 45.6 %copy-start.2 = (bf16[448,384]{1,0:T(8,128)(2,1)S(1)}, bf16[448,384]{1,0:T(8,128)(2,1)}, u32[]{:S(2)}) copy-start(bf16[448,384]{1,0:T(8,128)(2,1)} %constant.50.clone.table_ref) | copy-start | bytes 1032196
  608.1 45.6 %copy-start.4 = (f32[12,2,448]{2,1,0:T(2,128)S(1)}, f32[12,2,448]{2,1,0:T(2,128)}, u32[]{:S(2)}) copy-start(f32[12,2,448]{2,1,0:T(2,128)} %pad_maximum_fusion.3.stat_ref.refs_1_) | copy-start | bytes 129028
  608.1 45.6 %copy-start.11 = (f32[512]{0:T(512)S(1)}, f32[512]{0:T(512)}, u32[]{:S(2)}) copy-start(f32[512]{0:T(512)} %param.17) | copy-start | bytes 6148
  619.1 31.0 %collective-permute-start.4 = (f32[272,128]{1,0:T(8,128)S(1)}, f32[272,128]{1,0:T(8,128)S(1)}, u32[]{:S(2)}, u32[]{:S(2)}) collective-permute-start(f32[272,128]{1,0:T(8,128)S(1)} %add.33), channel_id=1, source_target_pairs={{0,4},{1,5},{2,6},{3,7},{4,0},{5,1},{6,2},{7,3},{8,12},{9,13},{10,... | collective-permute-start | bytes 417800 | tf_op jit(solution)/shard_map/ppermute | solution.py:311
  650.9 12.3 %collective-permute-start.5 = (f32[544,128]{1,0:T(8,128)}, f32[544,128]{1,0:T(8,128)S(1)}, u32[]{:S(2)}, u32[]{:S(2)}) collective-permute-start(f32[544,128]{1,0:T(8,128)} %pad_maximum_fusion.2), channel_id=1, source_target_pairs={{0,2},{1,3},{2,0},{3,1},{4,6},{5,7},{6,4},{7,5},{8,10},{9,11},{10,... | collective-permute-start | bytes 835592 | tf_op jit(solution)/shard_map/ppermute | solution.py:311
  653.7 2.6 copy-start
  663.1 5.5 copy-start.3
  663.1 5.5 copy-start.9
  663.2 2.4 collective-permute-start.7
  664.1 5.4 collective-permute-start.6
  (5 other events, 4.3 us)
